TPU v7x, 256 devices: a whole 4x4x8 slice. The times are simulated.
256 devices in a mesh: dp: 64 (over z, y, x_lo), mp: 4 (over x_hi, core).
Axes of the slice: x: 4 (x_hi: 2, x_lo: 2; x = x_hi * 2 + x_lo), y: 4, z: 8, core: 2. Of those that a mesh axis runs over, the one named last changes fastest.
Arguments:
- inputs: bfloat16 [128, 256, 1152], P('dp', 'mp'), may hold values from -6 to 6
- cotangent: bfloat16 [128, 256, 1152], P('dp', 'mp'), may hold values from -16 to 16
- lengths: int32 [128], P('dp'), may hold values from 64 to 256
- up_weight: bfloat16 [1152, 6144], P(None, 'mp'), may hold values from -0.1875 to 0.1875
- down_weight: bfloat16 [6144, 1152], P('mp'), may hold values from -0.1875 to 0.1875
- clip_ratio: float32 [1], replicated, may hold values from 0.8 to 1.3
- count_noise: float32 [1], replicated, may hold values from -40 to 40
Outputs:
- grad_down: float32 [6144, 1152], P(('mp', 'dp'))
- ratio_next: float32 [1], replicated
All inputs are finite; a program needn't handle non-finite values.
Results may differ from a plain program's by a relative error of at most 0.0029.
Values may be sent and summed in bfloat16 or wider, within the bound.
No kernel may reach another device: no remote copies, remote signals or barrier semaphores. Data moves between devices by JAX's collectives and lax.ppermute only.
A program may use at most 128 MiB of HBM per device.

v0:
```python
import jax
import jax.numpy as jnp
from jax import lax
from jax.sharding import PartitionSpec as P

D = 1152
FF = 6144
SEQ = 256


curve_scale = 0.7978845608028654
cubic_term = 0.044715
target_share = 0.5


def gelu_parts(preact):
    cubic = preact * preact * preact
    tangent = jnp.tanh(curve_scale * (preact + cubic_term * cubic))
    values = 0.5 * preact * (1.0 + tangent)
    slopes = 0.5 * (1.0 + tangent) + 0.5 * preact * (1.0 - tangent * tangent) * curve_scale * (
        1.0 + 3.0 * cubic_term * preact * preact
    )
    return (values, slopes)


def batch_outer(left, right):
    return jnp.einsum("bsf,bsd->bfd", left, right, preferred_element_type=jnp.float32)


def batch_gram(matrix):
    return jnp.einsum("bsd,btd->bst", matrix, matrix, preferred_element_type=jnp.float32)


def per_device(inputs, cotangent, lengths, up_weight, down_weight, clip_ratio, count_noise):
    inputs_all, cotan_all = (
        lax.all_gather(inputs, "mp", axis=1, tiled=True),
        lax.all_gather(cotangent, "mp", axis=1, tiled=True),
    )
    seq_total = inputs_all.shape[1]
    positions = lax.broadcasted_iota(jnp.int32, (lengths.shape[0], seq_total), 1)
    keep = (positions < lengths[:, None]).astype(jnp.bfloat16)
    masked = cotan_all * keep[:, :, None]
    preact = jnp.einsum("bsd,df->bsf", inputs_all, up_weight, preferred_element_type=jnp.float32)
    values, slopes = gelu_parts(preact)
    hidden = values.astype(jnp.bfloat16)
    backward = jnp.einsum("bsd,fd->bsf", masked, down_weight, preferred_element_type=jnp.float32)
    delta = (backward * slopes).astype(jnp.bfloat16)
    first = jnp.sum(batch_gram(inputs_all) * batch_gram(delta), axis=(1, 2))
    second = jnp.sum(batch_gram(hidden) * batch_gram(masked), axis=(1, 2))
    partial_squares = first + second
    squares = lax.psum(partial_squares, "mp")
    norms = jnp.sqrt(squares)
    clip = clip_ratio[0] * jnp.sqrt(jnp.float32(SEQ * D * FF))
    factors = clip / jnp.maximum(norms, clip)
    examples_all = lax.axis_size("dp") * lengths.shape[0]
    soft = jax.nn.sigmoid(4.0 * (clip - norms) / clip)
    count_total = lax.psum(jnp.sum(soft), "dp")
    share = (count_total + count_noise[0]) / examples_all
    ratio_next = clip_ratio * jnp.exp(-(share - target_share))
    pieces = batch_outer(hidden, masked)
    grad_down = lax.psum_scatter(
        jnp.sum(factors[:, None, None] * pieces, axis=0) / examples_all,
        "dp",
        scatter_dimension=0,
        tiled=True,
    )
    return (grad_down, ratio_next)


def solution(mesh):
    return jax.shard_map(
        per_device,
        mesh=mesh,
        in_specs=(
            P("dp", "mp", None),
            P("dp", "mp", None),
            P("dp"),
            P(None, "mp"),
            P("mp", None),
            P(),
            P(),
        ),
        out_specs=(P(("mp", "dp"), None), P()),
        check_vma=False,
    )
```

profile of v0, /device:TPU:6, one launch (start us, length us, event | category | flops | bytes accessed | tf_op | source)
XLA Modules:
  0.0 425.6 jit_solution(10125669803366043560)
XLA Ops:
  7.2 0.0 copy-start
  7.2 0.0 all-gather.5.cloned.1.call-start
  7.2 0.7 all-gather.5.cloned.1.call-update
  7.9 0.0 all-gather.3.cloned.1.call-start
  8.0 0.7 all-gather.3.cloned.1.call-update
  8.7 0.0 reduce-scatter.5.cloned.1.call-start
  9.4 0.7 compare_convert_fusion
  10.1 25.2 %all-gather.5.cloned.1.call-done = bf16[2,256,1152]{2,1,0:T(8,128)(2,1)} async-done(((bf16[2,64,1152]{2,1,0:T(8,128)(2,1)}), bf16[2,256,1152]{2,1,0:T(8,128)(2,1)}) %all-gather.5.cloned.1.call-update) | async-done | bytes 1179664 | tf_op jit(solution)/shard_map/all_gather | solution.py:37
  35.3 3.0 fusion.21
  38.3 22.3 %all-gather.3.cloned.1.call-done = bf16[2,256,1152]{2,1,0:T(8,128)(2,1)} async-done(((bf16[2,64,1152]{2,1,0:T(8,128)(2,1)}), bf16[2,256,1152]{2,1,0:T(8,128)(2,1)}) %all-gather.3.cloned.1.call-update) | async-done | bytes 1179664 | tf_op jit(solution)/shard_map/all_gather | solution.py:36
  60.7 3.5 fusion.1
  64.2 2.4 fusion.19
  66.6 0.5 fusion.27
  67.1 0.5 copy-done.2
  67.7 0.3 copy-done.3
  68.0 3.6 fusion.15
  71.6 0.7 fusion.18
  72.3 9.1 %psum.14 = f32[2]{0:T(128)S(1)} all-reduce(f32[2]{0:T(128)S(1)} %add.33), channel_id=1, replica_groups=mesh['dp'=64,'mp'=4] {'mp'}, use_global_device_ids=true, to_apply=%region_2.0 | all-reduce | flops 2 | bytes 16 | tf_op jit(solution)/shard_map/psum | solution.py:51
  81.3 0.7 divide_reduce_fusion
  82.0 5.8 %fusion = f32[1536,1152]{1,0:T(8,128)S(1)} fusion(f32[2]{0:T(128)S(1)} %get-tuple-element.3, bf16[2,256,1152]{2,1,0:T(8,128)(2,1)} %all-gather.5.cloned.1.call-done, bf16[2,256]{1,0:T(2,128)(2,1)S(1)} %compare_convert_fusion, f32[2,256,1536]{2,1,0:T(8,128)} %copy-done.4), kind=kOutput, calls=%fused_computation.3 | convolution fusion | flops 1824915456 | bytes 11404296 | tf_op jit(solution)/shard_map/bsf,bsd->bfd/dot_general | solution.py:27
  87.8 3.4 broadcast_multiply_fusion
  91.2 0.0 reduce-scatter.5.cloned.1.call-update
  91.9 154.9 %psum.15 = f32[]{:T(128)} all-reduce(f32[]{:T(128)} %get-tuple-element.2), channel_id=1, replica_groups=mesh['dp'=64,'mp'=4] {'dp'}, use_global_device_ids=true, to_apply=%region_6.0 | all-reduce | flops 1 | bytes 8 | tf_op jit(solution)/shard_map/psum | solution.py:57
  247.5 170.5 %reduce-scatter.5.cloned.1.call-done = f32[24,1152]{1,0:T(8,128)} async-done(((f32[1536,1152]{1,0:T(8,128)}), f32[24,1152]{1,0:T(8,128)}) %reduce-scatter.5.cloned.1.call-update) | async-done | bytes 110608
  (10 shorter events, 0.0 us)
Async XLA Ops:
  7.2 53.5 %copy-start = (bf16[1152,1536]{1,0:T(8,128)(2,1)S(1)}, bf16[1152,1536]{1,0:T(8,128)(2,1)}, u32[]{:S(2)}) copy-start(bf16[1152,1536]{1,0:T(8,128)(2,1)} %param.10) | copy-start | bytes 10616836
  7.2 28.1 %all-gather.5.cloned.1.call-start = ((), (), s32[]{:S(2)}) async-start(), calls=%async_computation.2 | async-start | bytes 1474560 | tf_op jit(solution)/shard_map/all_gather | solution.py:37
  7.9 52.7 %all-gather.3.cloned.1.call-start = ((), (), s32[]{:S(2)}) async-start(), calls=%async_computation.1 | async-start | bytes 1474560 | tf_op jit(solution)/shard_map/all_gather | solution.py:36
  8.7 409.3 %reduce-scatter.5.cloned.1.call-start = ((), (), s32[]{:S(2)}) async-start(), calls=%async_computation.3 | async-start | bytes 7188480
  60.6 3.5 copy-start.5
  64.2 3.0 copy-start.4
  64.2 2.4 copy-start.1
  64.2 3.5 copy-start.2
  64.2 3.8 copy-start.3
Sparse Core Ops, SparseCore 0:
  9.8 25.4 all-gather.4
  37.1 23.5 all-gather.2
  91.3 326.5 reduce-scatter.4
where the time goes:
time: 431 us; the launch traced here: 426 us
  waiting for transfers between devices  219 us (51%)
  blocking collectives  164 us (38%)
  matrix products  19.5 us (5%)
  between operations  17 us (4%)
  other arithmetic  4.76 us (1%)
    unnamed x4, waiting for transfers between devices  172 us
    psum x1, blocking collectives, per_device(): count_total = lax.psum(jnp.sum(soft), 'dp')  155 us
    all_gather x1, waiting for transfers between devices, per_device(): lax.all_gather(cotangent, 'mp', axis=1, tiled=True)  25.2 us
    all_gather x1, waiting for transfers between devices, per_device(): lax.all_gather(inputs, 'mp', axis=1, tiled=True)  22.3 us
    psum x1, blocking collectives, per_device(): squares = lax.psum(partial_squares, 'mp')  9.06 us
  transfers between devices with their start and end apart: 3, of which 3 were waited for; matrix products, arithmetic and copies ran while one was open for 1% of the time, Pallas kernels for 0%

commit v1 on v0

v1 whole, which is shorter than its diff:
```python
import jax
import jax.numpy as jnp
import numpy as np
from jax import lax
from jax.sharding import PartitionSpec as P

D = 1152
FF = 6144
SEQ = 256
AXES = ("dp", "mp")

curve_scale = 0.7978845608028654
cubic_term = 0.044715
target_share = 0.5

X, Y, Z, CORES = 4, 4, 8, 2


def coords(i):
    dp, mp = divmod(i, 4)
    z, rest = divmod(dp, 8)
    y, x_lo = divmod(rest, 2)
    x_hi, core = divmod(mp, 2)
    return (x_hi * 2 + x_lo, y, z, core)


def index_of(x, y, z, core):
    x, y, z = x % X, y % Y, z % Z
    return (z * 8 + y * 2 + x % 2) * 4 + (x // 2) * 2 + core


def permute(array, move):
    pairs = [(i, index_of(*move(*coords(i)))) for i in range(X * Y * Z * CORES)]
    return lax.ppermute(array, AXES, pairs)


def z_even(z, y):
    return (z ^ 1, y)


def z_odd(z, y):
    return ((((z - 1) % Z) ^ 1) + 1) % Z, y


def y_even(z, y):
    return (z, y ^ 1)


def y_odd(z, y):
    return (z, ((((y - 1) % Y) ^ 1) + 1) % Y)


def z_far(z, y):
    return ((z + 4) % Z, y)


STEPS = (
    ((z_even, z_odd, y_even, y_odd, z_far), (z_odd, z_even, y_even, y_odd, z_far)),
    ((y_even, y_odd, z_even, z_odd, z_far), (y_odd, y_even, z_even, z_odd, z_far)),
)


def block_orders(steps):
    places = [(z, y) for z in range(Z) for y in range(Y)]
    orders = {place: [place] for place in places}
    for step in reversed(steps):
        orders = {place: orders[place] + orders[step(*place)] for place in places}
    return orders


def row_table():
    table = np.zeros((CORES, Z, Y, 2, Z * Y), np.int32)
    for core in range(CORES):
        for chain in range(2):
            for (z, y), order in block_orders(STEPS[core][chain]).items():
                assert len(set(order)) == Z * Y
                table[core, z, y, chain] = [zb * Y + yb for zb, yb in order]
    return table


def exchange(array, number, chain):
    def move(x, y, z, core):
        z, y = STEPS[core][chain][number](z, y)
        return (x, y, z, core)

    return permute(array, move)


def gelu_parts(preact):
    cubic = preact * preact * preact
    tangent = jnp.tanh(curve_scale * (preact + cubic_term * cubic))
    values = 0.5 * preact * (1.0 + tangent)
    slopes = 0.5 * (1.0 + tangent) + 0.5 * preact * (1.0 - tangent * tangent) * curve_scale * (
        1.0 + 3.0 * cubic_term * preact * preact
    )
    return (values, slopes)


def batch_gram(matrix):
    return jnp.einsum("bsd,btd->bst", matrix, matrix, preferred_element_type=jnp.float32)


def right(x, y, z, core):
    return (x + 1, y, z, core)


def left(x, y, z, core):
    return (x - 1, y, z, core)


def other_core(x, y, z, core):
    return (x, y, z, 1 - core)


def swap_cores(*arrays):
    sent = jnp.concatenate(arrays, axis=0)
    got = permute(sent, other_core)
    return jnp.split(got, len(arrays), axis=0)


def example_pass(inputs, masked, up, down):
    preact = jnp.einsum("bsd,df->bsf", inputs, up, preferred_element_type=jnp.float32)
    values, slopes = gelu_parts(preact)
    hidden = values.astype(jnp.bfloat16)
    backward = jnp.einsum("bsd,fd->bsf", masked, down, preferred_element_type=jnp.float32)
    delta = (backward * slopes).astype(jnp.bfloat16)
    first = jnp.sum(batch_gram(inputs) * batch_gram(delta), axis=(1, 2))
    second = jnp.sum(batch_gram(hidden) * batch_gram(masked), axis=(1, 2))
    return hidden, first + second


def per_device(inputs, cotangent, lengths, up_weight, down_weight, clip_ratio, count_noise):
    dp = lax.axis_index("dp")
    mp = lax.axis_index("mp")
    z, y, x_lo, core = dp // 8, (dp // 2) % 4, dp % 2, mp % 2
    local = inputs.shape[1]

    positions = mp * local + lax.broadcasted_iota(jnp.int32, (lengths.shape[0], local), 1)
    keep = (positions < lengths[:, None]).astype(jnp.bfloat16)
    masked = cotangent * keep[:, :, None]

    in_l = permute(inputs, right)
    co_r = permute(masked, left)
    co_l = permute(masked, right)
    in_r = permute(inputs, left)
    in_o = permute(in_l, right)
    co_o = permute(co_r, left)
    in_s, co_s = swap_cores(inputs, masked)
    in_ls, co_rs = swap_cores(in_l, co_r)
    co_ls, in_rs = swap_cores(co_l, in_r)
    in_os, co_os = swap_cores(in_o, co_o)

    table = jnp.asarray(row_table())
    order = lax.dynamic_slice(table, (core, z, y, 0, 0), (1, 1, 1, 2, Z * Y)).reshape(2, 2, 16)
    order = jnp.stack([order[:, 1], order[:, 0]])
    rows = (
        order[..., None] * 48
        + x_lo * 24
        + jnp.arange(2, dtype=jnp.int32)[None, :, None, None] * 12
        + jnp.arange(12, dtype=jnp.int32)
    ).reshape(-1)
    units = up_weight.shape[1]
    pick = (lax.broadcasted_iota(jnp.int32, (units, rows.shape[0]), 0) == rows[None, :]).astype(jnp.bfloat16)
    up = jnp.einsum("df,fp->dp", up_weight, pick, preferred_element_type=jnp.bfloat16)
    down = jnp.einsum("fp,fd->pd", pick, down_weight, preferred_element_type=jnp.bfloat16)

    in_theirs = jnp.concatenate([in_l, in_ls, in_r, in_rs], axis=1)
    co_theirs = jnp.concatenate([co_l, co_ls, co_r, co_rs], axis=1)
    in_ours = jnp.concatenate([inputs, in_s, in_o, in_os], axis=1)
    co_ours = jnp.concatenate([masked, co_s, co_o, co_os], axis=1)
    hidden_theirs, squares_theirs = example_pass(in_theirs, co_theirs, up, down)
    hidden_ours, squares_ours = example_pass(in_ours, co_ours, up, down)

    both = jnp.stack([squares_ours, squares_theirs])
    both = jnp.where(x_lo == 0, both, both[::-1])
    for move in (other_core, lambda x, y, z, core: (x ^ 1, y, z, core), lambda x, y, z, core: (x ^ 2, y, z, core)):
        both = both + permute(both, move)
    norms_both = jnp.sqrt(both)
    clip = clip_ratio[0] * jnp.sqrt(jnp.float32(SEQ * D * FF))
    factors = clip / jnp.maximum(norms_both, clip)
    factors = jnp.where(x_lo == 0, factors, factors[::-1])
    norms = jnp.where(x_lo == 0, norms_both[0], norms_both[1])
    examples_all = lax.axis_size("dp") * lengths.shape[0]
    soft = jax.nn.sigmoid(4.0 * (clip - norms) / clip)
    count_total = jnp.sum(lax.all_gather(soft, "dp", axis=0, tiled=True))
    share = (count_total + count_noise[0]) / examples_all
    ratio_next = clip_ratio * jnp.exp(-(share - target_share))

    scale = (factors / examples_all).reshape(-1)

    def outer(lo, hi):
        hidden = jnp.concatenate([hidden_ours[:, :, lo:hi], hidden_theirs[:, :, lo:hi]], axis=0)
        cotan = jnp.concatenate([co_ours, co_theirs], axis=0)
        pieces = jnp.einsum("bsf,bsd->bfd", hidden, cotan, preferred_element_type=jnp.float32)
        return jnp.sum(scale[:, None, None] * pieces, axis=0)

    half = rows.shape[0] // 2
    quarter = half // 2
    sends = outer(0, half).astype(jnp.bfloat16)
    keeps = outer(half, 2 * half)
    got = [exchange(sends[chain * quarter : (chain + 1) * quarter], 0, chain) for chain in range(2)]
    sums = [keeps[chain * quarter : (chain + 1) * quarter] + got[chain].astype(jnp.float32) for chain in range(2)]
    size = quarter // 2
    got = [exchange(sums[chain][size:].astype(jnp.bfloat16), 1, chain) for chain in range(2)]
    sums = [sums[chain][:size] + got[chain].astype(jnp.float32) for chain in range(2)]
    total = jnp.stack(sums)
    for number in (2, 3, 4):
        size = size // 2
        got = exchange(total[:, size:].astype(jnp.bfloat16), number, 0)
        total = total[:, :size] + got.astype(jnp.float32)
    grad_down = total.reshape(-1, total.shape[-1])
    return (grad_down, ratio_next)


def solution(mesh):
    return jax.shard_map(
        per_device,
        mesh=mesh,
        in_specs=(
            P("dp", "mp", None),
            P("dp", "mp", None),
            P("dp"),
            P(None, "mp"),
            P("mp", None),
            P(),
            P(),
        ),
        out_specs=(P(("mp", "dp"), None), P()),
        check_vma=False,
    )
```

time: 431 us -> 296 us (0.69)
  waiting for transfers between devices: 219 us -> 27.7 us
  matrix products: 19.5 us -> 50.6 us
  starting transfers between devices: 0.11 us -> 27.7 us
  local copies, waits for them, and re-layouts: 0.9 us -> 15.3 us
  between operations: 17 us -> 4.82 us
  blocking collectives: 164 us -> 152 us
  other arithmetic: 4.76 us -> 12.4 us
    unnamed x4 -> x0, waiting for transfers between devices: 172 us -> none
    psum x2 -> x0, blocking collectives: 164 us -> none  [the longest x1 155 us: per_device(): count_total = lax.psum(jnp.sum(soft), 'dp')]
    unnamed x0 -> x1, blocking collectives: none -> 152 us
    all_gather x2 -> x0, waiting for transfers between devices: 47.5 us -> none  [the longest x1 25.2 us: per_device(): lax.all_gather(cotangent, 'mp', axis=1, tiled=True)]
    ppermute x0 -> x20, starting transfers between devices: none -> 27.7 us  [permute(): return lax.ppermute(array, AXES, pairs)]
    ppermute x0 -> x20, waiting for transfers between devices: none -> 27.7 us  [permute(): return lax.ppermute(array, AXES, pairs)]
    dot_general x4 -> x8, matrix products: 6.63 us -> 26.6 us  [batch_gram(): jnp.einsum('bsd,btd->bst', matrix, matrix, preferred_element_type=jnp.flo...]
    dot_general x3 -> x5, matrix products: 12.9 us -> 19.6 us  [the longest x2 8.61 us: outer(): jnp.einsum('bsf,bsd->bfd', hidden, cotan, preferred_element_type=jnp.floa...]
  transfers between devices with their start and end apart: 3 -> 20, of which waited for: 3 -> 10; matrix products, arithmetic and copies ran while one was open for 1% -> 16% of each run, Pallas kernels for 0% -> 0%
where the time goes in v1:
time: 296 us; the launch traced here: 291 us
  blocking collectives  152 us (51%)
  matrix products  50.6 us (17%)
  starting transfers between devices  27.7 us (9%)
  waiting for transfers between devices  27.7 us (9%)
  local copies, waits for them, and re-layouts  15.3 us (5%)
  other arithmetic  12.4 us (4%)
  between operations  4.82 us (2%)
    unnamed x1, blocking collectives  152 us
    ppermute x20, starting transfers between devices, permute(): return lax.ppermute(array, AXES, pairs)  27.7 us
    ppermute x20, waiting for transfers between devices, permute(): return lax.ppermute(array, AXES, pairs)  27.7 us
    dot_general x8, matrix products, batch_gram(): jnp.einsum('bsd,btd->bst', matrix, matrix, preferred_element_type=jnp.flo...  26.6 us
    dot_general x2, matrix products, outer(): jnp.einsum('bsf,bsd->bfd', hidden, cotan, preferred_element_type=jnp.floa...  8.61 us
    dot_general x2, matrix products, example_pass(): jnp.einsum('bsd,df->bsf', inputs, up, preferred_element_type=jnp.float32)  6.16 us
  transfers between devices with their start and end apart: 20, of which 10 were waited for; matrix products, arithmetic and copies ran while one was open for 16% of the time, Pallas kernels for 0%

profile of v1, /device:TPU:6, one launch (start us, length us, event | category | flops | bytes accessed | tf_op | source)
XLA Modules:
  0.0 290.9 jit_solution(7439759531423286340)
XLA Ops:
  3.5 2.2 collective-permute-start.8
  6.3 2.6 collective-permute-start.1
  13.3 4.4 %fusion.2 = bf16[768,1152,1]{1,0,2:T(8,128)(2,1)} fusion(bf16[1152,1536]{1,0:T(8,128)(2,1)S(1)} %copy-done, s32[768]{0:T(1024)S(1)} %add.176), kind=kOutput, calls=%fused_computation.6 | convolution fusion | flops 2721153024 | bytes 5311488
  17.8 4.8 %fusion.3 = bf16[768,1152,1]{1,0,2:T(8,128)(2,1)} fusion(bf16[1536,1152]{1,0:T(8,128)(2,1)S(1)} %copy-done.27, s32[768]{0:T(1024)S(1)} %add.176), kind=kOutput, calls=%fused_computation.7 | convolution fusion | flops 2719088640 | bytes 5311488 | tf_op jit(solution)/shard_map/fp,fd->pd/dot_general | solution.py:165
  23.3 3.2 %collective-permute-start.2 = (bf16[2,64,1152]{2,1,0:T(8,128)(2,1)}, bf16[2,64,1152]{2,1,0:T(8,128)(2,1)S(1)}, u32[]{:S(2)}, u32[]{:S(2)}) collective-permute-start(bf16[2,64,1152]{2,1,0:T(8,128)(2,1)} %collective-permute-done.1), channel_id=1, source_target_pairs={{0,4},{1,5},{2,6},{3,7},{4,2},{5,3},{6,0},{7,1},{8,12},{9,13},{10,... | collective-permute-start | bytes 884744 | tf_op jit(solution)/shard_map/ppermute | solution.py:34
  29.5 4.7 %collective-permute-done.4 = bf16[2,64,1152]{2,1,0:T(8,128)(2,1)S(1)} collective-permute-done((bf16[2,64,1152]{2,1,0:T(8,128)(2,1)}, bf16[2,64,1152]{2,1,0:T(8,128)(2,1)S(1)}, u32[]{:S(2)}, u32[]{:S(2)}) %collective-permute-start.4) | collective-permute-done | bytes 294944 | tf_op jit(solution)/shard_map/ppermute | solution.py:34
  35.1 2.1 fusion.78
  38.8 3.7 %multiply_convert_fusion = (bf16[2,256,768]{2,1,0:T(8,128)(2,1)S(1)}, f32[2,256,768]{2,1,0:T(8,128)}) fusion(bf16[768,1152,1]{1,0,2:T(8,128)(2,1)S(1)} %copy-done.29, bf16[2,64,1152]{2,1,0:T(8,128)(2,1)S(1)} %get-tuple-element.15, bf16[2,64,1152]{2,1,0:T(8,128)(2,1)} %collective-permute-done.7, bf16[2,64,1152]{2,1,0:T(8,128)(2,1)S(1)} %get-tuple-element.17, ...), kind=kOutput, calls=%fused_computation.33 | convolution fusion | flops 914227200 | bytes 5308416 | tf_op jit(solution)/shard_map/bsd,df->bsf/dot_general | solution.py:122
  44.5 7.8 %fusion.35 = f32[2,256,256]{2,1,0:T(8,128)} fusion(f32[2,256,768]{2,1,0:T(8,128)} %get-tuple-element.21, bf16[768,1152,1]{1,0,2:T(8,128)(2,1)} %fusion.3, bf16[2,64,1152]{2,1,0:T(8,128)(2,1)} %get-tuple-element.16, bf16[2,64,1152]{2,1,0:T(8,128)(2,1)} %collective-permute-done.3, bf16[2,64,1152]{2,1,0:T(8,128)(2,1)} %get-tuple-element.14, ...), kind=kOutput, calls=%fused_computation.57 | convolution fusion | flops 1119485952 | bytes 5046272 | tf_op jit(solution)/shard_map/bsd,btd->bst/dot_general | solution.py:100
  52.4 2.5 fusion.27
  59.8 2.5 multiply_convert_fusion.1
  64.5 7.8 %fusion.36 = f32[2,256,256]{2,1,0:T(8,128)} fusion(f32[2,256,768]{2,1,0:T(8,128)} %get-tuple-element.23, bf16[768,1152,1]{1,0,2:T(8,128)(2,1)} %fusion.3, bf16[2,64,1152]{2,1,0:T(8,128)(2,1)} %get-tuple-element.12, bf16[2,64,1152]{2,1,0:T(8,128)(2,1)} %copy-done.10, bf16[2,64,1152]{2,1,0:T(8,128)(2,1)} %get-tuple-element.10, ...), kind=kOutput, calls=%fused_computation.58 | convolution fusion | flops 1119485952 | bytes 5046272 | tf_op jit(solution)/shard_map/bsd,btd->bst/dot_general | solution.py:100
  72.3 2.5 fusion.25
  78.1 3.4 %collective-permute-done.11 = f32[2,2]{1,0:T(2,128)S(1)} collective-permute-done((f32[2,2]{1,0:T(2,128)S(1)}, f32[2,2]{1,0:T(2,128)S(1)}, u32[]{:S(2)}, u32[]{:S(2)}) %collective-permute-start.11) | collective-permute-done | bytes 48 | tf_op jit(solution)/shard_map/ppermute | solution.py:34
  81.5 2.4 collective-permute-start.12
  83.9 2.7 collective-permute-done.12
  86.8 3.2 %multiply_reduce_fusion = bf16[384,1152]{1,0:T(8,128)(2,1)S(1)} fusion(f32[4]{0:T(128)S(1)} %mul.204, bf16[2,256,384]{2,1,0:T(8,128)(2,1)} %get-tuple-element.8, bf16[2,256,384]{2,1,0:T(8,128)(2,1)} %get-tuple-element.6, bf16[2,64,1152]{2,1,0:T(8,128)(2,1)} %get-tuple-element.16, bf16[2,64,1152]{2,1,0:T(8,128)(2,1)} %collective-permute-done.3, ...), kind=kOutput, calls=%fused_computation | convolution fusion | flops 928333824 | bytes 4030480 | tf_op jit(solution)/shard_map/bsf,bsd->bfd/dot_general | solution.py:194
  90.1 5.7 %collective-permute-start.15 = (bf16[192,1152]{1,0:T(8,128)(2,1)S(1)}, bf16[192,1152]{1,0:T(8,128)(2,1)S(1)}, u32[]{:S(2)}, u32[]{:S(2)}) collective-permute-start(bf16[192,1152]{1,0:T(8,128)(2,1)S(1)} %get-tuple-element.4), channel_id=1, source_target_pairs={{0,224},{1,25},{2,226},{3,27},{4,228},{5,29},{6,230},{7,31},{8,232... | collective-permute-start | bytes 1327112 | tf_op jit(solution)/shard_map/ppermute | solution.py:34
  95.9 5.4 %multiply_reduce_fusion.1 = f32[384,1152]{1,0:T(8,128)S(1)} fusion(f32[4]{0:T(128)S(1)} %mul.204, bf16[2,256,384]{2,1,0:T(8,128)(2,1)S(1)} %copy-done.7, bf16[2,256,384]{2,1,0:T(8,128)(2,1)S(1)} %copy-done.8, bf16[2,64,1152]{2,1,0:T(8,128)(2,1)S(1)} %copy-done.18, bf16[2,64,1152]{2,1,0:T(8,128)(2,1)} %collective-permute-done.3, ...), kind=kOutput, calls=%fused_computation.1 | convolution fusion | flops 928333824 | bytes 4915216 | tf_op jit(solution)/shard_map/bsf,bsd->bfd/dot_general | solution.py:194
  105.7 5.8 %collective-permute-done.14 = bf16[96,1152]{1,0:T(8,128)(2,1)S(1)} collective-permute-done((bf16[96,1152]{1,0:T(8,128)(2,1)S(1)}, bf16[96,1152]{1,0:T(8,128)(2,1)S(1)}, u32[]{:S(2)}, u32[]{:S(2)}) %collective-permute-start.14) | collective-permute-done | bytes 221216 | tf_op jit(solution)/shard_map/ppermute | solution.py:34
  113.4 4.9 %collective-permute-done.17 = bf16[2,48,1152]{2,1,0:T(8,128)(2,1)S(1)} collective-permute-done((bf16[2,48,1152]{2,1,0:T(8,128)(2,1)S(1)}, bf16[2,48,1152]{2,1,0:T(8,128)(2,1)S(1)}, u32[]{:S(2)}, u32[]{:S(2)}) %collective-permute-start.17) | collective-permute-done | bytes 221216 | tf_op jit(solution)/shard_map/ppermute | solution.py:34
  119.8 2.5 collective-permute-start.18
  128.4 4.4 %collective-permute-start.19 = (bf16[2,12,1152]{2,1,0:T(8,128)(2,1)}, bf16[2,12,1152]{2,1,0:T(8,128)(2,1)}, u32[]{:S(2)}, u32[]{:S(2)}) collective-permute-start(bf16[2,12,1152]{2,1,0:T(8,128)(2,1)} %slice.144), channel_id=1, source_target_pairs={{0,128},{1,129},{2,130},{3,131},{4,132},{5,133},{6,134},{7,135},{8... | collective-permute-start | bytes 165896 | tf_op jit(solution)/shard_map/ppermute | solution.py:34
  132.9 152.3 %all-reduce = f32[128]{0:T(128)S(1)} all-reduce(f32[128]{0:T(128)S(1)} %bitcast_dynamic-update-slice_fusion), channel_id=2, replica_groups=mesh['dp'=64,'mp'=4] {'dp'}, use_global_device_ids=true, to_apply=%add | all-reduce | flops 128 | bytes 1024
  (141 shorter events, 42.5 us)
Async XLA Ops:
  0.6 12.7 %copy-start = (bf16[1152,1536]{1,0:T(8,128)(2,1)S(1)}, bf16[1152,1536]{1,0:T(8,128)(2,1)}, u32[]{:S(2)}) copy-start(bf16[1152,1536]{1,0:T(8,128)(2,1)} %param.11) | copy-start | bytes 10616836
  3.5 23.1 %collective-permute-start.8 = (bf16[2,64,1152]{2,1,0:T(8,128)(2,1)}, bf16[2,64,1152]{2,1,0:T(8,128)(2,1)}, u32[]{:S(2)}, u32[]{:S(2)}) collective-permute-start(bf16[2,64,1152]{2,1,0:T(8,128)(2,1)} %broadcast_multiply_fusion), channel_id=1, source_target_pairs={{0,4},{1,5},{2,6},{3,7},{4,2},{5,3},{6,0},{7,1},{8,12},{9,13},{10,... | collective-permute-start | bytes 884744 | tf_op jit(solution)/shard_map/ppermute | solution.py:34
  5.7 17.5 %collective-permute-start.3 = (bf16[2,64,1152]{2,1,0:T(8,128)(2,1)}, bf16[2,64,1152]{2,1,0:T(8,128)(2,1)}, u32[]{:S(2)}, u32[]{:S(2)}) collective-permute-start(bf16[2,64,1152]{2,1,0:T(8,128)(2,1)} %broadcast_multiply_fusion), channel_id=1, source_target_pairs={{0,6},{1,7},{2,4},{3,5},{4,0},{5,1},{6,2},{7,3},{8,14},{9,15},{10,... | collective-permute-start | bytes 884744 | tf_op jit(solution)/shard_map/ppermute | solution.py:34
  5.7 20.8 %collective-permute-start.7 = (bf16[2,64,1152]{2,1,0:T(8,128)(2,1)}, bf16[2,64,1152]{2,1,0:T(8,128)(2,1)}, u32[]{:S(2)}, u32[]{:S(2)}) collective-permute-start(bf16[2,64,1152]{2,1,0:T(8,128)(2,1)} %param.8), channel_id=1, source_target_pairs={{0,6},{1,7},{2,4},{3,5},{4,0},{5,1},{6,2},{7,3},{8,14},{9,15},{10,... | collective-permute-start | bytes 884744 | tf_op jit(solution)/shard_map/ppermute | solution.py:34
  6.3 17.0 %collective-permute-start.1 = (bf16[2,64,1152]{2,1,0:T(8,128)(2,1)}, bf16[2,64,1152]{2,1,0:T(8,128)(2,1)}, u32[]{:S(2)}, u32[]{:S(2)}) collective-permute-start(bf16[2,64,1152]{2,1,0:T(8,128)(2,1)} %param.8), channel_id=1, source_target_pairs={{0,4},{1,5},{2,6},{3,7},{4,2},{5,3},{6,0},{7,1},{8,12},{9,13},{10,... | collective-permute-start | bytes 884744 | tf_op jit(solution)/shard_map/ppermute | solution.py:34
  10.9 24.2 %collective-permute-start = (bf16[4,64,1152]{2,1,0:T(8,128)(2,1)}, bf16[4,64,1152]{2,1,0:T(8,128)(2,1)}, u32[]{:S(2)}, u32[]{:S(2)}) collective-permute-start(bf16[4,64,1152]{2,1,0:T(8,128)(2,1)} %pad_maximum_fusion.4), channel_id=1, source_target_pairs={{0,1},{1,0},{2,3},{3,2},{4,5},{5,4},{6,7},{7,6},{8,9},{9,8},{10,11... | collective-permute-start | bytes 1769480 | tf_op jit(solution)/shard_map/ppermute | solution.py:34
  23.2 10.9 %collective-permute-start.4 = (bf16[2,64,1152]{2,1,0:T(8,128)(2,1)}, bf16[2,64,1152]{2,1,0:T(8,128)(2,1)S(1)}, u32[]{:S(2)}, u32[]{:S(2)}) collective-permute-start(bf16[2,64,1152]{2,1,0:T(8,128)(2,1)} %collective-permute-done.3), channel_id=1, source_target_pairs={{0,6},{1,7},{2,4},{3,5},{4,0},{5,1},{6,2},{7,3},{8,14},{9,15},{10,... | collective-permute-start | bytes 884744 | tf_op jit(solution)/shard_map/ppermute | solution.py:34
  23.3 10.8 %collective-permute-start.2 = (bf16[2,64,1152]{2,1,0:T(8,128)(2,1)}, bf16[2,64,1152]{2,1,0:T(8,128)(2,1)S(1)}, u32[]{:S(2)}, u32[]{:S(2)}) collective-permute-start(bf16[2,64,1152]{2,1,0:T(8,128)(2,1)} %collective-permute-done.1), channel_id=1, source_target_pairs={{0,4},{1,5},{2,6},{3,7},{4,2},{5,3},{6,0},{7,1},{8,12},{9,13},{10,... | collective-permute-start | bytes 884744 | tf_op jit(solution)/shard_map/ppermute | solution.py:34
  27.7 9.5 %collective-permute-start.9 = (bf16[4,64,1152]{2,1,0:T(8,128)(2,1)S(1)}, bf16[4,64,1152]{2,1,0:T(8,128)(2,1)S(1)}, u32[]{:S(2)}, u32[]{:S(2)}) collective-permute-start(bf16[4,64,1152]{2,1,0:T(8,128)(2,1)S(1)} %pad_maximum_fusion.7), channel_id=1, source_target_pairs={{0,1},{1,0},{2,3},{3,2},{4,5},{5,4},{6,7},{7,6},{8,9},{9,8},{10,11... | collective-permute-start | bytes 1769480 | tf_op jit(solution)/shard_map/ppermute | solution.py:34
  28.9 9.1 %collective-permute-start.6 = (bf16[4,64,1152]{2,1,0:T(8,128)(2,1)S(1)}, bf16[4,64,1152]{2,1,0:T(8,128)(2,1)S(1)}, u32[]{:S(2)}, u32[]{:S(2)}) collective-permute-start(bf16[4,64,1152]{2,1,0:T(8,128)(2,1)S(1)} %pad_maximum_fusion.6), channel_id=1, source_target_pairs={{0,1},{1,0},{2,3},{3,2},{4,5},{5,4},{6,7},{7,6},{8,9},{9,8},{10,11... | collective-permute-start | bytes 1769480 | tf_op jit(solution)/shard_map/ppermute | solution.py:34
  35.1 22.8 %collective-permute-start.5 = (bf16[4,64,1152]{2,1,0:T(8,128)(2,1)}, bf16[4,64,1152]{2,1,0:T(8,128)(2,1)}, u32[]{:S(2)}, u32[]{:S(2)}) collective-permute-start(bf16[4,64,1152]{2,1,0:T(8,128)(2,1)} %pad_maximum_fusion.5), channel_id=1, source_target_pairs={{0,1},{1,0},{2,3},{3,2},{4,5},{5,4},{6,7},{7,6},{8,9},{9,8},{10,11... | collective-permute-start | bytes 1769480 | tf_op jit(solution)/shard_map/ppermute | solution.py:34
  76.6 1.3 collective-permute-start.10
  77.9 3.7 %collective-permute-start.11 = (f32[2,2]{1,0:T(2,128)S(1)}, f32[2,2]{1,0:T(2,128)S(1)}, u32[]{:S(2)}, u32[]{:S(2)}) collective-permute-start(f32[2,2]{1,0:T(2,128)S(1)} %fusion.95), channel_id=1, source_target_pairs={{0,4},{1,5},{2,6},{3,7},{4,0},{5,1},{6,2},{7,3},{8,12},{9,13},{10,... | collective-permute-start | bytes 56 | tf_op jit(solution)/shard_map/ppermute | solution.py:34
  81.5 5.1 %collective-permute-start.12 = (f32[2,2]{1,0:T(2,128)S(1)}, f32[2,2]{1,0:T(2,128)S(1)}, u32[]{:S(2)}, u32[]{:S(2)}) collective-permute-start(f32[2,2]{1,0:T(2,128)S(1)} %add.190), channel_id=1, source_target_pairs={{0,2},{1,3},{2,0},{3,1},{4,6},{5,7},{6,4},{7,5},{8,10},{9,11},{10,... | collective-permute-start | bytes 56 | tf_op jit(solution)/shard_map/ppermute | solution.py:34
  86.8 9.1 %copy-start.18 = (bf16[2,64,1152]{2,1,0:T(8,128)(2,1)S(1)}, bf16[2,64,1152]{2,1,0:T(8,128)(2,1)}, u32[]{:S(2)}) copy-start(bf16[2,64,1152]{2,1,0:T(8,128)(2,1)} %get-tuple-element.16) | copy-start | bytes 884740
  86.8 9.1 %copy-start.22 = (bf16[2,64,1152]{2,1,0:T(8,128)(2,1)S(1)}, bf16[2,64,1152]{2,1,0:T(8,128)(2,1)}, u32[]{:S(2)}) copy-start(bf16[2,64,1152]{2,1,0:T(8,128)(2,1)} %get-tuple-element.12) | copy-start | bytes 884740
  90.1 12.0 %collective-permute-start.15 = (bf16[192,1152]{1,0:T(8,128)(2,1)S(1)}, bf16[192,1152]{1,0:T(8,128)(2,1)S(1)}, u32[]{:S(2)}, u32[]{:S(2)}) collective-permute-start(bf16[192,1152]{1,0:T(8,128)(2,1)S(1)} %get-tuple-element.4), channel_id=1, source_target_pairs={{0,224},{1,25},{2,226},{3,27},{4,228},{5,29},{6,230},{7,31},{8,232... | collective-permute-start | bytes 1327112 | tf_op jit(solution)/shard_map/ppermute | solution.py:34
  95.8 8.3 %collective-permute-start.13 = (bf16[192,1152]{1,0:T(8,128)(2,1)S(1)}, bf16[192,1152]{1,0:T(8,128)(2,1)S(1)}, u32[]{:S(2)}, u32[]{:S(2)}) collective-permute-start(bf16[192,1152]{1,0:T(8,128)(2,1)S(1)} %get-tuple-element.5), channel_id=1, source_target_pairs={{0,32},{1,9},{2,34},{3,11},{4,36},{5,13},{6,38},{7,15},{8,40},{9,1... | collective-permute-start | bytes 1327112 | tf_op jit(solution)/shard_map/ppermute | solution.py:34
  104.3 7.2 %collective-permute-start.14 = (bf16[96,1152]{1,0:T(8,128)(2,1)S(1)}, bf16[96,1152]{1,0:T(8,128)(2,1)S(1)}, u32[]{:S(2)}, u32[]{:S(2)}) collective-permute-start(bf16[96,1152]{1,0:T(8,128)(2,1)S(1)} %slice.142), channel_id=1, source_target_pairs={{0,224},{1,25},{2,226},{3,27},{4,228},{5,29},{6,230},{7,31},{8,232... | collective-permute-start | bytes 663560 | tf_op jit(solution)/shard_map/ppermute | solution.py:34
  105.6 6.5 %collective-permute-start.16 = (bf16[96,1152]{1,0:T(8,128)(2,1)S(1)}, bf16[96,1152]{1,0:T(8,128)(2,1)S(1)}, u32[]{:S(2)}, u32[]{:S(2)}) collective-permute-start(bf16[96,1152]{1,0:T(8,128)(2,1)S(1)} %slice.141), channel_id=1, source_target_pairs={{0,32},{1,9},{2,34},{3,11},{4,36},{5,13},{6,38},{7,15},{8,40},{9,1... | collective-permute-start | bytes 663560 | tf_op jit(solution)/shard_map/ppermute | solution.py:34
  111.6 11.3 %copy-start.28 = (u32[256]{0:T(256)S(1)}, u32[256]{0:T(256)}, u32[]{:S(2)}) copy-start(u32[256]{0:T(256)} %constant.101) | copy-start | bytes 3076
  112.3 6.0 %collective-permute-start.17 = (bf16[2,48,1152]{2,1,0:T(8,128)(2,1)S(1)}, bf16[2,48,1152]{2,1,0:T(8,128)(2,1)S(1)}, u32[]{:S(2)}, u32[]{:S(2)}) collective-permute-start(bf16[2,48,1152]{2,1,0:T(8,128)(2,1)S(1)} %fusion.43), channel_id=1, source_target_pairs={{0,8},{1,33},{2,10},{3,35},{4,12},{5,37},{6,14},{7,39},{8,0},{9,41... | collective-permute-start | bytes 663560 | tf_op jit(solution)/shard_map/ppermute | solution.py:34
  119.8 6.3 %collective-permute-start.18 = (bf16[2,24,1152]{2,1,0:T(8,128)(2,1)}, bf16[2,24,1152]{2,1,0:T(8,128)(2,1)}, u32[]{:S(2)}, u32[]{:S(2)}) collective-permute-start(bf16[2,24,1152]{2,1,0:T(8,128)(2,1)} %slice.143), channel_id=1, source_target_pairs={{0,24},{1,225},{2,26},{3,227},{4,28},{5,229},{6,30},{7,231},{8,16}... | collective-permute-start | bytes 331784 | tf_op jit(solution)/shard_map/ppermute | solution.py:34
  128.4 158.1 %collective-permute-start.19 = (bf16[2,12,1152]{2,1,0:T(8,128)(2,1)}, bf16[2,12,1152]{2,1,0:T(8,128)(2,1)}, u32[]{:S(2)}, u32[]{:S(2)}) collective-permute-start(bf16[2,12,1152]{2,1,0:T(8,128)(2,1)} %slice.144), channel_id=1, source_target_pairs={{0,128},{1,129},{2,130},{3,131},{4,132},{5,133},{6,134},{7,135},{8... | collective-permute-start | bytes 165896 | tf_op jit(solution)/shard_map/ppermute | solution.py:34
  (27 other events, 89.6 us)

commit v2 on v0

v2 whole, which is shorter than its diff:
```python
import jax
import jax.numpy as jnp
import numpy as np
from jax import lax
from jax.experimental import pallas as pl
from jax.experimental.pallas import tpu as pltpu
from jax.sharding import PartitionSpec as P

D = 1152
FF = 6144
SEQ = 256
AXES = ("dp", "mp")

curve_scale = 0.7978845608028654
cubic_term = 0.044715
target_share = 0.5

X, Y, Z, CORES = 4, 4, 8, 2


def coords(i):
    dp, mp = divmod(i, 4)
    z, rest = divmod(dp, 8)
    y, x_lo = divmod(rest, 2)
    x_hi, core = divmod(mp, 2)
    return (x_hi * 2 + x_lo, y, z, core)


def index_of(x, y, z, core):
    x, y, z = x % X, y % Y, z % Z
    return (z * 8 + y * 2 + x % 2) * 4 + (x // 2) * 2 + core


def permute(array, move):
    pairs = [(i, index_of(*move(*coords(i)))) for i in range(X * Y * Z * CORES)]
    return lax.ppermute(array, AXES, pairs)


def z_even(z, y):
    return (z ^ 1, y)


def z_odd(z, y):
    return ((((z - 1) % Z) ^ 1) + 1) % Z, y


def y_even(z, y):
    return (z, y ^ 1)


def y_odd(z, y):
    return (z, ((((y - 1) % Y) ^ 1) + 1) % Y)


STEPS = (
    ((z_even, z_odd), (z_odd, z_even)),
    ((y_even, y_odd), (y_odd, y_even)),
)


def group_of(core, z, y):
    if core == 0:
        return [(zb, yb) for zb in sorted((z, (z + 4) % Z)) for yb in range(Y)]
    return [(zb, y) for zb in range(Z)]


GROUPS = []
for _i in range(X * Y * Z * CORES):
    _x, _y, _z, _core = coords(_i)
    _group = [index_of(_x, yb, zb, _core) for zb, yb in group_of(_core, _z, _y)]
    if _group not in GROUPS:
        GROUPS.append(_group)


def row_table():
    table = np.zeros((CORES, Z, Y, 2, 2, 192), np.int32)
    for core in range(CORES):
        for chain in range(2):
            places = [(z, y) for z in range(Z) for y in range(Y)]
            orders = {place: group_of(core, *place) for place in places}
            for step in reversed(STEPS[core][chain]):
                orders = {place: orders[place] + orders[step(*place)] for place in places}
            for (z, y), order in orders.items():
                assert len(set(order)) == Z * Y
                rows = []
                for number, (zb, yb) in enumerate(order):
                    first = (16, 8)[number % 2]
                    cut = range(first) if chain == 0 else range(first, 24)
                    rows += [(zb * Y + yb) * 48 + row for row in cut]
                table[core, z, y, 0, chain] = rows[192:]
                table[core, z, y, 1, chain] = rows[:192]
    return table


def exchange(array, number, chain):
    def move(x, y, z, core):
        z, y = STEPS[core][chain][number](z, y)
        return (x, y, z, core)

    return permute(array, move)


def gelu_parts(preact):
    square = preact * preact
    half = 0.5 * jnp.tanh(preact * (curve_scale + (curve_scale * cubic_term) * square)) + 0.5
    values = preact * half
    slopes = half + values * (1.0 - half) * (2.0 * curve_scale + (6.0 * curve_scale * cubic_term) * square)
    return (values, slopes)


def dot(left, right, contract):
    return lax.dot_general(left, right, ((contract[:1], contract[1:]), ((), ())), preferred_element_type=jnp.float32)


VMEM = pl.BlockSpec(memory_space=pltpu.VMEM)
HBM = pl.BlockSpec(memory_space=pltpu.HBM)
LANES = (8, 128)
LARGE = 60


def call(kernel, name, outs, args, specs=None, out_specs=None, scratch=(), limit=16):
    return pl.pallas_call(
        kernel,
        out_shape=outs,
        in_specs=specs or [VMEM] * len(args),
        out_specs=out_specs or jax.tree.map(lambda _: VMEM, outs),
        scratch_shapes=scratch,
        compiler_params=pltpu.CompilerParams(vmem_limit_bytes=limit * 2**20),
        cost_estimate=pl.CostEstimate(flops=0, bytes_accessed=0, transcendentals=0),
        name=name,
    )(*args)


def array(shape, kind):
    return jax.ShapeDtypeStruct(shape, kind)


def mask_kernel(left, cotangent, out):
    for e in range(out.shape[0]):
        positions = lax.broadcasted_iota(jnp.int32, out.shape[1:], 0)
        value = cotangent[e].astype(jnp.float32)
        out[e] = jnp.where(positions < left[e, :1, :1], value, 0.0).astype(out.dtype)


def products_of(rows, masked, up, down):
    values, slopes = gelu_parts(dot(rows, up[...], (1, 0)))
    delta = dot(masked, down[...], (1, 0)) * slopes
    return values.astype(jnp.bfloat16), delta.astype(jnp.bfloat16)


def stacked(refs, e):
    return jnp.concatenate([ref[e] for ref in refs], axis=0)


def both_examples(refs):
    return jnp.concatenate([stacked(refs, e) for e in range(2)], axis=0)


def copy_of(source, target, sems, number):
    return pltpu.make_async_copy(source, target, sems.at[number])


def write_example(e, masked, hidden, outs, held, sems):
    hidden_held, masked_held = held
    hidden_held[e] = hidden.T
    masked_held[e] = masked
    copies = [copy_of(kept.at[e], out.at[e], sems, 2 * e + k) for k, (kept, out) in enumerate(zip(held, outs))]
    for copy in copies:
        copy.start()
    return copies


def load_all(sources, targets, sems):
    loads = [copy_of(source, target, sems, k) for k, (source, target) in enumerate(zip(sources, targets))]
    for load in loads:
        load.start()
    return loads


def wait_all(copies):
    for copy in copies:
        copy.wait()


def theirs_kernel(*refs):
    sources, refs = refs[:14], refs[14:]
    hidden_out, masked_out, squares_out, hidden_early, delta_early, *refs = refs
    hidden_held, delta_held, *refs = refs
    held, sems, load_sems, refs = refs[:2], refs[2], refs[3], refs[4:]
    loads = load_all(sources, refs, load_sems)
    wait_all(loads[:3])
    up, down = refs[2], refs[5]
    values, slopes = gelu_parts(dot(both_examples(refs[:2]), up[...], (1, 0)))
    hidden_held[...] = values.astype(jnp.bfloat16)
    wait_all(loads[3:6])
    delta_held[...] = (dot(both_examples(refs[3:5]), down[...], (1, 0)) * slopes).astype(jnp.bfloat16)
    copies = [copy_of(hidden_held, hidden_early, sems, 4), copy_of(delta_held, delta_early, sems, 5)]
    for copy in copies:
        copy.start()
    wait_all(loads[6:])
    inputs, cotans = refs[6:10], refs[10:14]
    for e in range(2):
        rows, masked = stacked(inputs, e), stacked(cotans, e)
        hidden, delta = products_of(rows, masked, up, down)
        copies += write_example(e, masked, hidden, (hidden_out, masked_out), held, sems)
        first = dot(rows, rows, (1, 1)) * dot(delta, delta, (1, 1))
        second = dot(hidden, hidden, (1, 1)) * dot(masked, masked, (1, 1))
        squares_out[e] = jnp.broadcast_to(jnp.sum(first + second), LANES)
    wait_all(copies)


def pass_outs(units, tokens, width):
    return (
        array((2, units, tokens), jnp.bfloat16),
        array((2, tokens, width), jnp.bfloat16),
        array((2, *LANES), jnp.float32),
    )


def pass_scratch(units, tokens, width):
    return [
        pltpu.VMEM((2, units, tokens), jnp.bfloat16),
        pltpu.VMEM((2, tokens, width), jnp.bfloat16),
        pltpu.SemaphoreType.DMA((6,)),
    ]


def load_scratch(args):
    return [pltpu.SemaphoreType.DMA((len(args),))] + [pltpu.VMEM(arg.shape, arg.dtype) for arg in args]


def theirs_pass(inputs, cotans, own, up, down):
    width, units = up.shape
    tokens = 4 * inputs[0].shape[1]
    early = array((tokens, units), jnp.bfloat16)
    args = (*own[:2], up, *own[2:], down, *inputs, *cotans)
    return call(
        theirs_kernel,
        "theirs_pass",
        pass_outs(units, tokens, width) + (early, early),
        args,
        specs=[HBM] * 14,
        out_specs=(HBM, HBM, VMEM, HBM, HBM),
        scratch=[pltpu.VMEM(early.shape, early.dtype)] * 2 + pass_scratch(units, tokens, width) + load_scratch(args),
        limit=LARGE,
    )


def ours_kernel(*refs):
    sources, (hidden_out, masked_out, squares_out), refs = refs[:12], refs[12:15], refs[15:]
    held, sems, load_sems, refs = refs[:2], refs[2], refs[3], refs[4:]
    loads = load_all(sources, refs, load_sems)
    wait_all(loads[:3])
    up, down, hidden_early, delta_early = refs[2], refs[5], refs[10], refs[11]
    values, slopes = gelu_parts(dot(both_examples(refs[:2]), up[...], (1, 0)))
    hidden_late = values.astype(jnp.bfloat16)
    wait_all(loads[3:6])
    delta_late = (dot(both_examples(refs[3:5]), down[...], (1, 0)) * slopes).astype(jnp.bfloat16)
    wait_all(loads[6:])
    inputs, cotans = (*refs[6:8], *refs[:2]), (*refs[8:10], *refs[3:5])
    half = hidden_late.shape[0] // 2
    copies = []
    for e in range(2):
        at = slice(e * half, (e + 1) * half)
        rows, masked = stacked(inputs, e), stacked(cotans, e)
        hidden = jnp.concatenate([hidden_early[at, :], hidden_late[at, :]], axis=0)
        delta = jnp.concatenate([delta_early[at, :], delta_late[at, :]], axis=0)
        copies += write_example(e, masked, hidden, (hidden_out, masked_out), held, sems)
        first = dot(rows, rows, (1, 1)) * dot(delta, delta, (1, 1))
        second = dot(hidden, hidden, (1, 1)) * dot(masked, masked, (1, 1))
        squares_out[e] = jnp.broadcast_to(jnp.sum(first + second), LANES)
    wait_all(copies)


def ours_pass(early, up, down, inputs, cotans):
    width, units = up.shape
    tokens = 4 * inputs[0].shape[1]
    args = (*inputs[2:], up, *cotans[2:], down, *inputs[:2], *cotans[:2], *early)
    return call(
        ours_kernel,
        "ours_pass",
        pass_outs(units, tokens, width),
        args,
        specs=[HBM] * len(args),
        out_specs=(HBM, HBM, VMEM),
        scratch=pass_scratch(units, tokens, width) + load_scratch(args),
        limit=LARGE,
    )


def factors_kernel(examples, first, clip, chip, across, from_left, from_right, scale, count):
    total = (chip[...] + across[...]) + (from_left[...] + from_right[...])
    norms = jnp.sqrt(total)
    threshold = clip[...]
    factors = threshold / jnp.maximum(norms, threshold)
    swapped = jnp.concatenate([factors[2:], factors[:2]], axis=0)
    scale[...] = jnp.where(first[...] == 1, factors, swapped) * (1.0 / examples)
    soft = jnp.floor(jax.nn.sigmoid(4.0 * (threshold - norms) / threshold) * 131072.0 + 0.5) * (1.0 / 131072.0)
    count[...] = (soft[0] + soft[1]) + (soft[2] + soft[3])


TAIL = 16


def tail_rows(count, rows, width):
    count = count[:1, :1]
    whole = jnp.floor(count)
    rest = count - whole
    second = jnp.floor(rest * 256.0) * (1.0 / 256.0)
    rest = rest - second
    third = jnp.floor(rest * 65536.0) * (1.0 / 65536.0)
    row = lax.broadcasted_iota(jnp.int32, (8, 128), 0)
    parts = jnp.where(row == 0, whole, jnp.where(row == 1, second, jnp.where(row == 2, third, rest - third)))
    parts = jnp.where(row < 4, parts, 0.0)
    if width > 128:
        parts = jnp.concatenate([parts, jnp.zeros((8, width - 128), jnp.float32)], axis=1)
    return parts, jnp.zeros((rows - 8, width), jnp.float32)


def count_in(tail):
    return jnp.broadcast_to(jnp.sum(tail[:8, :128], axis=0, keepdims=True), LANES)


def outer_rows(scale, hidden, masked, loads):
    total = None
    for e in range(4):
        wait_all(loads[2 * e : 2 * e + 2])
        piece = scale[e, :1, :1] * dot(hidden[e], masked[e], (1, 0))
        total = piece if total is None else total + piece
    return total


def load_outer(first, refs, hidden, masked, sems):
    rows = hidden.shape[1]
    loads = []
    for e in range(4):
        hidden_from, masked_from = refs[e // 2], refs[2 + e // 2]
        loads.append(copy_of(hidden_from.at[e % 2, pl.ds(first, rows)], hidden.at[e], sems, 2 * e))
        loads.append(copy_of(masked_from.at[e % 2], masked.at[e], sems, 2 * e + 1))
    for load in loads:
        load.start()
    return loads


def outer_send_kernel(scale, count, *refs):
    operands, (out0, out1), (hidden, masked, sems) = refs[:4], refs[4:6], refs[6:]
    rows, width = out1.shape
    total = outer_rows(scale, hidden, masked, load_outer(0, operands, hidden, masked, sems))
    out0[...] = jnp.concatenate([total[:rows], *tail_rows(count[...], TAIL, width)], axis=0).astype(out0.dtype)
    out1[...] = total[rows:].astype(out1.dtype)


def outer_keep_kernel(scale, *refs):
    operands, outs, (hidden, masked, sems) = refs[:4], refs[4:6], refs[6:]
    rows = outs[0].shape[0]
    total = outer_rows(scale, hidden, masked, load_outer(2 * rows, operands, hidden, masked, sems))
    outs[0][...] = total[:rows]
    outs[1][...] = total[rows:]


def outer(kernel, name, rows, tail, kind, scalars, operands):
    _, tokens, width = operands[2].shape
    return call(
        kernel,
        name,
        (array((rows + tail, width), kind), array((rows, width), kind)),
        (*scalars, *operands),
        specs=[VMEM] * len(scalars) + [HBM] * 4,
        scratch=[
            pltpu.VMEM((4, 2 * rows, tokens), jnp.bfloat16),
            pltpu.VMEM((4, tokens, width), jnp.bfloat16),
            pltpu.SemaphoreType.DMA((8,)),
        ],
        limit=LARGE,
    )


def step_first_kernel(count, kept, got, count_out, keep, send):
    rows, width = kept.shape
    half = rows // 2
    message = got[...].astype(jnp.float32)
    total = kept[...] + message[:rows]
    keep[...] = total[:half]
    counted = count[...] + count_in(message[rows:])
    count_out[...] = counted
    send[...] = jnp.concatenate([total[half:], *tail_rows(counted, TAIL, width)], axis=0).astype(send.dtype)


def step_outs(kept, sent, width):
    return (array(LANES, jnp.float32), array((kept, width), jnp.float32), array((sent, width), jnp.bfloat16))


def step_first(count, kept, got):
    rows, width = kept.shape
    return call(step_first_kernel, "step_first", step_outs(rows // 2, rows // 2 + TAIL, width), (count, kept, got))


def step_second_kernel(kept, got, keep, send):
    half = kept.shape[0] // 2
    total = kept[...] + got[...].astype(jnp.float32)
    keep[...] = total[:half]
    send[...] = total[half:].astype(send.dtype)


def step_second(kept, got):
    rows, width = kept.shape
    outs = (array((rows // 2, width), jnp.float32), array((rows // 2, width), jnp.bfloat16))
    return call(step_second_kernel, "step_second", outs, (kept, got))


SIDE = 128


def step_join_kernel(count, kept0, kept1, got0, got1, send):
    rows, width = kept0.shape
    message = got0[...].astype(jnp.float32)
    total0 = kept0[...] + message[:rows]
    total1 = kept1[...] + got1[...].astype(jnp.float32)
    counted = count[...] + count_in(message[rows:])
    pieces = []
    for at in range(0, rows, 24):
        pieces += [total0[at : at + 16], total1[at : at + 8], total0[at + 16 : at + 24], total1[at + 8 : at + 24]]
    side = tail_rows(counted, 24, SIDE)
    side = jnp.concatenate(list(side) * (rows // 12), axis=0)
    send[...] = jnp.concatenate([jnp.concatenate(pieces, axis=0), side], axis=1).astype(send.dtype)


def step_join(count, kept0, kept1, got0, got1):
    rows, width = kept0.shape
    return call(step_join_kernel, "step_join", array((2 * rows, width + SIDE), jnp.bfloat16), (count, kept0, kept1, got0, got1))


def step_last_kernel(got, out, count):
    rows, width = out.shape
    message = got[...].astype(jnp.float32)
    chunks = [message[at : at + rows] for at in range(0, message.shape[0], rows)]
    while len(chunks) > 1:
        chunks = [a + b for a, b in zip(chunks[::2], chunks[1::2])]
    out[...] = chunks[0][:, :width]
    count[...] = jnp.broadcast_to(jnp.sum(chunks[0][:8, width:], axis=0, keepdims=True), LANES)


def step_last(got, rows, width):
    outs = (array((rows, width), jnp.float32), array(LANES, jnp.float32))
    return call(step_last_kernel, "step_last", outs, (got,))


def right(x, y, z, core):
    return (x + 1, y, z, core)


def left(x, y, z, core):
    return (x - 1, y, z, core)


def other_core(x, y, z, core):
    return (x, y, z, 1 - core)


def opposite(x, y, z, core):
    return (x + 2, y, z, core)


def swap_cores(*arrays):
    return [permute(array, other_core) for array in arrays]


def after(array, *others):
    return lax.optimization_barrier((array, *others))[0]


def per_device(inputs, cotangent, lengths, up_weight, down_weight, clip_ratio, count_noise):
    dp = lax.axis_index("dp")
    mp = lax.axis_index("mp")
    z, y, x_lo, core = dp // 8, (dp // 2) % 4, dp % 2, mp % 2
    local = inputs.shape[1]

    units = up_weight.shape[1]

    in_l = permute(inputs, right)
    in_r = permute(inputs, left)
    real = jnp.broadcast_to((lengths - mp * local)[:, None, None], (lengths.shape[0], *LANES))
    masked = call(mask_kernel, "mask", array(cotangent.shape, cotangent.dtype), (real, cotangent))
    co_r = permute(masked, left)
    co_l = permute(masked, right)
    in_s, co_s = swap_cores(inputs, masked)

    table = jnp.asarray(row_table())
    rows = lax.dynamic_slice(table, (core, z, y, 0, 0, 0), (1, 1, 1, 2, 2, 192)).reshape(-1) + x_lo * 24
    pick = (lax.broadcasted_iota(jnp.int32, (units, rows.shape[0]), 0) == rows[None, :]).astype(jnp.bfloat16)
    up = jnp.einsum("df,fp->dp", up_weight, pick, preferred_element_type=jnp.bfloat16)
    down = jnp.einsum("fd,fp->dp", down_weight, pick, preferred_element_type=jnp.bfloat16)

    in_o = permute(after(in_l, up, down), right)
    co_o = permute(after(co_r, up, down), left)
    in_ls, in_rs, co_ls, co_rs = swap_cores(in_l, in_r, co_l, co_r)
    hidden_theirs, masked_theirs, squares_theirs, *early = theirs_pass(
        (in_l, in_ls, in_r, in_rs), (co_l, co_ls, co_r, co_rs), (inputs, in_s, masked, co_s), up, down
    )
    in_os, co_os = swap_cores(after(in_o, squares_theirs), after(co_o, squares_theirs))
    hidden_ours, masked_ours, squares_ours = ours_pass(early, up, down, (inputs, in_s, in_o, in_os), (masked, co_s, co_o, co_os))

    first = jnp.where(x_lo == 0, squares_ours, squares_theirs)
    second = jnp.where(x_lo == 0, squares_theirs, squares_ours)
    both = jnp.concatenate([first, second], axis=0)
    both = both + permute(both, other_core)
    examples_all = lax.axis_size("dp") * lengths.shape[0]
    clip = clip_ratio[0] * jnp.sqrt(jnp.float32(SEQ * D * FF))
    scale, count = call(
        lambda *refs: factors_kernel(examples_all, *refs),
        "factors",
        (array((4, *LANES), jnp.float32), array(LANES, jnp.float32)),
        (
            jnp.broadcast_to((x_lo == 0).astype(jnp.int32), LANES),
            jnp.broadcast_to(clip, LANES),
            both,
            permute(both, opposite),
            permute(both, right),
            permute(both, left),
        ),
    )

    quarter = rows.shape[0] // 4
    operands = (hidden_ours, hidden_theirs, masked_ours, masked_theirs)
    send0, send1 = outer(outer_send_kernel, "outer_send", quarter, TAIL, jnp.bfloat16, (scale, count), operands)
    got0, got1 = exchange(send0, 0, 0), exchange(send1, 0, 1)
    keep0, keep1 = outer(outer_keep_kernel, "outer_keep", quarter, 0, jnp.float32, (scale,), operands)
    count, keep0, send0 = step_first(count, keep0, got0)
    got0 = exchange(send0, 1, 0)
    keep1, send1 = step_second(keep1, got1)
    got1 = exchange(send1, 1, 1)
    send = step_join(count, keep0, keep1, got0, got1)
    got = lax.all_to_all(send, AXES, 0, 0, axis_index_groups=GROUPS, tiled=True)
    grad_down, count = step_last(got, 4 * quarter // (Z * Y), send.shape[1] - SIDE)
    share = (count[0, 0] + count_noise[0]) / examples_all
    ratio_next = clip_ratio * jnp.exp(-(share - target_share))
    return (grad_down, ratio_next)


def solution(mesh):
    return jax.shard_map(
        per_device,
        mesh=mesh,
        in_specs=(
            P("dp", "mp", None),
            P("dp", "mp", None),
            P("dp"),
            P(None, "mp"),
            P("mp", None),
            P(),
            P(),
        ),
        out_specs=(P(("mp", "dp"), None), P()),
        check_vma=False,
    )
```

time: 431 us -> 108 us (0.25)
  waiting for transfers between devices: 219 us -> 26.1 us
  blocking collectives: 164 us -> 0 us
  Pallas kernels: 0 us -> 30.1 us
  starting transfers between devices: 0.11 us -> 29.5 us
  between operations: 17 us -> 3.96 us
  matrix products: 19.5 us -> 8.51 us
  local copies, waits for them, and re-layouts: 0.9 us -> 6.15 us
    unnamed x4 -> x0, waiting for transfers between devices: 172 us -> none
    psum x2 -> x0, blocking collectives: 164 us -> none  [the longest x1 155 us: per_device(): count_total = lax.psum(jnp.sum(soft), 'dp')]
    all_gather x2 -> x0, waiting for transfers between devices: 47.5 us -> none  [the longest x1 25.2 us: per_device(): lax.all_gather(cotangent, 'mp', axis=1, tiled=True)]
    pallas_call x0 -> x10, Pallas kernels: none -> 30.1 us  [call(): pl.pallas_call(kernel, out_shape=outs, in_specs=specs or [VMEM] * len(arg...]
    ppermute x0 -> x22, starting transfers between devices: none -> 23.8 us  [permute(): return lax.ppermute(array, AXES, pairs)]
    ppermute x0 -> x22, waiting for transfers between devices: none -> 13.1 us  [permute(): return lax.ppermute(array, AXES, pairs)]
    all_to_all x0 -> x1, waiting for transfers between devices: none -> 13.1 us  [per_device(): got = lax.all_to_all(send, AXES, 0, 0, axis_index_groups=GROUPS, tiled=True)]
    dot_general x7 -> x2, matrix products: 19.5 us -> 8.51 us  [the longest x1 4.3 us: per_device(): jnp.einsum('fd,fp->dp', down_weight, pick, preferred_element_type=jnp.bfl...]
  transfers between devices with their start and end apart: 3 -> 23, of which waited for: 3 -> 8; matrix products, arithmetic and copies ran while one was open for 1% -> 9% of each run, Pallas kernels for 0% -> 14%
where the time goes in v2:
time: 108 us; the launch traced here: 107 us
  Pallas kernels  30.1 us (28%)
  starting transfers between devices  29.5 us (27%)
  waiting for transfers between devices  26.1 us (24%)
  matrix products  8.51 us (8%)
  local copies, waits for them, and re-layouts  6.15 us (6%)
  between operations  3.96 us (4%)
  other arithmetic  2.21 us (2%)
    pallas_call x10, Pallas kernels, call(): pl.pallas_call(kernel, out_shape=outs, in_specs=specs or [VMEM] * len(arg...  30.1 us
    ppermute x22, starting transfers between devices, permute(): return lax.ppermute(array, AXES, pairs)  23.8 us
    ppermute x22, waiting for transfers between devices, permute(): return lax.ppermute(array, AXES, pairs)  13.1 us
    all_to_all x1, waiting for transfers between devices, per_device(): got = lax.all_to_all(send, AXES, 0, 0, axis_index_groups=GROUPS, tiled=True)  13.1 us
    all_to_all x1, starting transfers between devices, per_device(): got = lax.all_to_all(send, AXES, 0, 0, axis_index_groups=GROUPS, tiled=True)  5.74 us
    unnamed x24, local copies, waits for them, and re-layouts  5.48 us
    dot_general x1, matrix products, per_device(): jnp.einsum('fd,fp->dp', down_weight, pick, preferred_element_type=jnp.bfl...  4.3 us
    dot_general x1, matrix products, per_device(): jnp.einsum('df,fp->dp', up_weight, pick, preferred_element_type=jnp.bfloa...  4.21 us
  transfers between devices with their start and end apart: 23, of which 8 were waited for; matrix products, arithmetic and copies ran while one was open for 9% of the time, Pallas kernels for 14%

profile of v2, /device:TPU:6, one launch (start us, length us, event | category | flops | bytes accessed | tf_op | source)
XLA Modules:
  0.0 106.6 jit_solution(10110307584752685689)
XLA Ops:
  1.5 1.1 %copy-done.4 = bf16[2,64,1152]{2,1,0:T(8,128)(2,1)S(1)} copy-done((bf16[2,64,1152]{2,1,0:T(8,128)(2,1)S(1)}, bf16[2,64,1152]{2,1,0:T(8,128)(2,1)}, u32[]{:S(2)}) %copy-start.4) | copy-done | bytes 294936
  4.3 2.4 %collective-permute-start.7 = (bf16[2,64,1152]{2,1,0:T(8,128)(2,1)}, bf16[2,64,1152]{2,1,0:T(8,128)(2,1)}, u32[]{:S(2)}, u32[]{:S(2)}) collective-permute-start(bf16[2,64,1152]{2,1,0:T(8,128)(2,1)} %mask.1.refs_3_.refs_8_), channel_id=1, source_target_pairs={{0,4},{1,5},{2,6},{3,7},{4,2},{5,3},{6,0},{7,1},{8,12},{9,13},{10,... | collective-permute-start | bytes 884744 | tf_op jit(solution)/shard_map/ppermute | solution.py:36
  9.6 4.2 %fusion.2.refs_2_ = bf16[1152,768]{1,0:T(8,128)(2,1)} fusion(bf16[1152,1536]{1,0:T(8,128)(2,1)S(1)} %copy-done, s32[768]{0:T(1024)S(1)} %add.49), kind=kOutput, calls=%fused_computation.3 | convolution fusion | flops 2719088640 | bytes 5311488 | tf_op jit(solution)/shard_map/df,fp->dp/dot_general | solution.py:491
  13.8 1.2 %collective-permute-done.9.refs_12_ = bf16[2,64,1152]{2,1,0:T(8,128)(2,1)} collective-permute-done((bf16[2,64,1152]{2,1,0:T(8,128)(2,1)}, bf16[2,64,1152]{2,1,0:T(8,128)(2,1)}, u32[]{:S(2)}, u32[]{:S(2)}) %collective-permute-start.9) | collective-permute-done | bytes 294944 | tf_op jit(solution)/shard_map/ppermute | solution.py:36
  15.5 4.3 %fusion.3.refs_5_ = bf16[1152,768]{1,0:T(8,128)(2,1)} fusion(bf16[1536,1152]{1,0:T(8,128)(2,1)S(1)} %copy-done.11, s32[768]{0:T(1024)S(1)} %add.49), kind=kOutput, calls=%fused_computation.4 | convolution fusion | flops 2719088640 | bytes 5311488 | tf_op jit(solution)/shard_map/fd,fp->dp/dot_general | solution.py:492
  20.8 3.0 %collective-permute-start.1 = (bf16[2,64,1152]{2,1,0:T(8,128)(2,1)}, bf16[2,64,1152]{2,1,0:T(8,128)(2,1)}, u32[]{:S(2)}, u32[]{:S(2)}) collective-permute-start(bf16[2,64,1152]{2,1,0:T(8,128)(2,1)} %collective-permute-done.refs_6_), channel_id=1, source_target_pairs={{0,4},{1,5},{2,6},{3,7},{4,2},{5,3},{6,0},{7,1},{8,12},{9,13},{10,... | collective-permute-start | bytes 884744 | tf_op jit(solution)/shard_map/ppermute | solution.py:36
  23.8 8.8 %theirs_pass.1 = (bf16[2,768,256]{2,1,0:T(8,128)(2,1)}, bf16[2,256,1152]{2,1,0:T(8,128)(2,1)}, f32[2,8,128]{2,1,0:T(8,128)}, bf16[256,768]{1,0:T(8,128)(2,1)}, bf16[256,768]{1,0:T(8,128)(2,1)}) custom-call(bf16[2,64,1152]{2,1,0:T(8,128)(2,1)} %refs_6_.1, bf16[2,64,1152]{2,1,0:T(8,128)(2,1)} %copy-done.9, bf16[1152,768]{1,0:T(8,128)(2,1)} %fusion.2.refs_2_, ...), custom_call_target="tpu_custom_call" | custom-call | tf_op jit(solution)/shard_map/theirs_pass/pallas_call | solution.py:122
  33.3 1.4 %collective-permute-done.13.refs_4_ = bf16[2,64,1152]{2,1,0:T(8,128)(2,1)} collective-permute-done((bf16[2,64,1152]{2,1,0:T(8,128)(2,1)}, bf16[2,64,1152]{2,1,0:T(8,128)(2,1)}, u32[]{:S(2)}, u32[]{:S(2)}) %collective-permute-start.13) | collective-permute-done | bytes 294944 | tf_op jit(solution)/shard_map/ppermute | solution.py:36
  35.1 6.7 %ours_pass.1 = (bf16[2,768,256]{2,1,0:T(8,128)(2,1)}, bf16[2,256,1152]{2,1,0:T(8,128)(2,1)}, f32[2,8,128]{2,1,0:T(8,128)}) custom-call(bf16[2,64,1152]{2,1,0:T(8,128)(2,1)} %collective-permute-done.1.refs_0_, bf16[2,64,1152]{2,1,0:T(8,128)(2,1)} %collective-permute-done.11.refs_1_, bf16[1152,768]{1,0:T(8,128)(2,1)} %fusion.2.refs_2_, ...), custom_call_target="tpu_custom_call" | custom-call | tf_op jit(solution)/shard_map/ours_pass/pallas_call | solution.py:122
  43.7 1.3 %collective-permute-start.15 = (f32[4,8,128]{2,1,0:T(8,128)S(1)}, f32[4,8,128]{2,1,0:T(8,128)}, u32[]{:S(2)}, u32[]{:S(2)}) collective-permute-start(f32[4,8,128]{2,1,0:T(8,128)S(1)} %fusion.6.refs_2_), channel_id=1, source_target_pairs={{0,2},{1,3},{2,0},{3,1},{4,6},{5,7},{6,4},{7,5},{8,10},{9,11},{10,... | collective-permute-start | bytes 49160 | tf_op jit(solution)/shard_map/ppermute | solution.py:36
  45.7 1.3 %collective-permute-start.17 = (f32[4,8,128]{2,1,0:T(8,128)S(1)}, f32[4,8,128]{2,1,0:T(8,128)}, u32[]{:S(2)}, u32[]{:S(2)}) collective-permute-start(f32[4,8,128]{2,1,0:T(8,128)S(1)} %fusion.6.refs_2_), channel_id=1, source_target_pairs={{0,6},{1,7},{2,4},{3,5},{4,0},{5,1},{6,2},{7,3},{8,14},{9,15},{10,... | collective-permute-start | bytes 49160 | tf_op jit(solution)/shard_map/ppermute | solution.py:36
  47.6 1.4 %collective-permute-done.15.refs_3_ = f32[4,8,128]{2,1,0:T(8,128)} collective-permute-done((f32[4,8,128]{2,1,0:T(8,128)S(1)}, f32[4,8,128]{2,1,0:T(8,128)}, u32[]{:S(2)}, u32[]{:S(2)}) %collective-permute-start.15) | collective-permute-done | bytes 16416 | tf_op jit(solution)/shard_map/ppermute | solution.py:36
  49.0 1.7 %collective-permute-done.17.refs_5_ = f32[4,8,128]{2,1,0:T(8,128)} collective-permute-done((f32[4,8,128]{2,1,0:T(8,128)S(1)}, f32[4,8,128]{2,1,0:T(8,128)}, u32[]{:S(2)}, u32[]{:S(2)}) %collective-permute-start.17) | collective-permute-done | bytes 16416 | tf_op jit(solution)/shard_map/ppermute | solution.py:36
  52.7 4.8 %outer_send.1 = (bf16[208,1152]{1,0:T(8,128)(2,1)}, bf16[192,1152]{1,0:T(8,128)(2,1)}) custom-call(f32[4,8,128]{2,1,0:T(8,128)} %copy-done.5, f32[8,128]{1,0:T(8,128)} %copy-done.6, bf16[2,768,256]{2,1,0:T(8,128)(2,1)} %get-tuple-element.37.refs_0_, bf16[2,768,256]{2,1,0:T(8,128)(2,1)} %get-tuple-element.38.refs_1_, ...), custom_call_target="tpu_custom_call" | custom-call | tf_op jit(solution)/shard_map/outer_send/pallas_call | solution.py:122
  57.5 2.0 %collective-permute-start.18 = (bf16[208,1152]{1,0:T(8,128)(2,1)}, bf16[208,1152]{1,0:T(8,128)(2,1)S(1)}, u32[]{:S(2)}, u32[]{:S(2)}) collective-permute-start(bf16[208,1152]{1,0:T(8,128)(2,1)} %get-tuple-element.42), channel_id=1, source_target_pairs={{0,32},{1,9},{2,34},{3,11},{4,36},{5,13},{6,38},{7,15},{8,40},{9,1... | collective-permute-start | bytes 1437704 | tf_op jit(solution)/shard_map/ppermute | solution.py:36
  59.5 4.9 %collective-permute-start.19 = (bf16[192,1152]{1,0:T(8,128)(2,1)}, bf16[192,1152]{1,0:T(8,128)(2,1)}, u32[]{:S(2)}, u32[]{:S(2)}) collective-permute-start(bf16[192,1152]{1,0:T(8,128)(2,1)} %get-tuple-element.46), channel_id=1, source_target_pairs={{0,224},{1,25},{2,226},{3,27},{4,228},{5,29},{6,230},{7,31},{8,232... | collective-permute-start | bytes 1327112 | tf_op jit(solution)/shard_map/ppermute | solution.py:36
  64.4 5.0 %outer_keep.1 = (f32[192,1152]{1,0:T(8,128)}, f32[192,1152]{1,0:T(8,128)}) custom-call(f32[4,8,128]{2,1,0:T(8,128)} %copy-done.5, bf16[2,768,256]{2,1,0:T(8,128)(2,1)} %get-tuple-element.37.refs_0_, bf16[2,768,256]{2,1,0:T(8,128)(2,1)} %get-tuple-element.38.refs_1_, bf16[2,256,1152]{2,1,0:T(8,128)(2,1)} %get-tuple-element.39.refs_2_, ...), custom_call_target="tpu_custom_call" | custom-call | tf_op jit(solution)/shard_map/outer_keep/pallas_call | solution.py:122
  69.5 1.2 %copy-done.3 = f32[192,1152]{1,0:T(8,128)S(1)} copy-done((f32[192,1152]{1,0:T(8,128)S(1)}, f32[192,1152]{1,0:T(8,128)}, u32[]{:S(2)}) %copy-start.3) | copy-done | bytes 884760
  70.8 3.0 %collective-permute-start.20 = (bf16[112,1152]{1,0:T(8,128)(2,1)S(1)}, bf16[112,1152]{1,0:T(8,128)(2,1)S(1)}, u32[]{:S(2)}, u32[]{:S(2)}) collective-permute-start(bf16[112,1152]{1,0:T(8,128)(2,1)S(1)} %get-tuple-element.48), channel_id=1, source_target_pairs={{0,224},{1,25},{2,226},{3,27},{4,228},{5,29},{6,230},{7,31},{8,232... | collective-permute-start | bytes 774152 | tf_op jit(solution)/shard_map/ppermute | solution.py:36
  73.8 1.2 %copy-done.2 = f32[192,1152]{1,0:T(8,128)S(1)} copy-done((f32[192,1152]{1,0:T(8,128)S(1)}, f32[192,1152]{1,0:T(8,128)}, u32[]{:S(2)}) %copy-start.2) | copy-done | bytes 884760
  76.2 5.9 %collective-permute-done.21.got1 = bf16[96,1152]{1,0:T(8,128)(2,1)S(1)} collective-permute-done((bf16[96,1152]{1,0:T(8,128)(2,1)S(1)}, bf16[96,1152]{1,0:T(8,128)(2,1)S(1)}, u32[]{:S(2)}, u32[]{:S(2)}) %collective-permute-start.21) | collective-permute-done | bytes 221216 | tf_op jit(solution)/shard_map/ppermute | solution.py:36
  83.1 5.7 %all-to-all-start = ((bf16[8,24,1280]{2,1,0:T(8,128)(2,1)}), bf16[8,24,1280]{2,1,0:T(8,128)(2,1)}, u32[]{:S(2)}, u32[]{:S(2)}) async-start(bf16[8,24,1280]{2,1,0:T(8,128)(2,1)} %bitcast.13), calls=%async_computation | async-start | bytes 983040 | tf_op jit(solution)/shard_map/all_to_all | solution.py:533
  89.5 13.1 %all-to-all-done = bf16[8,24,1280]{2,1,0:T(8,128)(2,1)} async-done(((bf16[8,24,1280]{2,1,0:T(8,128)(2,1)}), bf16[8,24,1280]{2,1,0:T(8,128)(2,1)}, u32[]{:S(2)}, u32[]{:S(2)}) %all-to-all-start) | async-done | bytes 491552 | tf_op jit(solution)/shard_map/all_to_all | solution.py:533
  102.5 1.7 %step_last.1 = (f32[24,1152]{1,0:T(8,128)}, f32[8,128]{1,0:T(8,128)S(1)}) custom-call(bf16[192,1280]{1,0:T(8,128)(2,1)} %bitcast.4.got), custom_call_target="tpu_custom_call" | custom-call | tf_op jit(solution)/shard_map/step_last/pallas_call | solution.py:122
  (68 shorter events, 15.3 us)
Async XLA Ops:
  3.5 11.4 %collective-permute-start.9 = (bf16[2,64,1152]{2,1,0:T(8,128)(2,1)}, bf16[2,64,1152]{2,1,0:T(8,128)(2,1)}, u32[]{:S(2)}, u32[]{:S(2)}) collective-permute-start(bf16[2,64,1152]{2,1,0:T(8,128)(2,1)} %mask.1.refs_3_.refs_8_), channel_id=1, source_target_pairs={{0,6},{1,7},{2,4},{3,5},{4,0},{5,1},{6,2},{7,3},{8,14},{9,15},{10,... | collective-permute-start | bytes 884744 | tf_op jit(solution)/shard_map/ppermute | solution.py:36
  4.3 10.6 %collective-permute-start.7 = (bf16[2,64,1152]{2,1,0:T(8,128)(2,1)}, bf16[2,64,1152]{2,1,0:T(8,128)(2,1)}, u32[]{:S(2)}, u32[]{:S(2)}) collective-permute-start(bf16[2,64,1152]{2,1,0:T(8,128)(2,1)} %mask.1.refs_3_.refs_8_), channel_id=1, source_target_pairs={{0,4},{1,5},{2,6},{3,7},{4,2},{5,3},{6,0},{7,1},{8,12},{9,13},{10,... | collective-permute-start | bytes 884744 | tf_op jit(solution)/shard_map/ppermute | solution.py:36
  6.8 13.0 %collective-permute-start.3 = (bf16[2,64,1152]{2,1,0:T(8,128)(2,1)}, bf16[2,64,1152]{2,1,0:T(8,128)(2,1)}, u32[]{:S(2)}, u32[]{:S(2)}) collective-permute-start(bf16[2,64,1152]{2,1,0:T(8,128)(2,1)} %mask.1.refs_3_.refs_8_), channel_id=1, source_target_pairs={{0,1},{1,0},{2,3},{3,2},{4,5},{5,4},{6,7},{7,6},{8,9},{9,8},{10,11... | collective-permute-start | bytes 884744 | tf_op jit(solution)/shard_map/ppermute | solution.py:36
  6.8 13.1 %collective-permute-start = (bf16[2,64,1152]{2,1,0:T(8,128)(2,1)}, bf16[2,64,1152]{2,1,0:T(8,128)(2,1)}, u32[]{:S(2)}, u32[]{:S(2)}) collective-permute-start(bf16[2,64,1152]{2,1,0:T(8,128)(2,1)} %refs_6_.1), channel_id=1, source_target_pairs={{0,4},{1,5},{2,6},{3,7},{4,2},{5,3},{6,0},{7,1},{8,12},{9,13},{10,... | collective-permute-start | bytes 884744 | tf_op jit(solution)/shard_map/ppermute | solution.py:36
  7.8 12.5 %collective-permute-start.5 = (bf16[2,64,1152]{2,1,0:T(8,128)(2,1)}, bf16[2,64,1152]{2,1,0:T(8,128)(2,1)}, u32[]{:S(2)}, u32[]{:S(2)}) collective-permute-start(bf16[2,64,1152]{2,1,0:T(8,128)(2,1)} %refs_6_.1), channel_id=1, source_target_pairs={{0,6},{1,7},{2,4},{3,5},{4,0},{5,1},{6,2},{7,3},{8,14},{9,15},{10,... | collective-permute-start | bytes 884744 | tf_op jit(solution)/shard_map/ppermute | solution.py:36
  14.9 5.4 %collective-permute-start.2 = (bf16[2,64,1152]{2,1,0:T(8,128)(2,1)S(1)}, bf16[2,64,1152]{2,1,0:T(8,128)(2,1)S(1)}, u32[]{:S(2)}, u32[]{:S(2)}) collective-permute-start(bf16[2,64,1152]{2,1,0:T(8,128)(2,1)S(1)} %copy-done.8), channel_id=1, source_target_pairs={{0,1},{1,0},{2,3},{3,2},{4,5},{5,4},{6,7},{7,6},{8,9},{9,8},{10,11... | collective-permute-start | bytes 884744 | tf_op jit(solution)/shard_map/ppermute | solution.py:36
  14.9 5.8 %collective-permute-start.10 = (bf16[2,64,1152]{2,1,0:T(8,128)(2,1)}, bf16[2,64,1152]{2,1,0:T(8,128)(2,1)}, u32[]{:S(2)}, u32[]{:S(2)}) collective-permute-start(bf16[2,64,1152]{2,1,0:T(8,128)(2,1)} %collective-permute-done.9.refs_12_), channel_id=1, source_target_pairs={{0,1},{1,0},{2,3},{3,2},{4,5},{5,4},{6,7},{7,6},{8,9},{9,8},{10,11... | collective-permute-start | bytes 884744 | tf_op jit(solution)/shard_map/ppermute | solution.py:36
  19.8 4.0 %collective-permute-start.8 = (bf16[2,64,1152]{2,1,0:T(8,128)(2,1)}, bf16[2,64,1152]{2,1,0:T(8,128)(2,1)}, u32[]{:S(2)}, u32[]{:S(2)}) collective-permute-start(bf16[2,64,1152]{2,1,0:T(8,128)(2,1)} %collective-permute-done.7.refs_10_), channel_id=1, source_target_pairs={{0,1},{1,0},{2,3},{3,2},{4,5},{5,4},{6,7},{7,6},{8,9},{9,8},{10,11... | collective-permute-start | bytes 884744 | tf_op jit(solution)/shard_map/ppermute | solution.py:36
  19.9 3.9 %collective-permute-start.4 = (bf16[2,64,1152]{2,1,0:T(8,128)(2,1)}, bf16[2,64,1152]{2,1,0:T(8,128)(2,1)}, u32[]{:S(2)}, u32[]{:S(2)}) collective-permute-start(bf16[2,64,1152]{2,1,0:T(8,128)(2,1)} %collective-permute-done.refs_6_), channel_id=1, source_target_pairs={{0,1},{1,0},{2,3},{3,2},{4,5},{5,4},{6,7},{7,6},{8,9},{9,8},{10,11... | collective-permute-start | bytes 884744 | tf_op jit(solution)/shard_map/ppermute | solution.py:36
  20.3 3.5 %collective-permute-start.6 = (bf16[2,64,1152]{2,1,0:T(8,128)(2,1)}, bf16[2,64,1152]{2,1,0:T(8,128)(2,1)}, u32[]{:S(2)}, u32[]{:S(2)}) collective-permute-start(bf16[2,64,1152]{2,1,0:T(8,128)(2,1)} %collective-permute-done.5.refs_8_), channel_id=1, source_target_pairs={{0,1},{1,0},{2,3},{3,2},{4,5},{5,4},{6,7},{7,6},{8,9},{9,8},{10,11... | collective-permute-start | bytes 884744 | tf_op jit(solution)/shard_map/ppermute | solution.py:36
  20.4 12.3 %collective-permute-start.12 = (bf16[2,64,1152]{2,1,0:T(8,128)(2,1)}, bf16[2,64,1152]{2,1,0:T(8,128)(2,1)}, u32[]{:S(2)}, u32[]{:S(2)}) collective-permute-start(bf16[2,64,1152]{2,1,0:T(8,128)(2,1)} %collective-permute-done.9.refs_12_), channel_id=1, source_target_pairs={{0,6},{1,7},{2,4},{3,5},{4,0},{5,1},{6,2},{7,3},{8,14},{9,15},{10,... | collective-permute-start | bytes 884744 | tf_op jit(solution)/shard_map/ppermute | solution.py:36
  20.8 12.0 %collective-permute-start.1 = (bf16[2,64,1152]{2,1,0:T(8,128)(2,1)}, bf16[2,64,1152]{2,1,0:T(8,128)(2,1)}, u32[]{:S(2)}, u32[]{:S(2)}) collective-permute-start(bf16[2,64,1152]{2,1,0:T(8,128)(2,1)} %collective-permute-done.refs_6_), channel_id=1, source_target_pairs={{0,4},{1,5},{2,6},{3,7},{4,2},{5,3},{6,0},{7,1},{8,12},{9,13},{10,... | collective-permute-start | bytes 884744 | tf_op jit(solution)/shard_map/ppermute | solution.py:36
  32.7 2.0 %collective-permute-start.13 = (bf16[2,64,1152]{2,1,0:T(8,128)(2,1)}, bf16[2,64,1152]{2,1,0:T(8,128)(2,1)}, u32[]{:S(2)}, u32[]{:S(2)}) collective-permute-start(bf16[2,64,1152]{2,1,0:T(8,128)(2,1)} %collective-permute-done.12.refs_3_), channel_id=1, source_target_pairs={{0,1},{1,0},{2,3},{3,2},{4,5},{5,4},{6,7},{7,6},{8,9},{9,8},{10,11... | collective-permute-start | bytes 884744 | tf_op jit(solution)/shard_map/ppermute | solution.py:36
  32.8 2.3 %collective-permute-start.11 = (bf16[2,64,1152]{2,1,0:T(8,128)(2,1)}, bf16[2,64,1152]{2,1,0:T(8,128)(2,1)}, u32[]{:S(2)}, u32[]{:S(2)}) collective-permute-start(bf16[2,64,1152]{2,1,0:T(8,128)(2,1)} %collective-permute-done.1.refs_0_), channel_id=1, source_target_pairs={{0,1},{1,0},{2,3},{3,2},{4,5},{5,4},{6,7},{7,6},{8,9},{9,8},{10,11... | collective-permute-start | bytes 884744 | tf_op jit(solution)/shard_map/ppermute | solution.py:36
  42.5 1.2 %collective-permute-start.14 = (f32[4,8,128]{2,1,0:T(8,128)S(1)}, f32[4,8,128]{2,1,0:T(8,128)S(1)}, u32[]{:S(2)}, u32[]{:S(2)}) collective-permute-start(f32[4,8,128]{2,1,0:T(8,128)S(1)} %pad_maximum_fusion), channel_id=1, source_target_pairs={{0,1},{1,0},{2,3},{3,2},{4,5},{5,4},{6,7},{7,6},{8,9},{9,8},{10,11... | collective-permute-start | bytes 49160 | tf_op jit(solution)/shard_map/ppermute | solution.py:36
  43.7 5.3 %collective-permute-start.15 = (f32[4,8,128]{2,1,0:T(8,128)S(1)}, f32[4,8,128]{2,1,0:T(8,128)}, u32[]{:S(2)}, u32[]{:S(2)}) collective-permute-start(f32[4,8,128]{2,1,0:T(8,128)S(1)} %fusion.6.refs_2_), channel_id=1, source_target_pairs={{0,2},{1,3},{2,0},{3,1},{4,6},{5,7},{6,4},{7,5},{8,10},{9,11},{10,... | collective-permute-start | bytes 49160 | tf_op jit(solution)/shard_map/ppermute | solution.py:36
  45.0 4.1 %collective-permute-start.16 = (f32[4,8,128]{2,1,0:T(8,128)S(1)}, f32[4,8,128]{2,1,0:T(8,128)}, u32[]{:S(2)}, u32[]{:S(2)}) collective-permute-start(f32[4,8,128]{2,1,0:T(8,128)S(1)} %fusion.6.refs_2_), channel_id=1, source_target_pairs={{0,4},{1,5},{2,6},{3,7},{4,2},{5,3},{6,0},{7,1},{8,12},{9,13},{10,... | collective-permute-start | bytes 49160 | tf_op jit(solution)/shard_map/ppermute | solution.py:36
  45.7 5.1 %collective-permute-start.17 = (f32[4,8,128]{2,1,0:T(8,128)S(1)}, f32[4,8,128]{2,1,0:T(8,128)}, u32[]{:S(2)}, u32[]{:S(2)}) collective-permute-start(f32[4,8,128]{2,1,0:T(8,128)S(1)} %fusion.6.refs_2_), channel_id=1, source_target_pairs={{0,6},{1,7},{2,4},{3,5},{4,0},{5,1},{6,2},{7,3},{8,14},{9,15},{10,... | collective-permute-start | bytes 49160 | tf_op jit(solution)/shard_map/ppermute | solution.py:36
  52.7 16.8 %copy-start.7 = (f32[8,128]{1,0:T(8,128)S(1)}, f32[8,128]{1,0:T(8,128)}, u32[]{:S(2)}) copy-start(f32[8,128]{1,0:T(8,128)} %copy-done.6) | copy-start | bytes 12292
  57.5 12.0 %collective-permute-start.18 = (bf16[208,1152]{1,0:T(8,128)(2,1)}, bf16[208,1152]{1,0:T(8,128)(2,1)S(1)}, u32[]{:S(2)}, u32[]{:S(2)}) collective-permute-start(bf16[208,1152]{1,0:T(8,128)(2,1)} %get-tuple-element.42), channel_id=1, source_target_pairs={{0,32},{1,9},{2,34},{3,11},{4,36},{5,13},{6,38},{7,15},{8,40},{9,1... | collective-permute-start | bytes 1437704 | tf_op jit(solution)/shard_map/ppermute | solution.py:36
  59.5 14.3 %collective-permute-start.19 = (bf16[192,1152]{1,0:T(8,128)(2,1)}, bf16[192,1152]{1,0:T(8,128)(2,1)}, u32[]{:S(2)}, u32[]{:S(2)}) collective-permute-start(bf16[192,1152]{1,0:T(8,128)(2,1)} %get-tuple-element.46), channel_id=1, source_target_pairs={{0,224},{1,25},{2,226},{3,27},{4,228},{5,29},{6,230},{7,31},{8,232... | collective-permute-start | bytes 1327112 | tf_op jit(solution)/shard_map/ppermute | solution.py:36
  70.8 11.3 %collective-permute-start.20 = (bf16[112,1152]{1,0:T(8,128)(2,1)S(1)}, bf16[112,1152]{1,0:T(8,128)(2,1)S(1)}, u32[]{:S(2)}, u32[]{:S(2)}) collective-permute-start(bf16[112,1152]{1,0:T(8,128)(2,1)S(1)} %get-tuple-element.48), channel_id=1, source_target_pairs={{0,224},{1,25},{2,226},{3,27},{4,228},{5,29},{6,230},{7,31},{8,232... | collective-permute-start | bytes 774152 | tf_op jit(solution)/shard_map/ppermute | solution.py:36
  76.1 6.0 %collective-permute-start.21 = (bf16[96,1152]{1,0:T(8,128)(2,1)S(1)}, bf16[96,1152]{1,0:T(8,128)(2,1)S(1)}, u32[]{:S(2)}, u32[]{:S(2)}) collective-permute-start(bf16[96,1152]{1,0:T(8,128)(2,1)S(1)} %get-tuple-element.49), channel_id=1, source_target_pairs={{0,32},{1,9},{2,34},{3,11},{4,36},{5,13},{6,38},{7,15},{8,40},{9,1... | collective-permute-start | bytes 663560 | tf_op jit(solution)/shard_map/ppermute | solution.py:36
  83.1 19.5 %all-to-all-start = ((bf16[8,24,1280]{2,1,0:T(8,128)(2,1)}), bf16[8,24,1280]{2,1,0:T(8,128)(2,1)}, u32[]{:S(2)}, u32[]{:S(2)}) async-start(bf16[8,24,1280]{2,1,0:T(8,128)(2,1)} %bitcast.13), calls=%async_computation | async-start | bytes 983040 | tf_op jit(solution)/shard_map/all_to_all | solution.py:533
  (11 other events, 38.2 us)

commit v3 on v2

v3 whole, which is shorter than its diff:
```python
import jax
import jax.numpy as jnp
import numpy as np
from jax import lax
from jax.experimental import pallas as pl
from jax.experimental.pallas import tpu as pltpu
from jax.sharding import PartitionSpec as P

D = 1152
FF = 6144
SEQ = 256
AXES = ("dp", "mp")

curve_scale = 0.7978845608028654
cubic_term = 0.044715
target_share = 0.5

X, Y, Z, CORES = 4, 4, 8, 2


def coords(i):
    dp, mp = divmod(i, 4)
    z, rest = divmod(dp, 8)
    y, x_lo = divmod(rest, 2)
    x_hi, core = divmod(mp, 2)
    return (x_hi * 2 + x_lo, y, z, core)


def index_of(x, y, z, core):
    x, y, z = x % X, y % Y, z % Z
    return (z * 8 + y * 2 + x % 2) * 4 + (x // 2) * 2 + core


def permute(array, move):
    pairs = [(i, index_of(*move(*coords(i)))) for i in range(X * Y * Z * CORES)]
    return lax.ppermute(array, AXES, pairs)


def z_even(z, y):
    return (z ^ 1, y)


def z_odd(z, y):
    return ((((z - 1) % Z) ^ 1) + 1) % Z, y


def y_even(z, y):
    return (z, y ^ 1)


def y_odd(z, y):
    return (z, ((((y - 1) % Y) ^ 1) + 1) % Y)


STEPS = (
    ((z_even, z_odd), (z_odd, z_even)),
    ((y_even, y_odd), (y_odd, y_even)),
)


def group_of(core, z, y):
    if core == 0:
        return [(zb, yb) for zb in sorted((z, (z + 4) % Z)) for yb in range(Y)]
    return [(zb, y) for zb in range(Z)]


GROUPS = []
for _i in range(X * Y * Z * CORES):
    _x, _y, _z, _core = coords(_i)
    _group = [index_of(_x, yb, zb, _core) for zb, yb in group_of(_core, _z, _y)]
    if _group not in GROUPS:
        GROUPS.append(_group)


def row_table():
    table = np.zeros((CORES, Z, Y, 2, 2, 192), np.int32)
    for core in range(CORES):
        for chain in range(2):
            places = [(z, y) for z in range(Z) for y in range(Y)]
            orders = {place: group_of(core, *place) for place in places}
            for step in reversed(STEPS[core][chain]):
                orders = {place: orders[place] + orders[step(*place)] for place in places}
            for (z, y), order in orders.items():
                assert len(set(order)) == Z * Y
                rows = []
                for number, (zb, yb) in enumerate(order):
                    first = (16, 8)[number % 2]
                    cut = range(first) if chain == 0 else range(first, 24)
                    rows += [(zb * Y + yb) * 48 + row for row in cut]
                table[core, z, y, 0, chain] = rows[192:]
                table[core, z, y, 1, chain] = rows[:192]
    return table.reshape(CORES * Z * Y, 1, -1)


def exchange(array, number, chain):
    def move(x, y, z, core):
        z, y = STEPS[core][chain][number](z, y)
        return (x, y, z, core)

    return permute(array, move)


def gelu_parts(preact):
    square = preact * preact
    half = 0.5 * jnp.tanh(preact * (curve_scale + (curve_scale * cubic_term) * square)) + 0.5
    values = preact * half
    slopes = half + values * (1.0 - half) * (2.0 * curve_scale + (6.0 * curve_scale * cubic_term) * square)
    return (values, slopes)


def dot(left, right, contract):
    return lax.dot_general(left, right, ((contract[:1], contract[1:]), ((), ())), preferred_element_type=jnp.float32)


VMEM = pl.BlockSpec(memory_space=pltpu.VMEM)
HBM = pl.BlockSpec(memory_space=pl.ANY)
LANES = (8, 128)


def call(kernel, name, outs, args, specs=None, scratch=(), flops=0, limit=12):
    return pl.pallas_call(
        kernel,
        out_shape=outs,
        in_specs=specs or [VMEM] * len(args),
        out_specs=jax.tree.map(lambda _: VMEM, outs),
        scratch_shapes=scratch,
        compiler_params=pltpu.CompilerParams(vmem_limit_bytes=limit * 2**20),
        cost_estimate=pl.CostEstimate(flops=flops, bytes_accessed=0, transcendentals=0),
        name=name,
    )(*args)


def array(shape, kind):
    return jax.ShapeDtypeStruct(shape, kind)


def place():
    dp, mp = lax.axis_index("dp"), lax.axis_index("mp")
    return dp // 8, (dp // 2) % 4, dp % 2, mp % 2


def mask_kernel(lengths, cotangent, out):
    positions = lax.axis_index("mp") * out.shape[1] + lax.broadcasted_iota(jnp.int32, out.shape[1:], 0)
    for e in range(out.shape[0]):
        value = cotangent[e].astype(jnp.float32)
        out[e] = jnp.where(positions < lengths[:, e : e + 1], value, 0.0).astype(out.dtype)


def load_rows(table, rows, sem):
    z, y, x_lo, core = place()
    copy = pltpu.make_async_copy(table.at[(core * Z + z) * Y + y], rows, sem)
    copy.start()
    copy.wait()
    return rows[...] + x_lo * 24


def up_kernel(table, weight, out, rows, sem):
    chosen = load_rows(table, rows, sem)
    pick = lax.broadcasted_iota(jnp.int32, (weight.shape[1], out.shape[1]), 0) == chosen
    out[...] = dot(weight[...], pick.astype(jnp.bfloat16), (1, 0)).astype(out.dtype)


def down_kernel(table, weight, out, rows, sem):
    chosen = load_rows(table, rows, sem).astype(jnp.float32)
    chosen = jnp.broadcast_to(chosen, (8, chosen.shape[1])).T[:, :1].astype(jnp.int32)
    pick = lax.broadcasted_iota(jnp.int32, (out.shape[0], weight.shape[0]), 1) == chosen
    out[...] = dot(pick.astype(jnp.bfloat16), weight[...], (1, 0)).astype(out.dtype)


def select(kernel, name, table, weight, shape, units):
    scratch = [pltpu.VMEM(table.shape[1:], jnp.int32), pltpu.SemaphoreType.DMA]
    return call(kernel, name, array(shape, weight.dtype), (table, weight), [HBM, VMEM], scratch, limit=16)


def products_of(rows, masked, up, down):
    values, slopes = gelu_parts(dot(rows, up[...], (1, 0)))
    delta = dot(masked, down[...], (1, 1)) * slopes
    return values.astype(jnp.bfloat16), delta.astype(jnp.bfloat16)


def stacked(refs, e):
    return jnp.concatenate([ref[e] for ref in refs], axis=0)


def both_examples(refs):
    return jnp.concatenate([stacked(refs, e) for e in range(2)], axis=0)


def square_of(rows, masked, hidden, delta):
    first = dot(rows, rows, (1, 1)) * dot(delta, delta, (1, 1))
    second = dot(hidden, hidden, (1, 1)) * dot(masked, masked, (1, 1))
    return jnp.broadcast_to(jnp.sum(first + second), LANES)


def early_kernel(in_a, in_b, co_a, co_b, up, down, hidden, delta):
    hidden[...], delta[...] = products_of(both_examples((in_a, in_b)), both_examples((co_a, co_b)), up, down)


def early_pass(inputs, cotans, up, down):
    out = array((4 * inputs[0].shape[1], up.shape[1]), jnp.bfloat16)
    return call(early_kernel, "early_pass", (out, out), (*inputs, *cotans, up, down))


def theirs_kernel(*refs):
    inputs, cotans = refs[:4], refs[4:8]
    up, down, hidden_out, masked_out, squares_out = refs[8:]
    for e in range(2):
        rows, masked = stacked(inputs, e), stacked(cotans, e)
        hidden, delta = products_of(rows, masked, up, down)
        hidden_out[e] = hidden.T
        masked_out[e] = masked
        squares_out[e] = square_of(rows, masked, hidden, delta)


def pass_outs(units, tokens, width, squares):
    return (
        array((2, units, tokens), jnp.bfloat16),
        array((2, tokens, width), jnp.bfloat16),
        array((squares, *LANES), jnp.float32),
    )


def theirs_pass(inputs, cotans, up, down):
    width, units = up.shape
    tokens = 4 * inputs[0].shape[1]
    return call(theirs_kernel, "theirs_pass", pass_outs(units, tokens, width, 2), (*inputs, *cotans, up, down))


def ours_kernel(*refs):
    inputs, cotans = refs[:4], refs[4:8]
    up, down, hidden_early, delta_early, theirs = refs[8:13]
    hidden_out, masked_out, squares_out = refs[13:]
    hidden_late, delta_late = products_of(both_examples(inputs[2:]), both_examples(cotans[2:]), up, down)
    half = hidden_late.shape[0] // 2
    is_first = place()[2] == 0
    for e in range(2):
        at = slice(e * half, (e + 1) * half)
        rows, masked = stacked(inputs, e), stacked(cotans, e)
        hidden = jnp.concatenate([hidden_early[at, :], hidden_late[at, :]], axis=0)
        delta = jnp.concatenate([delta_early[at, :], delta_late[at, :]], axis=0)
        hidden_out[e] = hidden.T
        masked_out[e] = masked
        square = square_of(rows, masked, hidden, delta)
        squares_out[e] = jnp.where(is_first, square, theirs[e])
        squares_out[2 + e] = jnp.where(is_first, theirs[e], square)


def ours_pass(inputs, cotans, up, down, early, theirs):
    width, units = up.shape
    tokens = 4 * inputs[0].shape[1]
    outs = pass_outs(units, tokens, width, 4)
    return call(ours_kernel, "ours_pass", outs, (*inputs, *cotans, up, down, *early, theirs))


def add_kernel(left, right, out):
    out[...] = left[...] + right[...]


def factors_of(examples, ratio, chip, across, from_left, from_right):
    total = (chip[...] + across[...]) + (from_left[...] + from_right[...])
    norms = jnp.sqrt(total)
    clip = ratio[...] * np.sqrt(np.float32(SEQ * D * FF))
    factors = clip / jnp.maximum(norms, clip)
    is_first = place()[2] == 0
    scale = jnp.where(is_first, factors, jnp.concatenate([factors[2:], factors[:2]], axis=0)) * (1.0 / examples)
    soft = jnp.floor(jax.nn.sigmoid(4.0 * (clip - norms) / clip) * 131072.0 + 0.5) * (1.0 / 131072.0)
    return scale, (soft[0] + soft[1]) + (soft[2] + soft[3])


TAIL = 16


def tail_rows(count, rows, width):
    count = count[:1, :1]
    whole = jnp.floor(count)
    rest = count - whole
    second = jnp.floor(rest * 256.0) * (1.0 / 256.0)
    rest = rest - second
    third = jnp.floor(rest * 65536.0) * (1.0 / 65536.0)
    row = lax.broadcasted_iota(jnp.int32, (8, 128), 0)
    parts = jnp.where(row == 0, whole, jnp.where(row == 1, second, jnp.where(row == 2, third, rest - third)))
    parts = jnp.where(row < 4, parts, 0.0)
    if width > 128:
        parts = jnp.concatenate([parts, jnp.zeros((8, width - 128), jnp.float32)], axis=1)
    return parts, jnp.zeros((rows - 8, width), jnp.float32)


def count_in(tail):
    return jnp.broadcast_to(jnp.sum(tail[:8, :128], axis=0, keepdims=True), LANES)


def outer_rows(at, rows, scale, operands):
    hidden_a, hidden_b, masked_a, masked_b = operands
    total = None
    for e in range(4):
        hidden, masked = ((hidden_a, masked_a), (hidden_b, masked_b))[e // 2]
        piece = scale[e, :1, :1] * dot(hidden[e % 2, at : at + rows, :], masked[e % 2], (1, 0))
        total = piece if total is None else total + piece
    return total


def outer_send_kernel(examples, *refs):
    small, operands, (out0, out1, count_out, scale_out) = refs[:5], refs[5:9], refs[9:]
    rows, width = out1.shape
    scale, count = factors_of(examples, *small)
    count_out[...] = count
    scale_out[...] = scale
    total = outer_rows(0, rows, scale, operands)
    out0[...] = jnp.concatenate([total, *tail_rows(count, TAIL, width)], axis=0).astype(out0.dtype)
    out1[...] = outer_rows(rows, rows, scale, operands).astype(out1.dtype)


def outer_keep_kernel(scale, *refs):
    operands, outs = refs[:4], refs[4:]
    rows = outs[0].shape[0]
    for chain, out in enumerate(outs):
        out[...] = outer_rows((2 + chain) * rows, rows, scale[...], operands)


def outer_send(rows, examples, small, operands):
    width = operands[2].shape[2]
    outs = (
        array((rows + TAIL, width), jnp.bfloat16),
        array((rows, width), jnp.bfloat16),
        array(LANES, jnp.float32),
        array((4, *LANES), jnp.float32),
    )
    return call(lambda *refs: outer_send_kernel(examples, *refs), "outer_send", outs, (*small, *operands))


def outer_keep(rows, scale, operands):
    outs = (array((rows, operands[2].shape[2]), jnp.float32),) * 2
    return call(outer_keep_kernel, "outer_keep", outs, (scale, *operands))


def step_first_kernel(count, kept, got, count_out, keep, send):
    rows, width = kept.shape
    half = rows // 2
    message = got[...].astype(jnp.float32)
    total = kept[...] + message[:rows]
    keep[...] = total[:half]
    counted = count[...] + count_in(message[rows:])
    count_out[...] = counted
    send[...] = jnp.concatenate([total[half:], *tail_rows(counted, TAIL, width)], axis=0).astype(send.dtype)


def step_outs(kept, sent, width):
    return (array(LANES, jnp.float32), array((kept, width), jnp.float32), array((sent, width), jnp.bfloat16))


def step_first(count, kept, got):
    rows, width = kept.shape
    return call(step_first_kernel, "step_first", step_outs(rows // 2, rows // 2 + TAIL, width), (count, kept, got))


def step_second_kernel(kept, got, keep, send):
    half = kept.shape[0] // 2
    total = kept[...] + got[...].astype(jnp.float32)
    keep[...] = total[:half]
    send[...] = total[half:].astype(send.dtype)


def step_second(kept, got):
    rows, width = kept.shape
    outs = (array((rows // 2, width), jnp.float32), array((rows // 2, width), jnp.bfloat16))
    return call(step_second_kernel, "step_second", outs, (kept, got))


SIDE = 128


def step_join_kernel(count, kept0, kept1, got0, got1, send):
    rows, width = kept0.shape
    message = got0[...].astype(jnp.float32)
    total0 = kept0[...] + message[:rows]
    total1 = kept1[...] + got1[...].astype(jnp.float32)
    counted = count[...] + count_in(message[rows:])
    pieces = []
    for at in range(0, rows, 24):
        pieces += [total0[at : at + 16], total1[at : at + 8], total0[at + 16 : at + 24], total1[at + 8 : at + 24]]
    side = tail_rows(counted, 24, SIDE)
    side = jnp.concatenate(list(side) * (rows // 12), axis=0)
    send[...] = jnp.concatenate([jnp.concatenate(pieces, axis=0), side], axis=1).astype(send.dtype)


def step_join(count, kept0, kept1, got0, got1):
    rows, width = kept0.shape
    return call(step_join_kernel, "step_join", array((2 * rows, width + SIDE), jnp.bfloat16), (count, kept0, kept1, got0, got1))


def step_last_kernel(examples, ratio, noise, got, out, ratio_next):
    rows, width = out.shape
    message = got[...].astype(jnp.float32)
    chunks = [message[at : at + rows] for at in range(0, message.shape[0], rows)]
    while len(chunks) > 1:
        chunks = [a + b for a, b in zip(chunks[::2], chunks[1::2])]
    out[...] = chunks[0][:, :width]
    count = jnp.sum(chunks[0][:8, width:], axis=0, keepdims=True)
    share = (count[:, :1] + noise[...]) / examples
    ratio_next[...] = ratio[...] * jnp.exp(-(share - target_share))


def step_last(examples, ratio, noise, got, rows, width):
    outs = (array((rows, width), jnp.float32), array((1, 1), jnp.float32))
    args = (ratio.reshape(1, 1), noise.reshape(1, 1), got)
    return call(lambda *refs: step_last_kernel(examples, *refs), "step_last", outs, args)


def right(x, y, z, core):
    return (x + 1, y, z, core)


def left(x, y, z, core):
    return (x - 1, y, z, core)


def other_core(x, y, z, core):
    return (x, y, z, 1 - core)


def opposite(x, y, z, core):
    return (x + 2, y, z, core)


def swap_cores(*arrays):
    return [permute(array, other_core) for array in arrays]


def after(array, *others):
    return lax.optimization_barrier((array, *others))[0]


def per_device(inputs, cotangent, lengths, up_weight, down_weight, clip_ratio, count_noise):
    in_l = permute(inputs, right)
    masked = call(
        mask_kernel, "mask", array(cotangent.shape, cotangent.dtype), (lengths.reshape(1, -1), cotangent)
    )
    co_r = permute(masked, left)

    table = jnp.asarray(row_table())
    width, units = up_weight.shape
    up = select(up_kernel, "select_up", table, up_weight, (width, units // 2), units // 2)
    down = select(down_kernel, "select_down", table, down_weight, (units // 2, width), units // 2)

    in_s, co_s = swap_cores(inputs, masked)
    co_l = permute(masked, right)
    in_r = permute(inputs, left)
    early = early_pass((inputs, in_s), (masked, co_s), up, down)
    ratio = permute(after(clip_ratio.reshape(1, 1), *early), other_core)
    in_l, co_r = after(in_l, ratio), after(co_r, ratio)
    in_o = permute(in_l, right)
    co_o = permute(co_r, left)
    in_ls, in_rs, co_ls, co_rs = swap_cores(in_l, in_r, co_l, co_r)
    in_os, co_os = swap_cores(in_o, co_o)
    hidden_theirs, masked_theirs, squares_theirs = theirs_pass((in_l, in_ls, in_r, in_rs), (co_l, co_ls, co_r, co_rs), up, down)
    hidden_ours, masked_ours, squares = ours_pass(
        (inputs, in_s, in_o, in_os), (masked, co_s, co_o, co_os), up, down, early, squares_theirs
    )

    chip = call(add_kernel, "chip_squares", array(squares.shape, squares.dtype), (squares, permute(squares, other_core)))
    small = (ratio, chip, *(permute(chip, move) for move in (opposite, right, left)))
    examples_all = lax.axis_size("dp") * lengths.shape[0]
    operands = (hidden_ours, hidden_theirs, masked_ours, masked_theirs)
    quarter = units // 8
    send0, send1, count, scale = outer_send(quarter, examples_all, small, operands)
    got0, got1 = exchange(send0, 0, 0), exchange(send1, 0, 1)
    keep0, keep1 = outer_keep(quarter, scale, operands)
    count, keep0, send0 = step_first(count, keep0, got0)
    got0 = exchange(send0, 1, 0)
    keep1, send1 = step_second(keep1, got1)
    got1 = exchange(send1, 1, 1)
    send = step_join(count, keep0, keep1, got0, got1)
    got = lax.all_to_all(send, AXES, 0, 0, axis_index_groups=GROUPS, tiled=True)
    grad_down, ratio_next = step_last(
        examples_all, ratio, count_noise, got, 4 * quarter // (Z * Y), send.shape[1] - SIDE
    )
    return (grad_down, ratio_next.reshape(1))


def solution(mesh):
    return jax.shard_map(
        per_device,
        mesh=mesh,
        in_specs=(
            P("dp", "mp", None),
            P("dp", "mp", None),
            P("dp"),
            P(None, "mp"),
            P("mp", None),
            P(),
            P(),
        ),
        out_specs=(P(("mp", "dp"), None), P()),
        check_vma=False,
    )
```

time: 108 us -> 91.6 us (0.85)
  Pallas kernels: 30.1 us -> 19.9 us
  waiting for transfers between devices: 26.1 us -> 35.6 us
  matrix products: 8.51 us -> 0 us
  between operations: 3.96 us -> 1.48 us
  other arithmetic: 2.21 us -> 0 us
  local copies, waits for them, and re-layouts: 6.15 us -> 4.55 us
    ppermute x22 -> x23, waiting for transfers between devices: 13.1 us -> 23.7 us  [permute(): return lax.ppermute(array, AXES, pairs)]
    pallas_call x10 -> x13, Pallas kernels: 30.1 us -> 19.9 us  [call(): pl.pallas_call(kernel, out_shape=outs, in_specs=specs or [VMEM] * len(arg...]
    dot_general x2 -> x0, matrix products: 8.51 us -> none  [the longest x1 4.3 us: per_device(): jnp.einsum('fd,fp->dp', down_weight, pick, preferred_element_type=jnp.bfl...]
    all_to_all x1, waiting for transfers between devices: 13.1 us -> 11.9 us  [per_device(): got = lax.all_to_all(send, AXES, 0, 0, axis_index_groups=GROUPS, tiled=True)]
    unnamed x24 -> x12, local copies, waits for them, and re-layouts: 5.48 us -> 4.55 us
    ppermute x22 -> x23, starting transfers between devices: 23.8 us -> 22.9 us  [permute(): return lax.ppermute(array, AXES, pairs)]
  transfers between devices with their start and end apart: 23 -> 24, of which waited for: 8 -> 9; matrix products, arithmetic and copies ran while one was open for 9% -> 0% of each run, Pallas kernels for 14% -> 14%
where the time goes in v3:
time: 91.6 us; the launch traced here: 91.3 us
  waiting for transfers between devices  35.6 us (39%)
  starting transfers between devices  29.7 us (32%)
  Pallas kernels  19.9 us (22%)
  local copies, waits for them, and re-layouts  4.55 us (5%)
  between operations  1.48 us (2%)
    ppermute x23, waiting for transfers between devices, permute(): return lax.ppermute(array, AXES, pairs)  23.7 us
    ppermute x23, starting transfers between devices, permute(): return lax.ppermute(array, AXES, pairs)  22.9 us
    pallas_call x13, Pallas kernels, call(): pl.pallas_call(kernel, out_shape=outs, in_specs=specs or [VMEM] * len(arg...  19.9 us
    all_to_all x1, waiting for transfers between devices, per_device(): got = lax.all_to_all(send, AXES, 0, 0, axis_index_groups=GROUPS, tiled=True)  11.9 us
    all_to_all x1, starting transfers between devices, per_device(): got = lax.all_to_all(send, AXES, 0, 0, axis_index_groups=GROUPS, tiled=True)  6.8 us
    unnamed x12, local copies, waits for them, and re-layouts  4.55 us
  transfers between devices with their start and end apart: 24, of which 9 were waited for; matrix products, arithmetic and copies ran while one was open for 0% of the time, Pallas kernels for 14%

profile of v3, /device:TPU:6, one launch (start us, length us, event | category | flops | bytes accessed | tf_op | source)
XLA Modules:
  0.0 91.3 jit_solution(14024264448474032180)
XLA Ops:
  3.0 2.2 %collective-permute-start.12 = (bf16[2,64,1152]{2,1,0:T(8,128)(2,1)S(1)}, bf16[2,64,1152]{2,1,0:T(8,128)(2,1)S(1)}, u32[]{:S(2)}, u32[]{:S(2)}) collective-permute-start(bf16[2,64,1152]{2,1,0:T(8,128)(2,1)S(1)} %mask.1.co_a.refs_4_), channel_id=1, source_target_pairs={{0,4},{1,5},{2,6},{3,7},{4,2},{5,3},{6,0},{7,1},{8,12},{9,13},{10,... | collective-permute-start | bytes 884744 | tf_op jit(solution)/shard_map/ppermute | solution.py:36
  5.2 3.2 %collective-permute-start.3 = (bf16[2,64,1152]{2,1,0:T(8,128)(2,1)}, bf16[2,64,1152]{2,1,0:T(8,128)(2,1)S(1)}, u32[]{:S(2)}, u32[]{:S(2)}) collective-permute-start(bf16[2,64,1152]{2,1,0:T(8,128)(2,1)} %refs_0_.1), channel_id=1, source_target_pairs={{0,4},{1,5},{2,6},{3,7},{4,2},{5,3},{6,0},{7,1},{8,12},{9,13},{10,... | collective-permute-start | bytes 884744 | tf_op jit(solution)/shard_map/ppermute | solution.py:36
  8.4 2.0 %copy-done = bf16[1152,1536]{1,0:T(8,128)(2,1)S(1)} copy-done((bf16[1152,1536]{1,0:T(8,128)(2,1)S(1)}, bf16[1152,1536]{1,0:T(8,128)(2,1)}, u32[]{:S(2)}) %copy-start) | copy-done | bytes 3538968
  11.4 2.9 %select_up.1.up.refs_8_ = bf16[1152,768]{1,0:T(8,128)(2,1)S(1)} custom-call(s32[64,1,768]{2,1,0:T(1,128)S(1)} %copy-done.3, bf16[1152,1536]{1,0:T(8,128)(2,1)S(1)} %copy-done), custom_call_target="tpu_custom_call" | custom-call | tf_op jit(solution)/shard_map/select_up/pallas_call | solution.py:121
  14.3 3.5 %select_down.1.down.refs_9_ = bf16[768,1152]{1,0:T(8,128)(2,1)S(1)} custom-call(s32[64,1,768]{2,1,0:T(1,128)S(1)} %copy-done.3, bf16[1536,1152]{1,0:T(8,128)(2,1)S(1)} %copy-done.1), custom_call_target="tpu_custom_call" | custom-call | tf_op jit(solution)/shard_map/select_down/pallas_call | solution.py:121
  18.0 1.4 %early_pass.1 = (bf16[256,768]{1,0:T(8,128)(2,1)S(1)}, bf16[256,768]{1,0:T(8,128)(2,1)S(1)}) custom-call(bf16[2,64,1152]{2,1,0:T(8,128)(2,1)S(1)} %copy-done.2, bf16[2,64,1152]{2,1,0:T(8,128)(2,1)S(1)} %collective-permute-done.in_b.refs_1_, bf16[2,64,1152]{2,1,0:T(8,128)(2,1)S(1)} %mask.1.co_a.refs_4_, ...), custom_call_target="tpu_custom_call" | custom-call | tf_op jit(solution)/shard_map/early_pass/pallas_call | solution.py:121
  20.7 3.2 %collective-permute-start.4 = (bf16[2,64,1152]{2,1,0:T(8,128)(2,1)S(1)}, bf16[2,64,1152]{2,1,0:T(8,128)(2,1)S(1)}, u32[]{:S(2)}, u32[]{:S(2)}) collective-permute-start(bf16[2,64,1152]{2,1,0:T(8,128)(2,1)S(1)} %collective-permute-done.3.refs_0_), channel_id=1, source_target_pairs={{0,4},{1,5},{2,6},{3,7},{4,2},{5,3},{6,0},{7,1},{8,12},{9,13},{10,... | collective-permute-start | bytes 884744 | tf_op jit(solution)/shard_map/ppermute | solution.py:36
  23.9 5.2 %collective-permute-done.10.refs_2_ = bf16[2,64,1152]{2,1,0:T(8,128)(2,1)S(1)} collective-permute-done((bf16[2,64,1152]{2,1,0:T(8,128)(2,1)S(1)}, bf16[2,64,1152]{2,1,0:T(8,128)(2,1)S(1)}, u32[]{:S(2)}, u32[]{:S(2)}) %collective-permute-start.10) | collective-permute-done | bytes 294944 | tf_op jit(solution)/shard_map/ppermute | solution.py:36
  29.6 4.0 %collective-permute-done.7.refs_6_ = bf16[2,64,1152]{2,1,0:T(8,128)(2,1)S(1)} collective-permute-done((bf16[2,64,1152]{2,1,0:T(8,128)(2,1)S(1)}, bf16[2,64,1152]{2,1,0:T(8,128)(2,1)S(1)}, u32[]{:S(2)}, u32[]{:S(2)}) %collective-permute-start.7) | collective-permute-done | bytes 294944 | tf_op jit(solution)/shard_map/ppermute | solution.py:36
  34.2 3.6 %theirs_pass.1 = (bf16[2,768,256]{2,1,0:T(8,128)(2,1)S(1)}, bf16[2,256,1152]{2,1,0:T(8,128)(2,1)S(1)}, f32[2,8,128]{2,1,0:T(8,128)S(1)}) custom-call(bf16[2,64,1152]{2,1,0:T(8,128)(2,1)S(1)} %collective-permute-done.3.refs_0_, bf16[2,64,1152]{2,1,0:T(8,128)(2,1)S(1)} %collective-permute-done.9.refs_1_, ...), custom_call_target="tpu_custom_call" | custom-call | tf_op jit(solution)/shard_map/theirs_pass/pallas_call | solution.py:121
  37.8 2.5 %ours_pass.1 = (bf16[2,768,256]{2,1,0:T(8,128)(2,1)S(1)}, bf16[2,256,1152]{2,1,0:T(8,128)(2,1)S(1)}, f32[4,8,128]{2,1,0:T(8,128)S(1)}) custom-call(bf16[2,64,1152]{2,1,0:T(8,128)(2,1)S(1)} %copy-done.2, bf16[2,64,1152]{2,1,0:T(8,128)(2,1)S(1)} %collective-permute-done.in_b.refs_1_, bf16[2,64,1152]{2,1,0:T(8,128)(2,1)S(1)} %collective-permute-done.4.refs_2_, ...), custom_call_target="tpu_custom_call" | custom-call | tf_op jit(solution)/shard_map/ours_pass/pallas_call | solution.py:121
  40.4 1.2 %collective-permute-done.15.right = f32[4,8,128]{2,1,0:T(8,128)S(1)} collective-permute-done((f32[4,8,128]{2,1,0:T(8,128)S(1)}, f32[4,8,128]{2,1,0:T(8,128)S(1)}, u32[]{:S(2)}, u32[]{:S(2)}) %collective-permute-start.15) | collective-permute-done | bytes 16416 | tf_op jit(solution)/shard_map/ppermute | solution.py:36
  41.8 1.5 %collective-permute-start.17 = (f32[4,8,128]{2,1,0:T(8,128)S(1)}, f32[4,8,128]{2,1,0:T(8,128)S(1)}, u32[]{:S(2)}, u32[]{:S(2)}) collective-permute-start(f32[4,8,128]{2,1,0:T(8,128)S(1)} %chip_squares.1.refs_1_), channel_id=1, source_target_pairs={{0,4},{1,5},{2,6},{3,7},{4,2},{5,3},{6,0},{7,1},{8,12},{9,13},{10,... | collective-permute-start | bytes 49160 | tf_op jit(solution)/shard_map/ppermute | solution.py:36
  43.8 3.0 %collective-permute-done.16.refs_2_ = f32[4,8,128]{2,1,0:T(8,128)S(1)} collective-permute-done((f32[4,8,128]{2,1,0:T(8,128)S(1)}, f32[4,8,128]{2,1,0:T(8,128)S(1)}, u32[]{:S(2)}, u32[]{:S(2)}) %collective-permute-start.16) | collective-permute-done | bytes 16416 | tf_op jit(solution)/shard_map/ppermute | solution.py:36
  46.8 1.4 %collective-permute-done.18.refs_4_ = f32[4,8,128]{2,1,0:T(8,128)S(1)} collective-permute-done((f32[4,8,128]{2,1,0:T(8,128)S(1)}, f32[4,8,128]{2,1,0:T(8,128)S(1)}, u32[]{:S(2)}, u32[]{:S(2)}) %collective-permute-start.18) | collective-permute-done | bytes 16416 | tf_op jit(solution)/shard_map/ppermute | solution.py:36
  48.2 1.9 %outer_send.1 = (bf16[208,1152]{1,0:T(8,128)(2,1)S(1)}, bf16[192,1152]{1,0:T(8,128)(2,1)S(1)}, f32[8,128]{1,0:T(8,128)S(1)}, f32[4,8,128]{2,1,0:T(8,128)S(1)}) custom-call(f32[1,1]{1,0:T(1,128)} %collective-permute-done.2.refs_0_, f32[4,8,128]{2,1,0:T(8,128)S(1)} %chip_squares.1.refs_1_, f32[4,8,128]{2,1,0:T(8,128)S(1)} %collective-permute-done.16.refs_2_, ...), custom_call_target="tpu_custom_call" | custom-call | tf_op jit(solution)/shard_map/outer_send/pallas_call | solution.py:121
  50.5 4.9 %collective-permute-start.20 = (bf16[192,1152]{1,0:T(8,128)(2,1)S(1)}, bf16[192,1152]{1,0:T(8,128)(2,1)S(1)}, u32[]{:S(2)}, u32[]{:S(2)}) collective-permute-start(bf16[192,1152]{1,0:T(8,128)(2,1)S(1)} %get-tuple-element.44), channel_id=1, source_target_pairs={{0,224},{1,25},{2,226},{3,27},{4,228},{5,29},{6,230},{7,31},{8,232... | collective-permute-start | bytes 1327112 | tf_op jit(solution)/shard_map/ppermute | solution.py:36
  55.5 1.3 %outer_keep.1 = (f32[192,1152]{1,0:T(8,128)S(1)}, f32[192,1152]{1,0:T(8,128)S(1)}) custom-call(f32[4,8,128]{2,1,0:T(8,128)S(1)} %get-tuple-element.38.scale, bf16[2,768,256]{2,1,0:T(8,128)(2,1)S(1)} %get-tuple-element.33.refs_5_.refs_0_, bf16[2,768,256]{2,1,0:T(8,128)(2,1)S(1)} %get-tuple-element.34.refs_6_.refs_1_, ...), custom_call_target="tpu_custom_call" | custom-call | tf_op jit(solution)/shard_map/outer_keep/pallas_call | solution.py:121
  56.8 2.2 %collective-permute-done.19.got = bf16[208,1152]{1,0:T(8,128)(2,1)S(1)} collective-permute-done((bf16[208,1152]{1,0:T(8,128)(2,1)S(1)}, bf16[208,1152]{1,0:T(8,128)(2,1)S(1)}, u32[]{:S(2)}, u32[]{:S(2)}) %collective-permute-start.19) | collective-permute-done | bytes 479264 | tf_op jit(solution)/shard_map/ppermute | solution.py:36
  59.2 4.2 %collective-permute-start.21 = (bf16[112,1152]{1,0:T(8,128)(2,1)S(1)}, bf16[112,1152]{1,0:T(8,128)(2,1)S(1)}, u32[]{:S(2)}, u32[]{:S(2)}) collective-permute-start(bf16[112,1152]{1,0:T(8,128)(2,1)S(1)} %get-tuple-element.46), channel_id=1, source_target_pairs={{0,224},{1,25},{2,226},{3,27},{4,228},{5,29},{6,230},{7,31},{8,232... | collective-permute-start | bytes 774152 | tf_op jit(solution)/shard_map/ppermute | solution.py:36
  63.6 5.9 %collective-permute-done.22.got1 = bf16[96,1152]{1,0:T(8,128)(2,1)S(1)} collective-permute-done((bf16[96,1152]{1,0:T(8,128)(2,1)S(1)}, bf16[96,1152]{1,0:T(8,128)(2,1)S(1)}, u32[]{:S(2)}, u32[]{:S(2)}) %collective-permute-start.22) | collective-permute-done | bytes 221216 | tf_op jit(solution)/shard_map/ppermute | solution.py:36
  70.5 6.8 %all-to-all-start = ((bf16[8,24,1280]{2,1,0:T(8,128)(2,1)}), bf16[8,24,1280]{2,1,0:T(8,128)(2,1)S(1)}, u32[]{:S(2)}, u32[]{:S(2)}) async-start(bf16[8,24,1280]{2,1,0:T(8,128)(2,1)} %bitcast.3), calls=%async_computation | async-start | bytes 983040 | tf_op jit(solution)/shard_map/all_to_all | solution.py:473
  77.9 11.9 %all-to-all-done = bf16[8,24,1280]{2,1,0:T(8,128)(2,1)S(1)} async-done(((bf16[8,24,1280]{2,1,0:T(8,128)(2,1)}), bf16[8,24,1280]{2,1,0:T(8,128)(2,1)S(1)}, u32[]{:S(2)}, u32[]{:S(2)}) %all-to-all-start) | async-done | bytes 491552 | tf_op jit(solution)/shard_map/all_to_all | solution.py:473
  89.9 1.4 %step_last.1 = (f32[24,1152]{1,0:T(8,128)}, f32[1,1]{1,0:T(1,128)}) custom-call(f32[1,1]{1,0:T(1,128)} %collective-permute-done.2.refs_0_, f32[1,1]{1,0:T(1,128)} %bitcast.6.refs_1_, bf16[192,1280]{1,0:T(8,128)(2,1)S(1)} %bitcast.7), custom_call_target="tpu_custom_call" | custom-call | tf_op jit(solution)/shard_map/step_last/pallas_call | solution.py:121
  (49 shorter events, 8.2 us)
Async XLA Ops:
  2.4 15.5 %collective-permute-start.1 = (bf16[2,64,1152]{2,1,0:T(8,128)(2,1)S(1)}, bf16[2,64,1152]{2,1,0:T(8,128)(2,1)S(1)}, u32[]{:S(2)}, u32[]{:S(2)}) collective-permute-start(bf16[2,64,1152]{2,1,0:T(8,128)(2,1)S(1)} %mask.1.co_a.refs_4_), channel_id=1, source_target_pairs={{0,1},{1,0},{2,3},{3,2},{4,5},{5,4},{6,7},{7,6},{8,9},{9,8},{10,11... | collective-permute-start | bytes 884744 | tf_op jit(solution)/shard_map/ppermute | solution.py:36
  2.5 15.5 %collective-permute-start = (bf16[2,64,1152]{2,1,0:T(8,128)(2,1)}, bf16[2,64,1152]{2,1,0:T(8,128)(2,1)S(1)}, u32[]{:S(2)}, u32[]{:S(2)}) collective-permute-start(bf16[2,64,1152]{2,1,0:T(8,128)(2,1)} %refs_0_.1), channel_id=1, source_target_pairs={{0,1},{1,0},{2,3},{3,2},{4,5},{5,4},{6,7},{7,6},{8,9},{9,8},{10,11... | collective-permute-start | bytes 884744 | tf_op jit(solution)/shard_map/ppermute | solution.py:36
  3.0 16.5 %collective-permute-start.12 = (bf16[2,64,1152]{2,1,0:T(8,128)(2,1)S(1)}, bf16[2,64,1152]{2,1,0:T(8,128)(2,1)S(1)}, u32[]{:S(2)}, u32[]{:S(2)}) collective-permute-start(bf16[2,64,1152]{2,1,0:T(8,128)(2,1)S(1)} %mask.1.co_a.refs_4_), channel_id=1, source_target_pairs={{0,4},{1,5},{2,6},{3,7},{4,2},{5,3},{6,0},{7,1},{8,12},{9,13},{10,... | collective-permute-start | bytes 884744 | tf_op jit(solution)/shard_map/ppermute | solution.py:36
  5.2 14.8 %collective-permute-start.6 = (bf16[2,64,1152]{2,1,0:T(8,128)(2,1)S(1)}, bf16[2,64,1152]{2,1,0:T(8,128)(2,1)S(1)}, u32[]{:S(2)}, u32[]{:S(2)}) collective-permute-start(bf16[2,64,1152]{2,1,0:T(8,128)(2,1)S(1)} %mask.1.co_a.refs_4_), channel_id=1, source_target_pairs={{0,6},{1,7},{2,4},{3,5},{4,0},{5,1},{6,2},{7,3},{8,14},{9,15},{10,... | collective-permute-start | bytes 884744 | tf_op jit(solution)/shard_map/ppermute | solution.py:36
  5.2 15.5 %collective-permute-start.3 = (bf16[2,64,1152]{2,1,0:T(8,128)(2,1)}, bf16[2,64,1152]{2,1,0:T(8,128)(2,1)S(1)}, u32[]{:S(2)}, u32[]{:S(2)}) collective-permute-start(bf16[2,64,1152]{2,1,0:T(8,128)(2,1)} %refs_0_.1), channel_id=1, source_target_pairs={{0,4},{1,5},{2,6},{3,7},{4,2},{5,3},{6,0},{7,1},{8,12},{9,13},{10,... | collective-permute-start | bytes 884744 | tf_op jit(solution)/shard_map/ppermute | solution.py:36
  17.9 11.2 %collective-permute-start.10 = (bf16[2,64,1152]{2,1,0:T(8,128)(2,1)S(1)}, bf16[2,64,1152]{2,1,0:T(8,128)(2,1)S(1)}, u32[]{:S(2)}, u32[]{:S(2)}) collective-permute-start(bf16[2,64,1152]{2,1,0:T(8,128)(2,1)S(1)} %copy-done.2), channel_id=1, source_target_pairs={{0,6},{1,7},{2,4},{3,5},{4,0},{5,1},{6,2},{7,3},{8,14},{9,15},{10,... | collective-permute-start | bytes 884744 | tf_op jit(solution)/shard_map/ppermute | solution.py:36
  19.3 1.3 %collective-permute-start.2 = (f32[1,1]{1,0:T(1,128)}, f32[1,1]{1,0:T(1,128)}, u32[]{:S(2)}, u32[]{:S(2)}) collective-permute-start(f32[1,1]{1,0:T(1,128)} %bitcast), channel_id=1, source_target_pairs={{0,1},{1,0},{2,3},{3,2},{4,5},{5,4},{6,7},{7,6},{8,9},{9,8},{10,11... | collective-permute-start | bytes 20 | tf_op jit(solution)/shard_map/ppermute | solution.py:36
  19.5 10.2 %collective-permute-start.13 = (bf16[2,64,1152]{2,1,0:T(8,128)(2,1)S(1)}, bf16[2,64,1152]{2,1,0:T(8,128)(2,1)S(1)}, u32[]{:S(2)}, u32[]{:S(2)}) collective-permute-start(bf16[2,64,1152]{2,1,0:T(8,128)(2,1)S(1)} %collective-permute-done.12.refs_4_), channel_id=1, source_target_pairs={{0,1},{1,0},{2,3},{3,2},{4,5},{5,4},{6,7},{7,6},{8,9},{9,8},{10,11... | collective-permute-start | bytes 884744 | tf_op jit(solution)/shard_map/ppermute | solution.py:36
  20.7 13.0 %collective-permute-start.7 = (bf16[2,64,1152]{2,1,0:T(8,128)(2,1)S(1)}, bf16[2,64,1152]{2,1,0:T(8,128)(2,1)S(1)}, u32[]{:S(2)}, u32[]{:S(2)}) collective-permute-start(bf16[2,64,1152]{2,1,0:T(8,128)(2,1)S(1)} %collective-permute-done.6.refs_6_), channel_id=1, source_target_pairs={{0,6},{1,7},{2,4},{3,5},{4,0},{5,1},{6,2},{7,3},{8,14},{9,15},{10,... | collective-permute-start | bytes 884744 | tf_op jit(solution)/shard_map/ppermute | solution.py:36
  20.7 13.0 %collective-permute-start.4 = (bf16[2,64,1152]{2,1,0:T(8,128)(2,1)S(1)}, bf16[2,64,1152]{2,1,0:T(8,128)(2,1)S(1)}, u32[]{:S(2)}, u32[]{:S(2)}) collective-permute-start(bf16[2,64,1152]{2,1,0:T(8,128)(2,1)S(1)} %collective-permute-done.3.refs_0_), channel_id=1, source_target_pairs={{0,4},{1,5},{2,6},{3,7},{4,2},{5,3},{6,0},{7,1},{8,12},{9,13},{10,... | collective-permute-start | bytes 884744 | tf_op jit(solution)/shard_map/ppermute | solution.py:36
  29.1 5.1 %collective-permute-start.11 = (bf16[2,64,1152]{2,1,0:T(8,128)(2,1)S(1)}, bf16[2,64,1152]{2,1,0:T(8,128)(2,1)S(1)}, u32[]{:S(2)}, u32[]{:S(2)}) collective-permute-start(bf16[2,64,1152]{2,1,0:T(8,128)(2,1)S(1)} %collective-permute-done.10.refs_2_), channel_id=1, source_target_pairs={{0,1},{1,0},{2,3},{3,2},{4,5},{5,4},{6,7},{7,6},{8,9},{9,8},{10,11... | collective-permute-start | bytes 884744 | tf_op jit(solution)/shard_map/ppermute | solution.py:36
  29.1 5.1 %collective-permute-start.14 = (bf16[2,64,1152]{2,1,0:T(8,128)(2,1)S(1)}, bf16[2,64,1152]{2,1,0:T(8,128)(2,1)S(1)}, u32[]{:S(2)}, u32[]{:S(2)}) collective-permute-start(bf16[2,64,1152]{2,1,0:T(8,128)(2,1)S(1)} %collective-permute-done.6.refs_6_), channel_id=1, source_target_pairs={{0,1},{1,0},{2,3},{3,2},{4,5},{5,4},{6,7},{7,6},{8,9},{9,8},{10,11... | collective-permute-start | bytes 884744 | tf_op jit(solution)/shard_map/ppermute | solution.py:36
  29.6 4.6 %collective-permute-start.9 = (bf16[2,64,1152]{2,1,0:T(8,128)(2,1)S(1)}, bf16[2,64,1152]{2,1,0:T(8,128)(2,1)S(1)}, u32[]{:S(2)}, u32[]{:S(2)}) collective-permute-start(bf16[2,64,1152]{2,1,0:T(8,128)(2,1)S(1)} %collective-permute-done.3.refs_0_), channel_id=1, source_target_pairs={{0,1},{1,0},{2,3},{3,2},{4,5},{5,4},{6,7},{7,6},{8,9},{9,8},{10,11... | collective-permute-start | bytes 884744 | tf_op jit(solution)/shard_map/ppermute | solution.py:36
  33.6 4.1 %collective-permute-start.8 = (bf16[2,64,1152]{2,1,0:T(8,128)(2,1)S(1)}, bf16[2,64,1152]{2,1,0:T(8,128)(2,1)S(1)}, u32[]{:S(2)}, u32[]{:S(2)}) collective-permute-start(bf16[2,64,1152]{2,1,0:T(8,128)(2,1)S(1)} %collective-permute-done.7.refs_6_), channel_id=1, source_target_pairs={{0,1},{1,0},{2,3},{3,2},{4,5},{5,4},{6,7},{7,6},{8,9},{9,8},{10,11... | collective-permute-start | bytes 884744 | tf_op jit(solution)/shard_map/ppermute | solution.py:36
  33.6 4.2 %collective-permute-start.5 = (bf16[2,64,1152]{2,1,0:T(8,128)(2,1)S(1)}, bf16[2,64,1152]{2,1,0:T(8,128)(2,1)S(1)}, u32[]{:S(2)}, u32[]{:S(2)}) collective-permute-start(bf16[2,64,1152]{2,1,0:T(8,128)(2,1)S(1)} %collective-permute-done.4.refs_2_), channel_id=1, source_target_pairs={{0,1},{1,0},{2,3},{3,2},{4,5},{5,4},{6,7},{7,6},{8,9},{9,8},{10,11... | collective-permute-start | bytes 884744 | tf_op jit(solution)/shard_map/ppermute | solution.py:36
  40.3 1.3 %collective-permute-start.15 = (f32[4,8,128]{2,1,0:T(8,128)S(1)}, f32[4,8,128]{2,1,0:T(8,128)S(1)}, u32[]{:S(2)}, u32[]{:S(2)}) collective-permute-start(f32[4,8,128]{2,1,0:T(8,128)S(1)} %get-tuple-element.32.left), channel_id=1, source_target_pairs={{0,1},{1,0},{2,3},{3,2},{4,5},{5,4},{6,7},{7,6},{8,9},{9,8},{10,11... | collective-permute-start | bytes 49160 | tf_op jit(solution)/shard_map/ppermute | solution.py:36
  41.5 5.2 %collective-permute-start.16 = (f32[4,8,128]{2,1,0:T(8,128)S(1)}, f32[4,8,128]{2,1,0:T(8,128)S(1)}, u32[]{:S(2)}, u32[]{:S(2)}) collective-permute-start(f32[4,8,128]{2,1,0:T(8,128)S(1)} %chip_squares.1.refs_1_), channel_id=1, source_target_pairs={{0,2},{1,3},{2,0},{3,1},{4,6},{5,7},{6,4},{7,5},{8,10},{9,11},{10,... | collective-permute-start | bytes 49160 | tf_op jit(solution)/shard_map/ppermute | solution.py:36
  41.8 5.0 %collective-permute-start.17 = (f32[4,8,128]{2,1,0:T(8,128)S(1)}, f32[4,8,128]{2,1,0:T(8,128)S(1)}, u32[]{:S(2)}, u32[]{:S(2)}) collective-permute-start(f32[4,8,128]{2,1,0:T(8,128)S(1)} %chip_squares.1.refs_1_), channel_id=1, source_target_pairs={{0,4},{1,5},{2,6},{3,7},{4,2},{5,3},{6,0},{7,1},{8,12},{9,13},{10,... | collective-permute-start | bytes 49160 | tf_op jit(solution)/shard_map/ppermute | solution.py:36
  43.3 5.0 %collective-permute-start.18 = (f32[4,8,128]{2,1,0:T(8,128)S(1)}, f32[4,8,128]{2,1,0:T(8,128)S(1)}, u32[]{:S(2)}, u32[]{:S(2)}) collective-permute-start(f32[4,8,128]{2,1,0:T(8,128)S(1)} %chip_squares.1.refs_1_), channel_id=1, source_target_pairs={{0,6},{1,7},{2,4},{3,5},{4,0},{5,1},{6,2},{7,3},{8,14},{9,15},{10,... | collective-permute-start | bytes 49160 | tf_op jit(solution)/shard_map/ppermute | solution.py:36
  50.2 8.8 %collective-permute-start.19 = (bf16[208,1152]{1,0:T(8,128)(2,1)S(1)}, bf16[208,1152]{1,0:T(8,128)(2,1)S(1)}, u32[]{:S(2)}, u32[]{:S(2)}) collective-permute-start(bf16[208,1152]{1,0:T(8,128)(2,1)S(1)} %get-tuple-element.40), channel_id=1, source_target_pairs={{0,32},{1,9},{2,34},{3,11},{4,36},{5,13},{6,38},{7,15},{8,40},{9,1... | collective-permute-start | bytes 1437704 | tf_op jit(solution)/shard_map/ppermute | solution.py:36
  50.5 12.9 %collective-permute-start.20 = (bf16[192,1152]{1,0:T(8,128)(2,1)S(1)}, bf16[192,1152]{1,0:T(8,128)(2,1)S(1)}, u32[]{:S(2)}, u32[]{:S(2)}) collective-permute-start(bf16[192,1152]{1,0:T(8,128)(2,1)S(1)} %get-tuple-element.44), channel_id=1, source_target_pairs={{0,224},{1,25},{2,226},{3,27},{4,228},{5,29},{6,230},{7,31},{8,232... | collective-permute-start | bytes 1327112 | tf_op jit(solution)/shard_map/ppermute | solution.py:36
  59.2 10.4 %collective-permute-start.21 = (bf16[112,1152]{1,0:T(8,128)(2,1)S(1)}, bf16[112,1152]{1,0:T(8,128)(2,1)S(1)}, u32[]{:S(2)}, u32[]{:S(2)}) collective-permute-start(bf16[112,1152]{1,0:T(8,128)(2,1)S(1)} %get-tuple-element.46), channel_id=1, source_target_pairs={{0,224},{1,25},{2,226},{3,27},{4,228},{5,29},{6,230},{7,31},{8,232... | collective-permute-start | bytes 774152 | tf_op jit(solution)/shard_map/ppermute | solution.py:36
  63.5 6.0 %collective-permute-start.22 = (bf16[96,1152]{1,0:T(8,128)(2,1)S(1)}, bf16[96,1152]{1,0:T(8,128)(2,1)S(1)}, u32[]{:S(2)}, u32[]{:S(2)}) collective-permute-start(bf16[96,1152]{1,0:T(8,128)(2,1)S(1)} %get-tuple-element.47), channel_id=1, source_target_pairs={{0,32},{1,9},{2,34},{3,11},{4,36},{5,13},{6,38},{7,15},{8,40},{9,1... | collective-permute-start | bytes 663560 | tf_op jit(solution)/shard_map/ppermute | solution.py:36
  70.5 19.4 %all-to-all-start = ((bf16[8,24,1280]{2,1,0:T(8,128)(2,1)}), bf16[8,24,1280]{2,1,0:T(8,128)(2,1)S(1)}, u32[]{:S(2)}, u32[]{:S(2)}) async-start(bf16[8,24,1280]{2,1,0:T(8,128)(2,1)} %bitcast.3), calls=%async_computation | async-start | bytes 983040 | tf_op jit(solution)/shard_map/all_to_all | solution.py:473
  (6 other events, 11.0 us)

commit v4 on v3

--- a/solution.py
+++ b/solution.py
@@ -446,13 +446,15 @@
     co_l = permute(masked, right)
     in_r = permute(inputs, left)
     early = early_pass((inputs, in_s), (masked, co_s), up, down)
-    ratio = permute(after(clip_ratio.reshape(1, 1), *early), other_core)
-    in_l, co_r = after(in_l, ratio), after(co_r, ratio)
+    ratio = permute(after(clip_ratio.reshape(1, 1), up, down), other_core)
+    in_l, in_r, co_l, co_r = (after(part, ratio) for part in (in_l, in_r, co_l, co_r))
     in_o = permute(in_l, right)
     co_o = permute(co_r, left)
     in_ls, in_rs, co_ls, co_rs = swap_cores(in_l, in_r, co_l, co_r)
-    in_os, co_os = swap_cores(in_o, co_o)
-    hidden_theirs, masked_theirs, squares_theirs = theirs_pass((in_l, in_ls, in_r, in_rs), (co_l, co_ls, co_r, co_rs), up, down)
+    hidden_theirs, masked_theirs, squares_theirs = theirs_pass(
+        (in_l, in_ls, in_r, in_rs), (co_l, co_ls, co_r, co_rs), *after((up, down), *early)
+    )
+    in_os, co_os = swap_cores(after(in_o, squares_theirs), after(co_o, squares_theirs))
     hidden_ours, masked_ours, squares = ours_pass(
         (inputs, in_s, in_o, in_os), (masked, co_s, co_o, co_os), up, down, early, squares_theirs
     )

time: 91.6 us -> 89.3 us (0.975)
  waiting for transfers between devices: 35.6 us -> 29.1 us
  starting transfers between devices: 29.7 us -> 34 us
    ppermute x23, waiting for transfers between devices: 23.7 us -> 17.1 us  [permute(): return lax.ppermute(array, AXES, pairs)]
    ppermute x23, starting transfers between devices: 22.9 us -> 27.2 us  [permute(): return lax.ppermute(array, AXES, pairs)]
  transfers between devices with their start and end apart: 24 -> 24, of which waited for: 9 -> 14; matrix products, arithmetic and copies ran while one was open for 0% -> 0% of each run, Pallas kernels for 14% -> 15%
where the time goes in v4:
time: 89.3 us; the launch traced here: 89 us
  starting transfers between devices  34 us (38%)
  waiting for transfers between devices  29.1 us (33%)
  Pallas kernels  19.9 us (22%)
  local copies, waits for them, and re-layouts  4.55 us (5%)
  between operations  1.44 us (2%)
    ppermute x23, starting transfers between devices, permute(): return lax.ppermute(array, AXES, pairs)  27.2 us
    pallas_call x13, Pallas kernels, call(): pl.pallas_call(kernel, out_shape=outs, in_specs=specs or [VMEM] * len(arg...  19.9 us
    ppermute x23, waiting for transfers between devices, permute(): return lax.ppermute(array, AXES, pairs)  17.1 us
    all_to_all x1, waiting for transfers between devices, per_device(): got = lax.all_to_all(send, AXES, 0, 0, axis_index_groups=GROUPS, tiled=True)  12.1 us
    all_to_all x1, starting transfers between devices, per_device(): got = lax.all_to_all(send, AXES, 0, 0, axis_index_groups=GROUPS, tiled=True)  6.79 us
    unnamed x12, local copies, waits for them, and re-layouts  4.55 us
  transfers between devices with their start and end apart: 24, of which 14 were waited for; matrix products, arithmetic and copies ran while one was open for 0% of the time, Pallas kernels for 15%

profile of v4, /device:TPU:6, one launch (start us, length us, event | category | flops | bytes accessed | tf_op | source)
XLA Modules:
  0.0 89.0 jit_solution(10934067527645162543)
XLA Ops:
  3.3 2.4 %collective-permute-start.7 = (bf16[2,64,1152]{2,1,0:T(8,128)(2,1)S(1)}, bf16[2,64,1152]{2,1,0:T(8,128)(2,1)S(1)}, u32[]{:S(2)}, u32[]{:S(2)}) collective-permute-start(bf16[2,64,1152]{2,1,0:T(8,128)(2,1)S(1)} %mask.1.co_a.refs_4_), channel_id=1, source_target_pairs={{0,4},{1,5},{2,6},{3,7},{4,2},{5,3},{6,0},{7,1},{8,12},{9,13},{10,... | collective-permute-start | bytes 884744 | tf_op jit(solution)/shard_map/ppermute | solution.py:36
  7.7 2.0 %copy-done = bf16[1152,1536]{1,0:T(8,128)(2,1)S(1)} copy-done((bf16[1152,1536]{1,0:T(8,128)(2,1)S(1)}, bf16[1152,1536]{1,0:T(8,128)(2,1)}, u32[]{:S(2)}) %copy-start) | copy-done | bytes 3538968
  10.7 2.9 %select_up.1.up.refs_8_ = bf16[1152,768]{1,0:T(8,128)(2,1)S(1)} custom-call(s32[64,1,768]{2,1,0:T(1,128)S(1)} %copy-done.3, bf16[1152,1536]{1,0:T(8,128)(2,1)S(1)} %copy-done), custom_call_target="tpu_custom_call" | custom-call | tf_op jit(solution)/shard_map/select_up/pallas_call | solution.py:121
  13.6 3.5 %select_down.1.down.refs_9_ = bf16[768,1152]{1,0:T(8,128)(2,1)S(1)} custom-call(s32[64,1,768]{2,1,0:T(1,128)S(1)} %copy-done.3, bf16[1536,1152]{1,0:T(8,128)(2,1)S(1)} %copy-done.1), custom_call_target="tpu_custom_call" | custom-call | tf_op jit(solution)/shard_map/select_down/pallas_call | solution.py:121
  17.2 1.2 %collective-permute-done.refs_0_ = f32[1,1]{1,0:T(1,128)} collective-permute-done((f32[1,1]{1,0:T(1,128)}, f32[1,1]{1,0:T(1,128)}, u32[]{:S(2)}, u32[]{:S(2)}) %collective-permute-start) | collective-permute-done | bytes 36 | tf_op jit(solution)/shard_map/ppermute | solution.py:36
  20.9 2.8 %collective-permute-start.3 = (bf16[2,64,1152]{2,1,0:T(8,128)(2,1)S(1)}, bf16[2,64,1152]{2,1,0:T(8,128)(2,1)S(1)}, u32[]{:S(2)}, u32[]{:S(2)}) collective-permute-start(bf16[2,64,1152]{2,1,0:T(8,128)(2,1)S(1)} %collective-permute-done.2.refs_0_), channel_id=1, source_target_pairs={{0,4},{1,5},{2,6},{3,7},{4,2},{5,3},{6,0},{7,1},{8,12},{9,13},{10,... | collective-permute-start | bytes 884744 | tf_op jit(solution)/shard_map/ppermute | solution.py:36
  23.7 1.4 %early_pass.1 = (bf16[256,768]{1,0:T(8,128)(2,1)S(1)}, bf16[256,768]{1,0:T(8,128)(2,1)S(1)}) custom-call(bf16[2,64,1152]{2,1,0:T(8,128)(2,1)S(1)} %copy-done.2, bf16[2,64,1152]{2,1,0:T(8,128)(2,1)S(1)} %collective-permute-done.1.in_b.refs_1_, bf16[2,64,1152]{2,1,0:T(8,128)(2,1)S(1)} %mask.1.co_a.refs_4_, ...), custom_call_target="tpu_custom_call" | custom-call | tf_op jit(solution)/shard_map/early_pass/pallas_call | solution.py:121
  25.1 3.6 %theirs_pass.1 = (bf16[2,768,256]{2,1,0:T(8,128)(2,1)S(1)}, bf16[2,256,1152]{2,1,0:T(8,128)(2,1)S(1)}, f32[2,8,128]{2,1,0:T(8,128)S(1)}) custom-call(bf16[2,64,1152]{2,1,0:T(8,128)(2,1)S(1)} %collective-permute-done.2.refs_0_, bf16[2,64,1152]{2,1,0:T(8,128)(2,1)S(1)} %collective-permute-done.4.refs_1_, ...), custom_call_target="tpu_custom_call" | custom-call | tf_op jit(solution)/shard_map/theirs_pass/pallas_call | solution.py:121
  28.7 2.1 %collective-permute-done.13.refs_6_ = bf16[2,64,1152]{2,1,0:T(8,128)(2,1)S(1)} collective-permute-done((bf16[2,64,1152]{2,1,0:T(8,128)(2,1)S(1)}, bf16[2,64,1152]{2,1,0:T(8,128)(2,1)S(1)}, u32[]{:S(2)}, u32[]{:S(2)}) %collective-permute-start.13) | collective-permute-done | bytes 294944 | tf_op jit(solution)/shard_map/ppermute | solution.py:36
  31.3 1.1 %collective-permute-done.14.refs_7_ = bf16[2,64,1152]{2,1,0:T(8,128)(2,1)S(1)} collective-permute-done((bf16[2,64,1152]{2,1,0:T(8,128)(2,1)S(1)}, bf16[2,64,1152]{2,1,0:T(8,128)(2,1)S(1)}, u32[]{:S(2)}, u32[]{:S(2)}) %collective-permute-start.14) | collective-permute-done | bytes 294944 | tf_op jit(solution)/shard_map/ppermute | solution.py:36
  32.8 2.5 %ours_pass.1 = (bf16[2,768,256]{2,1,0:T(8,128)(2,1)S(1)}, bf16[2,256,1152]{2,1,0:T(8,128)(2,1)S(1)}, f32[4,8,128]{2,1,0:T(8,128)S(1)}) custom-call(bf16[2,64,1152]{2,1,0:T(8,128)(2,1)S(1)} %copy-done.2, bf16[2,64,1152]{2,1,0:T(8,128)(2,1)S(1)} %collective-permute-done.1.in_b.refs_1_, bf16[2,64,1152]{2,1,0:T(8,128)(2,1)S(1)} %collective-permute-done.3.refs_2_, ...), custom_call_target="tpu_custom_call" | custom-call | tf_op jit(solution)/shard_map/ours_pass/pallas_call | solution.py:121
  36.6 1.8 %collective-permute-start.16 = (f32[4,8,128]{2,1,0:T(8,128)S(1)}, f32[4,8,128]{2,1,0:T(8,128)S(1)}, u32[]{:S(2)}, u32[]{:S(2)}) collective-permute-start(f32[4,8,128]{2,1,0:T(8,128)S(1)} %chip_squares.1.refs_1_), channel_id=1, source_target_pairs={{0,2},{1,3},{2,0},{3,1},{4,6},{5,7},{6,4},{7,5},{8,10},{9,11},{10,... | collective-permute-start | bytes 49160 | tf_op jit(solution)/shard_map/ppermute | solution.py:36
  39.2 1.1 %collective-permute-start.18 = (f32[4,8,128]{2,1,0:T(8,128)S(1)}, f32[4,8,128]{2,1,0:T(8,128)S(1)}, u32[]{:S(2)}, u32[]{:S(2)}) collective-permute-start(f32[4,8,128]{2,1,0:T(8,128)S(1)} %chip_squares.1.refs_1_), channel_id=1, source_target_pairs={{0,6},{1,7},{2,4},{3,5},{4,0},{5,1},{6,2},{7,3},{8,14},{9,15},{10,... | collective-permute-start | bytes 49160 | tf_op jit(solution)/shard_map/ppermute | solution.py:36
  40.4 1.4 %collective-permute-done.16.refs_2_ = f32[4,8,128]{2,1,0:T(8,128)S(1)} collective-permute-done((f32[4,8,128]{2,1,0:T(8,128)S(1)}, f32[4,8,128]{2,1,0:T(8,128)S(1)}, u32[]{:S(2)}, u32[]{:S(2)}) %collective-permute-start.16) | collective-permute-done | bytes 16416 | tf_op jit(solution)/shard_map/ppermute | solution.py:36
  42.1 2.1 %collective-permute-done.18.refs_4_ = f32[4,8,128]{2,1,0:T(8,128)S(1)} collective-permute-done((f32[4,8,128]{2,1,0:T(8,128)S(1)}, f32[4,8,128]{2,1,0:T(8,128)S(1)}, u32[]{:S(2)}, u32[]{:S(2)}) %collective-permute-start.18) | collective-permute-done | bytes 16416 | tf_op jit(solution)/shard_map/ppermute | solution.py:36
  44.2 1.9 %outer_send.1 = (bf16[208,1152]{1,0:T(8,128)(2,1)S(1)}, bf16[192,1152]{1,0:T(8,128)(2,1)S(1)}, f32[8,128]{1,0:T(8,128)S(1)}, f32[4,8,128]{2,1,0:T(8,128)S(1)}) custom-call(f32[1,1]{1,0:T(1,128)} %collective-permute-done.refs_0_, f32[4,8,128]{2,1,0:T(8,128)S(1)} %chip_squares.1.refs_1_, f32[4,8,128]{2,1,0:T(8,128)S(1)} %collective-permute-done.16.refs_2_, ...), custom_call_target="tpu_custom_call" | custom-call | tf_op jit(solution)/shard_map/outer_send/pallas_call | solution.py:121
  46.1 2.0 %collective-permute-start.19 = (bf16[208,1152]{1,0:T(8,128)(2,1)S(1)}, bf16[208,1152]{1,0:T(8,128)(2,1)S(1)}, u32[]{:S(2)}, u32[]{:S(2)}) collective-permute-start(bf16[208,1152]{1,0:T(8,128)(2,1)S(1)} %get-tuple-element.52), channel_id=1, source_target_pairs={{0,32},{1,9},{2,34},{3,11},{4,36},{5,13},{6,38},{7,15},{8,40},{9,1... | collective-permute-start | bytes 1437704 | tf_op jit(solution)/shard_map/ppermute | solution.py:36
  48.1 4.9 %collective-permute-start.20 = (bf16[192,1152]{1,0:T(8,128)(2,1)S(1)}, bf16[192,1152]{1,0:T(8,128)(2,1)S(1)}, u32[]{:S(2)}, u32[]{:S(2)}) collective-permute-start(bf16[192,1152]{1,0:T(8,128)(2,1)S(1)} %get-tuple-element.56), channel_id=1, source_target_pairs={{0,224},{1,25},{2,226},{3,27},{4,228},{5,29},{6,230},{7,31},{8,232... | collective-permute-start | bytes 1327112 | tf_op jit(solution)/shard_map/ppermute | solution.py:36
  53.1 1.3 %outer_keep.1 = (f32[192,1152]{1,0:T(8,128)S(1)}, f32[192,1152]{1,0:T(8,128)S(1)}) custom-call(f32[4,8,128]{2,1,0:T(8,128)S(1)} %get-tuple-element.50.scale, bf16[2,768,256]{2,1,0:T(8,128)(2,1)S(1)} %get-tuple-element.45.refs_5_.refs_0_, bf16[2,768,256]{2,1,0:T(8,128)(2,1)S(1)} %get-tuple-element.46.refs_6_.refs_1_, ...), custom_call_target="tpu_custom_call" | custom-call | tf_op jit(solution)/shard_map/outer_keep/pallas_call | solution.py:121
  55.1 5.9 %collective-permute-start.21 = (bf16[112,1152]{1,0:T(8,128)(2,1)S(1)}, bf16[112,1152]{1,0:T(8,128)(2,1)S(1)}, u32[]{:S(2)}, u32[]{:S(2)}) collective-permute-start(bf16[112,1152]{1,0:T(8,128)(2,1)S(1)} %get-tuple-element.58), channel_id=1, source_target_pairs={{0,224},{1,25},{2,226},{3,27},{4,228},{5,29},{6,230},{7,31},{8,232... | collective-permute-start | bytes 774152 | tf_op jit(solution)/shard_map/ppermute | solution.py:36
  61.2 5.9 %collective-permute-done.22.got1 = bf16[96,1152]{1,0:T(8,128)(2,1)S(1)} collective-permute-done((bf16[96,1152]{1,0:T(8,128)(2,1)S(1)}, bf16[96,1152]{1,0:T(8,128)(2,1)S(1)}, u32[]{:S(2)}, u32[]{:S(2)}) %collective-permute-start.22) | collective-permute-done | bytes 221216 | tf_op jit(solution)/shard_map/ppermute | solution.py:36
  68.1 6.8 %all-to-all-start = ((bf16[8,24,1280]{2,1,0:T(8,128)(2,1)}), bf16[8,24,1280]{2,1,0:T(8,128)(2,1)S(1)}, u32[]{:S(2)}, u32[]{:S(2)}) async-start(bf16[8,24,1280]{2,1,0:T(8,128)(2,1)} %bitcast.3), calls=%async_computation | async-start | bytes 983040 | tf_op jit(solution)/shard_map/all_to_all | solution.py:475
  75.5 12.1 %all-to-all-done = bf16[8,24,1280]{2,1,0:T(8,128)(2,1)S(1)} async-done(((bf16[8,24,1280]{2,1,0:T(8,128)(2,1)}), bf16[8,24,1280]{2,1,0:T(8,128)(2,1)S(1)}, u32[]{:S(2)}, u32[]{:S(2)}) %all-to-all-start) | async-done | bytes 491552 | tf_op jit(solution)/shard_map/all_to_all | solution.py:475
  87.6 1.4 %step_last.1 = (f32[24,1152]{1,0:T(8,128)}, f32[1,1]{1,0:T(1,128)}) custom-call(f32[1,1]{1,0:T(1,128)} %collective-permute-done.refs_0_, f32[1,1]{1,0:T(1,128)} %bitcast.6.refs_1_, bf16[192,1280]{1,0:T(8,128)(2,1)S(1)} %bitcast.7), custom_call_target="tpu_custom_call" | custom-call | tf_op jit(solution)/shard_map/step_last/pallas_call | solution.py:121
  (49 shorter events, 13.4 us)
Async XLA Ops:
  2.4 16.3 %collective-permute-start.9 = (bf16[2,64,1152]{2,1,0:T(8,128)(2,1)S(1)}, bf16[2,64,1152]{2,1,0:T(8,128)(2,1)S(1)}, u32[]{:S(2)}, u32[]{:S(2)}) collective-permute-start(bf16[2,64,1152]{2,1,0:T(8,128)(2,1)S(1)} %mask.1.co_a.refs_4_), channel_id=1, source_target_pairs={{0,6},{1,7},{2,4},{3,5},{4,0},{5,1},{6,2},{7,3},{8,14},{9,15},{10,... | collective-permute-start | bytes 884744 | tf_op jit(solution)/shard_map/ppermute | solution.py:36
  3.3 15.7 %collective-permute-start.7 = (bf16[2,64,1152]{2,1,0:T(8,128)(2,1)S(1)}, bf16[2,64,1152]{2,1,0:T(8,128)(2,1)S(1)}, u32[]{:S(2)}, u32[]{:S(2)}) collective-permute-start(bf16[2,64,1152]{2,1,0:T(8,128)(2,1)S(1)} %mask.1.co_a.refs_4_), channel_id=1, source_target_pairs={{0,4},{1,5},{2,6},{3,7},{4,2},{5,3},{6,0},{7,1},{8,12},{9,13},{10,... | collective-permute-start | bytes 884744 | tf_op jit(solution)/shard_map/ppermute | solution.py:36
  5.7 13.5 %collective-permute-start.2 = (bf16[2,64,1152]{2,1,0:T(8,128)(2,1)}, bf16[2,64,1152]{2,1,0:T(8,128)(2,1)S(1)}, u32[]{:S(2)}, u32[]{:S(2)}) collective-permute-start(bf16[2,64,1152]{2,1,0:T(8,128)(2,1)} %refs_0_.1), channel_id=1, source_target_pairs={{0,4},{1,5},{2,6},{3,7},{4,2},{5,3},{6,0},{7,1},{8,12},{9,13},{10,... | collective-permute-start | bytes 884744 | tf_op jit(solution)/shard_map/ppermute | solution.py:36
  6.7 12.8 %collective-permute-start.5 = (bf16[2,64,1152]{2,1,0:T(8,128)(2,1)}, bf16[2,64,1152]{2,1,0:T(8,128)(2,1)S(1)}, u32[]{:S(2)}, u32[]{:S(2)}) collective-permute-start(bf16[2,64,1152]{2,1,0:T(8,128)(2,1)} %refs_0_.1), channel_id=1, source_target_pairs={{0,6},{1,7},{2,4},{3,5},{4,0},{5,1},{6,2},{7,3},{8,14},{9,15},{10,... | collective-permute-start | bytes 884744 | tf_op jit(solution)/shard_map/ppermute | solution.py:36
  17.1 1.3 %collective-permute-start = (f32[1,1]{1,0:T(1,128)}, f32[1,1]{1,0:T(1,128)}, u32[]{:S(2)}, u32[]{:S(2)}) collective-permute-start(f32[1,1]{1,0:T(1,128)} %bitcast), channel_id=1, source_target_pairs={{0,1},{1,0},{2,3},{3,2},{4,5},{5,4},{6,7},{7,6},{8,9},{9,8},{10,11... | collective-permute-start | bytes 20 | tf_op jit(solution)/shard_map/ppermute | solution.py:36
  18.5 1.6 %collective-permute-start.11 = (bf16[2,64,1152]{2,1,0:T(8,128)(2,1)S(1)}, bf16[2,64,1152]{2,1,0:T(8,128)(2,1)S(1)}, u32[]{:S(2)}, u32[]{:S(2)}) collective-permute-start(bf16[2,64,1152]{2,1,0:T(8,128)(2,1)S(1)} %mask.1.co_a.refs_4_), channel_id=1, source_target_pairs={{0,1},{1,0},{2,3},{3,2},{4,5},{5,4},{6,7},{7,6},{8,9},{9,8},{10,11... | collective-permute-start | bytes 884744 | tf_op jit(solution)/shard_map/ppermute | solution.py:36
  18.7 1.8 %collective-permute-start.1 = (bf16[2,64,1152]{2,1,0:T(8,128)(2,1)S(1)}, bf16[2,64,1152]{2,1,0:T(8,128)(2,1)S(1)}, u32[]{:S(2)}, u32[]{:S(2)}) collective-permute-start(bf16[2,64,1152]{2,1,0:T(8,128)(2,1)S(1)} %copy-done.2), channel_id=1, source_target_pairs={{0,1},{1,0},{2,3},{3,2},{4,5},{5,4},{6,7},{7,6},{8,9},{9,8},{10,11... | collective-permute-start | bytes 884744 | tf_op jit(solution)/shard_map/ppermute | solution.py:36
  19.0 1.9 %collective-permute-start.10 = (bf16[2,64,1152]{2,1,0:T(8,128)(2,1)S(1)}, bf16[2,64,1152]{2,1,0:T(8,128)(2,1)S(1)}, u32[]{:S(2)}, u32[]{:S(2)}) collective-permute-start(bf16[2,64,1152]{2,1,0:T(8,128)(2,1)S(1)} %collective-permute-done.9.refs_6_), channel_id=1, source_target_pairs={{0,1},{1,0},{2,3},{3,2},{4,5},{5,4},{6,7},{7,6},{8,9},{9,8},{10,11... | collective-permute-start | bytes 884744 | tf_op jit(solution)/shard_map/ppermute | solution.py:36
  19.2 5.9 %collective-permute-start.8 = (bf16[2,64,1152]{2,1,0:T(8,128)(2,1)S(1)}, bf16[2,64,1152]{2,1,0:T(8,128)(2,1)S(1)}, u32[]{:S(2)}, u32[]{:S(2)}) collective-permute-start(bf16[2,64,1152]{2,1,0:T(8,128)(2,1)S(1)} %collective-permute-done.7.refs_4_), channel_id=1, source_target_pairs={{0,1},{1,0},{2,3},{3,2},{4,5},{5,4},{6,7},{7,6},{8,9},{9,8},{10,11... | collective-permute-start | bytes 884744 | tf_op jit(solution)/shard_map/ppermute | solution.py:36
  19.5 5.6 %collective-permute-start.4 = (bf16[2,64,1152]{2,1,0:T(8,128)(2,1)S(1)}, bf16[2,64,1152]{2,1,0:T(8,128)(2,1)S(1)}, u32[]{:S(2)}, u32[]{:S(2)}) collective-permute-start(bf16[2,64,1152]{2,1,0:T(8,128)(2,1)S(1)} %collective-permute-done.2.refs_0_), channel_id=1, source_target_pairs={{0,1},{1,0},{2,3},{3,2},{4,5},{5,4},{6,7},{7,6},{8,9},{9,8},{10,11... | collective-permute-start | bytes 884744 | tf_op jit(solution)/shard_map/ppermute | solution.py:36
  20.0 5.1 %collective-permute-start.6 = (bf16[2,64,1152]{2,1,0:T(8,128)(2,1)S(1)}, bf16[2,64,1152]{2,1,0:T(8,128)(2,1)S(1)}, u32[]{:S(2)}, u32[]{:S(2)}) collective-permute-start(bf16[2,64,1152]{2,1,0:T(8,128)(2,1)S(1)} %collective-permute-done.5.refs_2_), channel_id=1, source_target_pairs={{0,1},{1,0},{2,3},{3,2},{4,5},{5,4},{6,7},{7,6},{8,9},{9,8},{10,11... | collective-permute-start | bytes 884744 | tf_op jit(solution)/shard_map/ppermute | solution.py:36
  20.5 10.4 %collective-permute-start.13 = (bf16[2,64,1152]{2,1,0:T(8,128)(2,1)S(1)}, bf16[2,64,1152]{2,1,0:T(8,128)(2,1)S(1)}, u32[]{:S(2)}, u32[]{:S(2)}) collective-permute-start(bf16[2,64,1152]{2,1,0:T(8,128)(2,1)S(1)} %collective-permute-done.9.refs_6_), channel_id=1, source_target_pairs={{0,6},{1,7},{2,4},{3,5},{4,0},{5,1},{6,2},{7,3},{8,14},{9,15},{10,... | collective-permute-start | bytes 884744 | tf_op jit(solution)/shard_map/ppermute | solution.py:36
  20.9 9.9 %collective-permute-start.3 = (bf16[2,64,1152]{2,1,0:T(8,128)(2,1)S(1)}, bf16[2,64,1152]{2,1,0:T(8,128)(2,1)S(1)}, u32[]{:S(2)}, u32[]{:S(2)}) collective-permute-start(bf16[2,64,1152]{2,1,0:T(8,128)(2,1)S(1)} %collective-permute-done.2.refs_0_), channel_id=1, source_target_pairs={{0,4},{1,5},{2,6},{3,7},{4,2},{5,3},{6,0},{7,1},{8,12},{9,13},{10,... | collective-permute-start | bytes 884744 | tf_op jit(solution)/shard_map/ppermute | solution.py:36
  30.8 1.6 %collective-permute-start.14 = (bf16[2,64,1152]{2,1,0:T(8,128)(2,1)S(1)}, bf16[2,64,1152]{2,1,0:T(8,128)(2,1)S(1)}, u32[]{:S(2)}, u32[]{:S(2)}) collective-permute-start(bf16[2,64,1152]{2,1,0:T(8,128)(2,1)S(1)} %collective-permute-done.13.refs_6_), channel_id=1, source_target_pairs={{0,1},{1,0},{2,3},{3,2},{4,5},{5,4},{6,7},{7,6},{8,9},{9,8},{10,11... | collective-permute-start | bytes 884744 | tf_op jit(solution)/shard_map/ppermute | solution.py:36
  30.8 2.0 %collective-permute-start.12 = (bf16[2,64,1152]{2,1,0:T(8,128)(2,1)S(1)}, bf16[2,64,1152]{2,1,0:T(8,128)(2,1)S(1)}, u32[]{:S(2)}, u32[]{:S(2)}) collective-permute-start(bf16[2,64,1152]{2,1,0:T(8,128)(2,1)S(1)} %collective-permute-done.3.refs_2_), channel_id=1, source_target_pairs={{0,1},{1,0},{2,3},{3,2},{4,5},{5,4},{6,7},{7,6},{8,9},{9,8},{10,11... | collective-permute-start | bytes 884744 | tf_op jit(solution)/shard_map/ppermute | solution.py:36
  35.3 1.3 %collective-permute-start.15 = (f32[4,8,128]{2,1,0:T(8,128)S(1)}, f32[4,8,128]{2,1,0:T(8,128)S(1)}, u32[]{:S(2)}, u32[]{:S(2)}) collective-permute-start(f32[4,8,128]{2,1,0:T(8,128)S(1)} %get-tuple-element.44.left), channel_id=1, source_target_pairs={{0,1},{1,0},{2,3},{3,2},{4,5},{5,4},{6,7},{7,6},{8,9},{9,8},{10,11... | collective-permute-start | bytes 49160 | tf_op jit(solution)/shard_map/ppermute | solution.py:36
  36.6 5.2 %collective-permute-start.16 = (f32[4,8,128]{2,1,0:T(8,128)S(1)}, f32[4,8,128]{2,1,0:T(8,128)S(1)}, u32[]{:S(2)}, u32[]{:S(2)}) collective-permute-start(f32[4,8,128]{2,1,0:T(8,128)S(1)} %chip_squares.1.refs_1_), channel_id=1, source_target_pairs={{0,2},{1,3},{2,0},{3,1},{4,6},{5,7},{6,4},{7,5},{8,10},{9,11},{10,... | collective-permute-start | bytes 49160 | tf_op jit(solution)/shard_map/ppermute | solution.py:36
  38.3 3.7 %collective-permute-start.17 = (f32[4,8,128]{2,1,0:T(8,128)S(1)}, f32[4,8,128]{2,1,0:T(8,128)S(1)}, u32[]{:S(2)}, u32[]{:S(2)}) collective-permute-start(f32[4,8,128]{2,1,0:T(8,128)S(1)} %chip_squares.1.refs_1_), channel_id=1, source_target_pairs={{0,4},{1,5},{2,6},{3,7},{4,2},{5,3},{6,0},{7,1},{8,12},{9,13},{10,... | collective-permute-start | bytes 49160 | tf_op jit(solution)/shard_map/ppermute | solution.py:36
  39.2 5.0 %collective-permute-start.18 = (f32[4,8,128]{2,1,0:T(8,128)S(1)}, f32[4,8,128]{2,1,0:T(8,128)S(1)}, u32[]{:S(2)}, u32[]{:S(2)}) collective-permute-start(f32[4,8,128]{2,1,0:T(8,128)S(1)} %chip_squares.1.refs_1_), channel_id=1, source_target_pairs={{0,6},{1,7},{2,4},{3,5},{4,0},{5,1},{6,2},{7,3},{8,14},{9,15},{10,... | collective-permute-start | bytes 49160 | tf_op jit(solution)/shard_map/ppermute | solution.py:36
  46.1 8.8 %collective-permute-start.19 = (bf16[208,1152]{1,0:T(8,128)(2,1)S(1)}, bf16[208,1152]{1,0:T(8,128)(2,1)S(1)}, u32[]{:S(2)}, u32[]{:S(2)}) collective-permute-start(bf16[208,1152]{1,0:T(8,128)(2,1)S(1)} %get-tuple-element.52), channel_id=1, source_target_pairs={{0,32},{1,9},{2,34},{3,11},{4,36},{5,13},{6,38},{7,15},{8,40},{9,1... | collective-permute-start | bytes 1437704 | tf_op jit(solution)/shard_map/ppermute | solution.py:36
  48.1 12.9 %collective-permute-start.20 = (bf16[192,1152]{1,0:T(8,128)(2,1)S(1)}, bf16[192,1152]{1,0:T(8,128)(2,1)S(1)}, u32[]{:S(2)}, u32[]{:S(2)}) collective-permute-start(bf16[192,1152]{1,0:T(8,128)(2,1)S(1)} %get-tuple-element.56), channel_id=1, source_target_pairs={{0,224},{1,25},{2,226},{3,27},{4,228},{5,29},{6,230},{7,31},{8,232... | collective-permute-start | bytes 1327112 | tf_op jit(solution)/shard_map/ppermute | solution.py:36
  55.1 12.0 %collective-permute-start.21 = (bf16[112,1152]{1,0:T(8,128)(2,1)S(1)}, bf16[112,1152]{1,0:T(8,128)(2,1)S(1)}, u32[]{:S(2)}, u32[]{:S(2)}) collective-permute-start(bf16[112,1152]{1,0:T(8,128)(2,1)S(1)} %get-tuple-element.58), channel_id=1, source_target_pairs={{0,224},{1,25},{2,226},{3,27},{4,228},{5,29},{6,230},{7,31},{8,232... | collective-permute-start | bytes 774152 | tf_op jit(solution)/shard_map/ppermute | solution.py:36
  61.1 6.0 %collective-permute-start.22 = (bf16[96,1152]{1,0:T(8,128)(2,1)S(1)}, bf16[96,1152]{1,0:T(8,128)(2,1)S(1)}, u32[]{:S(2)}, u32[]{:S(2)}) collective-permute-start(bf16[96,1152]{1,0:T(8,128)(2,1)S(1)} %get-tuple-element.59), channel_id=1, source_target_pairs={{0,32},{1,9},{2,34},{3,11},{4,36},{5,13},{6,38},{7,15},{8,40},{9,1... | collective-permute-start | bytes 663560 | tf_op jit(solution)/shard_map/ppermute | solution.py:36
  68.1 19.5 %all-to-all-start = ((bf16[8,24,1280]{2,1,0:T(8,128)(2,1)}), bf16[8,24,1280]{2,1,0:T(8,128)(2,1)S(1)}, u32[]{:S(2)}, u32[]{:S(2)}) async-start(bf16[8,24,1280]{2,1,0:T(8,128)(2,1)} %bitcast.3), calls=%async_computation | async-start | bytes 983040 | tf_op jit(solution)/shard_map/all_to_all | solution.py:475
  (6 other events, 12.6 us)

commit v5 on v4

--- a/solution.py
+++ b/solution.py
@@ -299,15 +299,20 @@
     return total
 
 
-def outer_send_kernel(examples, *refs):
-    small, operands, (out0, out1, count_out, scale_out) = refs[:5], refs[5:9], refs[9:]
-    rows, width = out1.shape
+def outer_first_kernel(examples, *refs):
+    small, operands, (out, count_out, scale_out) = refs[:5], refs[5:9], refs[9:]
+    rows, width = out.shape[0] - TAIL, out.shape[1]
     scale, count = factors_of(examples, *small)
     count_out[...] = count
     scale_out[...] = scale
     total = outer_rows(0, rows, scale, operands)
-    out0[...] = jnp.concatenate([total, *tail_rows(count, TAIL, width)], axis=0).astype(out0.dtype)
-    out1[...] = outer_rows(rows, rows, scale, operands).astype(out1.dtype)
+    out[...] = jnp.concatenate([total, *tail_rows(count, TAIL, width)], axis=0).astype(out.dtype)
+
+
+def outer_second_kernel(scale, *refs):
+    operands, out = refs[:4], refs[4]
+    rows = out.shape[0]
+    out[...] = outer_rows(rows, rows, scale[...], operands).astype(out.dtype)
 
 
 def outer_keep_kernel(scale, *refs):
@@ -317,15 +322,18 @@
         out[...] = outer_rows((2 + chain) * rows, rows, scale[...], operands)
 
 
-def outer_send(rows, examples, small, operands):
-    width = operands[2].shape[2]
+def outer_first(rows, examples, small, operands):
     outs = (
-        array((rows + TAIL, width), jnp.bfloat16),
-        array((rows, width), jnp.bfloat16),
+        array((rows + TAIL, operands[2].shape[2]), jnp.bfloat16),
         array(LANES, jnp.float32),
         array((4, *LANES), jnp.float32),
     )
-    return call(lambda *refs: outer_send_kernel(examples, *refs), "outer_send", outs, (*small, *operands))
+    return call(lambda *refs: outer_first_kernel(examples, *refs), "outer_first", outs, (*small, *operands))
+
+
+def outer_second(rows, scale, operands):
+    out = array((rows, operands[2].shape[2]), jnp.bfloat16)
+    return call(outer_second_kernel, "outer_second", out, (scale, *operands))
 
 
 def outer_keep(rows, scale, operands):
@@ -433,7 +441,7 @@
 def per_device(inputs, cotangent, lengths, up_weight, down_weight, clip_ratio, count_noise):
     in_l = permute(inputs, right)
     masked = call(
-        mask_kernel, "mask", array(cotangent.shape, cotangent.dtype), (lengths.reshape(1, -1), cotangent)
+        mask_kernel, "mask", array(cotangent.shape, cotangent.dtype), (lengths.reshape(1, -1), cotangent), flops=5 * 10**9
     )
     co_r = permute(masked, left)
 
@@ -464,7 +472,8 @@
     examples_all = lax.axis_size("dp") * lengths.shape[0]
     operands = (hidden_ours, hidden_theirs, masked_ours, masked_theirs)
     quarter = units // 8
-    send0, send1, count, scale = outer_send(quarter, examples_all, small, operands)
+    send0, count, scale = outer_first(quarter, examples_all, small, operands)
+    send1 = outer_second(quarter, scale, operands)
     got0, got1 = exchange(send0, 0, 0), exchange(send1, 0, 1)
     keep0, keep1 = outer_keep(quarter, scale, operands)
     count, keep0, send0 = step_first(count, keep0, got0)

time: 89.3 us -> 89.1 us (level)
  local copies, waits for them, and re-layouts: 4.55 us -> 1.63 us
  starting transfers between devices: 34 us -> 35.9 us
    unnamed x12, local copies, waits for them, and re-layouts: 4.55 us -> 1.63 us
    ppermute x23, waiting for transfers between devices: 17.1 us -> 18.3 us  [permute(): return lax.ppermute(array, AXES, pairs)]
    ppermute x23, starting transfers between devices: 27.2 us -> 28.2 us  [permute(): return lax.ppermute(array, AXES, pairs)]
    pallas_call x13 -> x14, Pallas kernels: 19.9 us -> 20.1 us  [call(): pl.pallas_call(kernel, out_shape=outs, in_specs=specs or [VMEM] * len(arg...]
  transfers between devices with their start and end apart: 24 -> 24, of which waited for: 14 -> 12; matrix products, arithmetic and copies ran while one was open for 0% -> 0% of each run, Pallas kernels for 15% -> 15%
where the time goes in v5:
time: 89.1 us; the launch traced here: 88.9 us
  starting transfers between devices  35.9 us (40%)
  waiting for transfers between devices  29.8 us (33%)
  Pallas kernels  20.1 us (23%)
  local copies, waits for them, and re-layouts  1.63 us (2%)
  between operations  1.45 us (2%)
    ppermute x23, starting transfers between devices, permute(): return lax.ppermute(array, AXES, pairs)  28.2 us
    pallas_call x14, Pallas kernels, call(): pl.pallas_call(kernel, out_shape=outs, in_specs=specs or [VMEM] * len(arg...  20.1 us
    ppermute x23, waiting for transfers between devices, permute(): return lax.ppermute(array, AXES, pairs)  18.3 us
    all_to_all x1, waiting for transfers between devices, per_device(): got = lax.all_to_all(send, AXES, 0, 0, axis_index_groups=GROUPS, tiled=True)  11.5 us
    all_to_all x1, starting transfers between devices, per_device(): got = lax.all_to_all(send, AXES, 0, 0, axis_index_groups=GROUPS, tiled=True)  7.61 us
  transfers between devices with their start and end apart: 24, of which 12 were waited for; matrix products, arithmetic and copies ran while one was open for 0% of the time, Pallas kernels for 15%

profile of v5, /device:TPU:6, one launch (start us, length us, event | category | flops | bytes accessed | tf_op | source)
XLA Modules:
  0.0 88.9 jit_solution(4057412526628383210)
XLA Ops:
  3.3 2.4 %collective-permute-start.7 = (bf16[2,64,1152]{2,1,0:T(8,128)(2,1)S(1)}, bf16[2,64,1152]{2,1,0:T(8,128)(2,1)S(1)}, u32[]{:S(2)}, u32[]{:S(2)}) collective-permute-start(bf16[2,64,1152]{2,1,0:T(8,128)(2,1)S(1)} %mask.1.co_a.refs_4_), channel_id=1, source_target_pairs={{0,4},{1,5},{2,6},{3,7},{4,2},{5,3},{6,0},{7,1},{8,12},{9,13},{10,... | collective-permute-start | bytes 884744 | tf_op jit(solution)/shard_map/ppermute | solution.py:36
  7.8 2.9 %select_up.1.up.refs_8_ = bf16[1152,768]{1,0:T(8,128)(2,1)S(1)} custom-call(s32[64,1,768]{2,1,0:T(1,128)S(1)} %copy-done.3, bf16[1152,1536]{1,0:T(8,128)(2,1)S(1)} %copy-done), custom_call_target="tpu_custom_call" | custom-call | tf_op jit(solution)/shard_map/select_up/pallas_call | solution.py:121
  10.7 3.5 %select_down.1.down.refs_9_ = bf16[768,1152]{1,0:T(8,128)(2,1)S(1)} custom-call(s32[64,1,768]{2,1,0:T(1,128)S(1)} %copy-done.3, bf16[1536,1152]{1,0:T(8,128)(2,1)S(1)} %copy-done.1), custom_call_target="tpu_custom_call" | custom-call | tf_op jit(solution)/shard_map/select_down/pallas_call | solution.py:121
  14.3 1.2 %collective-permute-done.refs_0_ = f32[1,1]{1,0:T(1,128)} collective-permute-done((f32[1,1]{1,0:T(1,128)}, f32[1,1]{1,0:T(1,128)}, u32[]{:S(2)}, u32[]{:S(2)}) %collective-permute-start) | collective-permute-done | bytes 36 | tf_op jit(solution)/shard_map/ppermute | solution.py:36
  16.3 1.8 %collective-permute-done.2.refs_0_ = bf16[2,64,1152]{2,1,0:T(8,128)(2,1)S(1)} collective-permute-done((bf16[2,64,1152]{2,1,0:T(8,128)(2,1)S(1)}, bf16[2,64,1152]{2,1,0:T(8,128)(2,1)S(1)}, u32[]{:S(2)}, u32[]{:S(2)}) %collective-permute-start.2) | collective-permute-done | bytes 294944 | tf_op jit(solution)/shard_map/ppermute | solution.py:36
  19.4 3.2 %collective-permute-start.3 = (bf16[2,64,1152]{2,1,0:T(8,128)(2,1)S(1)}, bf16[2,64,1152]{2,1,0:T(8,128)(2,1)S(1)}, u32[]{:S(2)}, u32[]{:S(2)}) collective-permute-start(bf16[2,64,1152]{2,1,0:T(8,128)(2,1)S(1)} %collective-permute-done.2.refs_0_), channel_id=1, source_target_pairs={{0,4},{1,5},{2,6},{3,7},{4,2},{5,3},{6,0},{7,1},{8,12},{9,13},{10,... | collective-permute-start | bytes 884744 | tf_op jit(solution)/shard_map/ppermute | solution.py:36
  22.6 1.4 %early_pass.1 = (bf16[256,768]{1,0:T(8,128)(2,1)S(1)}, bf16[256,768]{1,0:T(8,128)(2,1)S(1)}) custom-call(bf16[2,64,1152]{2,1,0:T(8,128)(2,1)S(1)} %copy-done.2, bf16[2,64,1152]{2,1,0:T(8,128)(2,1)S(1)} %collective-permute-done.1.in_b.refs_1_, bf16[2,64,1152]{2,1,0:T(8,128)(2,1)S(1)} %mask.1.co_a.refs_4_, ...), custom_call_target="tpu_custom_call" | custom-call | tf_op jit(solution)/shard_map/early_pass/pallas_call | solution.py:121
  24.0 3.6 %theirs_pass.1 = (bf16[2,768,256]{2,1,0:T(8,128)(2,1)S(1)}, bf16[2,256,1152]{2,1,0:T(8,128)(2,1)S(1)}, f32[2,8,128]{2,1,0:T(8,128)S(1)}) custom-call(bf16[2,64,1152]{2,1,0:T(8,128)(2,1)S(1)} %collective-permute-done.2.refs_0_, bf16[2,64,1152]{2,1,0:T(8,128)(2,1)S(1)} %collective-permute-done.4.refs_1_, ...), custom_call_target="tpu_custom_call" | custom-call | tf_op jit(solution)/shard_map/theirs_pass/pallas_call | solution.py:121
  27.6 2.3 %collective-permute-done.13.refs_6_ = bf16[2,64,1152]{2,1,0:T(8,128)(2,1)S(1)} collective-permute-done((bf16[2,64,1152]{2,1,0:T(8,128)(2,1)S(1)}, bf16[2,64,1152]{2,1,0:T(8,128)(2,1)S(1)}, u32[]{:S(2)}, u32[]{:S(2)}) %collective-permute-start.13) | collective-permute-done | bytes 294944 | tf_op jit(solution)/shard_map/ppermute | solution.py:36
  30.4 1.1 %collective-permute-done.14.refs_7_ = bf16[2,64,1152]{2,1,0:T(8,128)(2,1)S(1)} collective-permute-done((bf16[2,64,1152]{2,1,0:T(8,128)(2,1)S(1)}, bf16[2,64,1152]{2,1,0:T(8,128)(2,1)S(1)}, u32[]{:S(2)}, u32[]{:S(2)}) %collective-permute-start.14) | collective-permute-done | bytes 294944 | tf_op jit(solution)/shard_map/ppermute | solution.py:36
  31.9 2.5 %ours_pass.1 = (bf16[2,768,256]{2,1,0:T(8,128)(2,1)S(1)}, bf16[2,256,1152]{2,1,0:T(8,128)(2,1)S(1)}, f32[4,8,128]{2,1,0:T(8,128)S(1)}) custom-call(bf16[2,64,1152]{2,1,0:T(8,128)(2,1)S(1)} %copy-done.2, bf16[2,64,1152]{2,1,0:T(8,128)(2,1)S(1)} %collective-permute-done.1.in_b.refs_1_, bf16[2,64,1152]{2,1,0:T(8,128)(2,1)S(1)} %collective-permute-done.3.refs_2_, ...), custom_call_target="tpu_custom_call" | custom-call | tf_op jit(solution)/shard_map/ours_pass/pallas_call | solution.py:121
  34.6 1.0 %collective-permute-done.15.right = f32[4,8,128]{2,1,0:T(8,128)S(1)} collective-permute-done((f32[4,8,128]{2,1,0:T(8,128)S(1)}, f32[4,8,128]{2,1,0:T(8,128)S(1)}, u32[]{:S(2)}, u32[]{:S(2)}) %collective-permute-start.15) | collective-permute-done | bytes 16416 | tf_op jit(solution)/shard_map/ppermute | solution.py:36
  35.7 2.5 %collective-permute-start.16 = (f32[4,8,128]{2,1,0:T(8,128)S(1)}, f32[4,8,128]{2,1,0:T(8,128)S(1)}, u32[]{:S(2)}, u32[]{:S(2)}) collective-permute-start(f32[4,8,128]{2,1,0:T(8,128)S(1)} %chip_squares.1.refs_1_), channel_id=1, source_target_pairs={{0,2},{1,3},{2,0},{3,1},{4,6},{5,7},{6,4},{7,5},{8,10},{9,11},{10,... | collective-permute-start | bytes 49160 | tf_op jit(solution)/shard_map/ppermute | solution.py:36
  39.1 1.1 %collective-permute-start.18 = (f32[4,8,128]{2,1,0:T(8,128)S(1)}, f32[4,8,128]{2,1,0:T(8,128)S(1)}, u32[]{:S(2)}, u32[]{:S(2)}) collective-permute-start(f32[4,8,128]{2,1,0:T(8,128)S(1)} %chip_squares.1.refs_1_), channel_id=1, source_target_pairs={{0,6},{1,7},{2,4},{3,5},{4,0},{5,1},{6,2},{7,3},{8,14},{9,15},{10,... | collective-permute-start | bytes 49160 | tf_op jit(solution)/shard_map/ppermute | solution.py:36
  41.9 2.1 %collective-permute-done.18.refs_4_ = f32[4,8,128]{2,1,0:T(8,128)S(1)} collective-permute-done((f32[4,8,128]{2,1,0:T(8,128)S(1)}, f32[4,8,128]{2,1,0:T(8,128)S(1)}, u32[]{:S(2)}, u32[]{:S(2)}) %collective-permute-start.18) | collective-permute-done | bytes 16416 | tf_op jit(solution)/shard_map/ppermute | solution.py:36
  44.0 1.4 %outer_first.1 = (bf16[208,1152]{1,0:T(8,128)(2,1)S(1)}, f32[8,128]{1,0:T(8,128)S(1)}, f32[4,8,128]{2,1,0:T(8,128)S(1)}) custom-call(f32[1,1]{1,0:T(1,128)} %collective-permute-done.refs_0_, f32[4,8,128]{2,1,0:T(8,128)S(1)} %chip_squares.1.refs_1_, f32[4,8,128]{2,1,0:T(8,128)S(1)} %collective-permute-done.16.refs_2_, ...), custom_call_target="tpu_custom_call" | custom-call | tf_op jit(solution)/shard_map/outer_first/pallas_call | solution.py:121
  45.5 2.2 %collective-permute-start.19 = (bf16[208,1152]{1,0:T(8,128)(2,1)S(1)}, bf16[208,1152]{1,0:T(8,128)(2,1)S(1)}, u32[]{:S(2)}, u32[]{:S(2)}) collective-permute-start(bf16[208,1152]{1,0:T(8,128)(2,1)S(1)} %get-tuple-element.51), channel_id=1, source_target_pairs={{0,32},{1,9},{2,34},{3,11},{4,36},{5,13},{6,38},{7,15},{8,40},{9,1... | collective-permute-start | bytes 1437704 | tf_op jit(solution)/shard_map/ppermute | solution.py:36
  48.4 5.0 %collective-permute-start.20 = (bf16[192,1152]{1,0:T(8,128)(2,1)S(1)}, bf16[192,1152]{1,0:T(8,128)(2,1)S(1)}, u32[]{:S(2)}, u32[]{:S(2)}) collective-permute-start(bf16[192,1152]{1,0:T(8,128)(2,1)S(1)} %outer_second.1), channel_id=1, source_target_pairs={{0,224},{1,25},{2,226},{3,27},{4,228},{5,29},{6,230},{7,31},{8,232... | collective-permute-start | bytes 1327112 | tf_op jit(solution)/shard_map/ppermute | solution.py:36
  53.5 1.3 %outer_keep.1 = (f32[192,1152]{1,0:T(8,128)S(1)}, f32[192,1152]{1,0:T(8,128)S(1)}) custom-call(f32[4,8,128]{2,1,0:T(8,128)S(1)} %get-tuple-element.49.scale, bf16[2,768,256]{2,1,0:T(8,128)(2,1)S(1)} %get-tuple-element.44.refs_5_.refs_0_, bf16[2,768,256]{2,1,0:T(8,128)(2,1)S(1)} %get-tuple-element.45.refs_6_.refs_1_, ...), custom_call_target="tpu_custom_call" | custom-call | tf_op jit(solution)/shard_map/outer_keep/pallas_call | solution.py:121
  55.0 5.6 %collective-permute-start.21 = (bf16[112,1152]{1,0:T(8,128)(2,1)S(1)}, bf16[112,1152]{1,0:T(8,128)(2,1)S(1)}, u32[]{:S(2)}, u32[]{:S(2)}) collective-permute-start(bf16[112,1152]{1,0:T(8,128)(2,1)S(1)} %get-tuple-element.56), channel_id=1, source_target_pairs={{0,224},{1,25},{2,226},{3,27},{4,228},{5,29},{6,230},{7,31},{8,232... | collective-permute-start | bytes 774152 | tf_op jit(solution)/shard_map/ppermute | solution.py:36
  60.8 5.9 %collective-permute-done.22.got1 = bf16[96,1152]{1,0:T(8,128)(2,1)S(1)} collective-permute-done((bf16[96,1152]{1,0:T(8,128)(2,1)S(1)}, bf16[96,1152]{1,0:T(8,128)(2,1)S(1)}, u32[]{:S(2)}, u32[]{:S(2)}) %collective-permute-start.22) | collective-permute-done | bytes 221216 | tf_op jit(solution)/shard_map/ppermute | solution.py:36
  67.7 7.6 %all-to-all-start = ((bf16[8,24,1280]{2,1,0:T(8,128)(2,1)}), bf16[8,24,1280]{2,1,0:T(8,128)(2,1)S(1)}, u32[]{:S(2)}, u32[]{:S(2)}) async-start(bf16[8,24,1280]{2,1,0:T(8,128)(2,1)} %bitcast.3), calls=%async_computation | async-start | bytes 983040 | tf_op jit(solution)/shard_map/all_to_all | solution.py:484
  75.9 11.5 %all-to-all-done = bf16[8,24,1280]{2,1,0:T(8,128)(2,1)S(1)} async-done(((bf16[8,24,1280]{2,1,0:T(8,128)(2,1)}), bf16[8,24,1280]{2,1,0:T(8,128)(2,1)S(1)}, u32[]{:S(2)}, u32[]{:S(2)}) %all-to-all-start) | async-done | bytes 491552 | tf_op jit(solution)/shard_map/all_to_all | solution.py:484
  87.5 1.4 %step_last.1 = (f32[24,1152]{1,0:T(8,128)}, f32[1,1]{1,0:T(1,128)}) custom-call(f32[1,1]{1,0:T(1,128)} %collective-permute-done.refs_0_, f32[1,1]{1,0:T(1,128)} %bitcast.6.refs_1_, bf16[192,1280]{1,0:T(8,128)(2,1)S(1)} %bitcast.7), custom_call_target="tpu_custom_call" | custom-call | tf_op jit(solution)/shard_map/step_last/pallas_call | solution.py:121
  (50 shorter events, 12.7 us)
Async XLA Ops:
  2.4 13.4 %collective-permute-start.9 = (bf16[2,64,1152]{2,1,0:T(8,128)(2,1)S(1)}, bf16[2,64,1152]{2,1,0:T(8,128)(2,1)S(1)}, u32[]{:S(2)}, u32[]{:S(2)}) collective-permute-start(bf16[2,64,1152]{2,1,0:T(8,128)(2,1)S(1)} %mask.1.co_a.refs_4_), channel_id=1, source_target_pairs={{0,6},{1,7},{2,4},{3,5},{4,0},{5,1},{6,2},{7,3},{8,14},{9,15},{10,... | collective-permute-start | bytes 884744 | tf_op jit(solution)/shard_map/ppermute | solution.py:36
  3.3 12.8 %collective-permute-start.7 = (bf16[2,64,1152]{2,1,0:T(8,128)(2,1)S(1)}, bf16[2,64,1152]{2,1,0:T(8,128)(2,1)S(1)}, u32[]{:S(2)}, u32[]{:S(2)}) collective-permute-start(bf16[2,64,1152]{2,1,0:T(8,128)(2,1)S(1)} %mask.1.co_a.refs_4_), channel_id=1, source_target_pairs={{0,4},{1,5},{2,6},{3,7},{4,2},{5,3},{6,0},{7,1},{8,12},{9,13},{10,... | collective-permute-start | bytes 884744 | tf_op jit(solution)/shard_map/ppermute | solution.py:36
  5.7 12.4 %collective-permute-start.2 = (bf16[2,64,1152]{2,1,0:T(8,128)(2,1)S(1)}, bf16[2,64,1152]{2,1,0:T(8,128)(2,1)S(1)}, u32[]{:S(2)}, u32[]{:S(2)}) collective-permute-start(bf16[2,64,1152]{2,1,0:T(8,128)(2,1)S(1)} %copy-done.2), channel_id=1, source_target_pairs={{0,4},{1,5},{2,6},{3,7},{4,2},{5,3},{6,0},{7,1},{8,12},{9,13},{10,... | collective-permute-start | bytes 884744 | tf_op jit(solution)/shard_map/ppermute | solution.py:36
  6.7 12.0 %collective-permute-start.5 = (bf16[2,64,1152]{2,1,0:T(8,128)(2,1)S(1)}, bf16[2,64,1152]{2,1,0:T(8,128)(2,1)S(1)}, u32[]{:S(2)}, u32[]{:S(2)}) collective-permute-start(bf16[2,64,1152]{2,1,0:T(8,128)(2,1)S(1)} %copy-done.2), channel_id=1, source_target_pairs={{0,6},{1,7},{2,4},{3,5},{4,0},{5,1},{6,2},{7,3},{8,14},{9,15},{10,... | collective-permute-start | bytes 884744 | tf_op jit(solution)/shard_map/ppermute | solution.py:36
  14.2 1.3 %collective-permute-start = (f32[1,1]{1,0:T(1,128)}, f32[1,1]{1,0:T(1,128)}, u32[]{:S(2)}, u32[]{:S(2)}) collective-permute-start(f32[1,1]{1,0:T(1,128)} %bitcast), channel_id=1, source_target_pairs={{0,1},{1,0},{2,3},{3,2},{4,5},{5,4},{6,7},{7,6},{8,9},{9,8},{10,11... | collective-permute-start | bytes 20 | tf_op jit(solution)/shard_map/ppermute | solution.py:36
  15.5 3.2 %collective-permute-start.11 = (bf16[2,64,1152]{2,1,0:T(8,128)(2,1)S(1)}, bf16[2,64,1152]{2,1,0:T(8,128)(2,1)S(1)}, u32[]{:S(2)}, u32[]{:S(2)}) collective-permute-start(bf16[2,64,1152]{2,1,0:T(8,128)(2,1)S(1)} %mask.1.co_a.refs_4_), channel_id=1, source_target_pairs={{0,1},{1,0},{2,3},{3,2},{4,5},{5,4},{6,7},{7,6},{8,9},{9,8},{10,11... | collective-permute-start | bytes 884744 | tf_op jit(solution)/shard_map/ppermute | solution.py:36
  15.8 3.5 %collective-permute-start.1 = (bf16[2,64,1152]{2,1,0:T(8,128)(2,1)S(1)}, bf16[2,64,1152]{2,1,0:T(8,128)(2,1)S(1)}, u32[]{:S(2)}, u32[]{:S(2)}) collective-permute-start(bf16[2,64,1152]{2,1,0:T(8,128)(2,1)S(1)} %copy-done.2), channel_id=1, source_target_pairs={{0,1},{1,0},{2,3},{3,2},{4,5},{5,4},{6,7},{7,6},{8,9},{9,8},{10,11... | collective-permute-start | bytes 884744 | tf_op jit(solution)/shard_map/ppermute | solution.py:36
  16.1 3.4 %collective-permute-start.10 = (bf16[2,64,1152]{2,1,0:T(8,128)(2,1)S(1)}, bf16[2,64,1152]{2,1,0:T(8,128)(2,1)S(1)}, u32[]{:S(2)}, u32[]{:S(2)}) collective-permute-start(bf16[2,64,1152]{2,1,0:T(8,128)(2,1)S(1)} %collective-permute-done.9.refs_6_), channel_id=1, source_target_pairs={{0,1},{1,0},{2,3},{3,2},{4,5},{5,4},{6,7},{7,6},{8,9},{9,8},{10,11... | collective-permute-start | bytes 884744 | tf_op jit(solution)/shard_map/ppermute | solution.py:36
  18.1 5.9 %collective-permute-start.8 = (bf16[2,64,1152]{2,1,0:T(8,128)(2,1)S(1)}, bf16[2,64,1152]{2,1,0:T(8,128)(2,1)S(1)}, u32[]{:S(2)}, u32[]{:S(2)}) collective-permute-start(bf16[2,64,1152]{2,1,0:T(8,128)(2,1)S(1)} %collective-permute-done.7.refs_4_), channel_id=1, source_target_pairs={{0,1},{1,0},{2,3},{3,2},{4,5},{5,4},{6,7},{7,6},{8,9},{9,8},{10,11... | collective-permute-start | bytes 884744 | tf_op jit(solution)/shard_map/ppermute | solution.py:36
  18.8 5.2 %collective-permute-start.4 = (bf16[2,64,1152]{2,1,0:T(8,128)(2,1)S(1)}, bf16[2,64,1152]{2,1,0:T(8,128)(2,1)S(1)}, u32[]{:S(2)}, u32[]{:S(2)}) collective-permute-start(bf16[2,64,1152]{2,1,0:T(8,128)(2,1)S(1)} %collective-permute-done.2.refs_0_), channel_id=1, source_target_pairs={{0,1},{1,0},{2,3},{3,2},{4,5},{5,4},{6,7},{7,6},{8,9},{9,8},{10,11... | collective-permute-start | bytes 884744 | tf_op jit(solution)/shard_map/ppermute | solution.py:36
  18.8 5.2 %collective-permute-start.6 = (bf16[2,64,1152]{2,1,0:T(8,128)(2,1)S(1)}, bf16[2,64,1152]{2,1,0:T(8,128)(2,1)S(1)}, u32[]{:S(2)}, u32[]{:S(2)}) collective-permute-start(bf16[2,64,1152]{2,1,0:T(8,128)(2,1)S(1)} %collective-permute-done.5.refs_2_), channel_id=1, source_target_pairs={{0,1},{1,0},{2,3},{3,2},{4,5},{5,4},{6,7},{7,6},{8,9},{9,8},{10,11... | collective-permute-start | bytes 884744 | tf_op jit(solution)/shard_map/ppermute | solution.py:36
  19.3 10.6 %collective-permute-start.13 = (bf16[2,64,1152]{2,1,0:T(8,128)(2,1)S(1)}, bf16[2,64,1152]{2,1,0:T(8,128)(2,1)S(1)}, u32[]{:S(2)}, u32[]{:S(2)}) collective-permute-start(bf16[2,64,1152]{2,1,0:T(8,128)(2,1)S(1)} %collective-permute-done.9.refs_6_), channel_id=1, source_target_pairs={{0,6},{1,7},{2,4},{3,5},{4,0},{5,1},{6,2},{7,3},{8,14},{9,15},{10,... | collective-permute-start | bytes 884744 | tf_op jit(solution)/shard_map/ppermute | solution.py:36
  19.4 10.5 %collective-permute-start.3 = (bf16[2,64,1152]{2,1,0:T(8,128)(2,1)S(1)}, bf16[2,64,1152]{2,1,0:T(8,128)(2,1)S(1)}, u32[]{:S(2)}, u32[]{:S(2)}) collective-permute-start(bf16[2,64,1152]{2,1,0:T(8,128)(2,1)S(1)} %collective-permute-done.2.refs_0_), channel_id=1, source_target_pairs={{0,4},{1,5},{2,6},{3,7},{4,2},{5,3},{6,0},{7,1},{8,12},{9,13},{10,... | collective-permute-start | bytes 884744 | tf_op jit(solution)/shard_map/ppermute | solution.py:36
  29.9 1.6 %collective-permute-start.14 = (bf16[2,64,1152]{2,1,0:T(8,128)(2,1)S(1)}, bf16[2,64,1152]{2,1,0:T(8,128)(2,1)S(1)}, u32[]{:S(2)}, u32[]{:S(2)}) collective-permute-start(bf16[2,64,1152]{2,1,0:T(8,128)(2,1)S(1)} %collective-permute-done.13.refs_6_), channel_id=1, source_target_pairs={{0,1},{1,0},{2,3},{3,2},{4,5},{5,4},{6,7},{7,6},{8,9},{9,8},{10,11... | collective-permute-start | bytes 884744 | tf_op jit(solution)/shard_map/ppermute | solution.py:36
  29.9 2.0 %collective-permute-start.12 = (bf16[2,64,1152]{2,1,0:T(8,128)(2,1)S(1)}, bf16[2,64,1152]{2,1,0:T(8,128)(2,1)S(1)}, u32[]{:S(2)}, u32[]{:S(2)}) collective-permute-start(bf16[2,64,1152]{2,1,0:T(8,128)(2,1)S(1)} %collective-permute-done.3.refs_2_), channel_id=1, source_target_pairs={{0,1},{1,0},{2,3},{3,2},{4,5},{5,4},{6,7},{7,6},{8,9},{9,8},{10,11... | collective-permute-start | bytes 884744 | tf_op jit(solution)/shard_map/ppermute | solution.py:36
  34.4 1.3 %collective-permute-start.15 = (f32[4,8,128]{2,1,0:T(8,128)S(1)}, f32[4,8,128]{2,1,0:T(8,128)S(1)}, u32[]{:S(2)}, u32[]{:S(2)}) collective-permute-start(f32[4,8,128]{2,1,0:T(8,128)S(1)} %get-tuple-element.43.left), channel_id=1, source_target_pairs={{0,1},{1,0},{2,3},{3,2},{4,5},{5,4},{6,7},{7,6},{8,9},{9,8},{10,11... | collective-permute-start | bytes 49160 | tf_op jit(solution)/shard_map/ppermute | solution.py:36
  35.7 5.2 %collective-permute-start.16 = (f32[4,8,128]{2,1,0:T(8,128)S(1)}, f32[4,8,128]{2,1,0:T(8,128)S(1)}, u32[]{:S(2)}, u32[]{:S(2)}) collective-permute-start(f32[4,8,128]{2,1,0:T(8,128)S(1)} %chip_squares.1.refs_1_), channel_id=1, source_target_pairs={{0,2},{1,3},{2,0},{3,1},{4,6},{5,7},{6,4},{7,5},{8,10},{9,11},{10,... | collective-permute-start | bytes 49160 | tf_op jit(solution)/shard_map/ppermute | solution.py:36
  38.2 3.7 %collective-permute-start.17 = (f32[4,8,128]{2,1,0:T(8,128)S(1)}, f32[4,8,128]{2,1,0:T(8,128)S(1)}, u32[]{:S(2)}, u32[]{:S(2)}) collective-permute-start(f32[4,8,128]{2,1,0:T(8,128)S(1)} %chip_squares.1.refs_1_), channel_id=1, source_target_pairs={{0,4},{1,5},{2,6},{3,7},{4,2},{5,3},{6,0},{7,1},{8,12},{9,13},{10,... | collective-permute-start | bytes 49160 | tf_op jit(solution)/shard_map/ppermute | solution.py:36
  39.1 4.9 %collective-permute-start.18 = (f32[4,8,128]{2,1,0:T(8,128)S(1)}, f32[4,8,128]{2,1,0:T(8,128)S(1)}, u32[]{:S(2)}, u32[]{:S(2)}) collective-permute-start(f32[4,8,128]{2,1,0:T(8,128)S(1)} %chip_squares.1.refs_1_), channel_id=1, source_target_pairs={{0,6},{1,7},{2,4},{3,5},{4,0},{5,1},{6,2},{7,3},{8,14},{9,15},{10,... | collective-permute-start | bytes 49160 | tf_op jit(solution)/shard_map/ppermute | solution.py:36
  45.5 9.3 %collective-permute-start.19 = (bf16[208,1152]{1,0:T(8,128)(2,1)S(1)}, bf16[208,1152]{1,0:T(8,128)(2,1)S(1)}, u32[]{:S(2)}, u32[]{:S(2)}) collective-permute-start(bf16[208,1152]{1,0:T(8,128)(2,1)S(1)} %get-tuple-element.51), channel_id=1, source_target_pairs={{0,32},{1,9},{2,34},{3,11},{4,36},{5,13},{6,38},{7,15},{8,40},{9,1... | collective-permute-start | bytes 1437704 | tf_op jit(solution)/shard_map/ppermute | solution.py:36
  48.4 12.2 %collective-permute-start.20 = (bf16[192,1152]{1,0:T(8,128)(2,1)S(1)}, bf16[192,1152]{1,0:T(8,128)(2,1)S(1)}, u32[]{:S(2)}, u32[]{:S(2)}) collective-permute-start(bf16[192,1152]{1,0:T(8,128)(2,1)S(1)} %outer_second.1), channel_id=1, source_target_pairs={{0,224},{1,25},{2,226},{3,27},{4,228},{5,29},{6,230},{7,31},{8,232... | collective-permute-start | bytes 1327112 | tf_op jit(solution)/shard_map/ppermute | solution.py:36
  55.0 11.7 %collective-permute-start.21 = (bf16[112,1152]{1,0:T(8,128)(2,1)S(1)}, bf16[112,1152]{1,0:T(8,128)(2,1)S(1)}, u32[]{:S(2)}, u32[]{:S(2)}) collective-permute-start(bf16[112,1152]{1,0:T(8,128)(2,1)S(1)} %get-tuple-element.56), channel_id=1, source_target_pairs={{0,224},{1,25},{2,226},{3,27},{4,228},{5,29},{6,230},{7,31},{8,232... | collective-permute-start | bytes 774152 | tf_op jit(solution)/shard_map/ppermute | solution.py:36
  60.7 6.0 %collective-permute-start.22 = (bf16[96,1152]{1,0:T(8,128)(2,1)S(1)}, bf16[96,1152]{1,0:T(8,128)(2,1)S(1)}, u32[]{:S(2)}, u32[]{:S(2)}) collective-permute-start(bf16[96,1152]{1,0:T(8,128)(2,1)S(1)} %get-tuple-element.57), channel_id=1, source_target_pairs={{0,32},{1,9},{2,34},{3,11},{4,36},{5,13},{6,38},{7,15},{8,40},{9,1... | collective-permute-start | bytes 663560 | tf_op jit(solution)/shard_map/ppermute | solution.py:36
  67.7 19.8 %all-to-all-start = ((bf16[8,24,1280]{2,1,0:T(8,128)(2,1)}), bf16[8,24,1280]{2,1,0:T(8,128)(2,1)S(1)}, u32[]{:S(2)}, u32[]{:S(2)}) async-start(bf16[8,24,1280]{2,1,0:T(8,128)(2,1)} %bitcast.3), calls=%async_computation | async-start | bytes 983040 | tf_op jit(solution)/shard_map/all_to_all | solution.py:484
  (6 other events, 24.4 us)

commit v6 on v5

--- a/solution.py
+++ b/solution.py
@@ -36,31 +36,15 @@
     return lax.ppermute(array, AXES, pairs)
 
 
-def z_even(z, y):
-    return (z ^ 1, y)
-
-
-def z_odd(z, y):
-    return ((((z - 1) % Z) ^ 1) + 1) % Z, y
-
-
-def y_even(z, y):
-    return (z, y ^ 1)
-
-
-def y_odd(z, y):
-    return (z, ((((y - 1) % Y) ^ 1) + 1) % Y)
-
-
-STEPS = (
-    ((z_even, z_odd), (z_odd, z_even)),
-    ((y_even, y_odd), (y_odd, y_even)),
-)
+def partners(core, z, y):
+    if core == 0:
+        return (((z + 1) % Z, y), ((z - 1) % Z, y), ((z + (2 if z % 4 < 2 else -2)) % Z, y))
+    return ((z, (y + 1) % Y), (z, (y - 1) % Y), (z, (y + 2) % Y))
 
 
 def group_of(core, z, y):
     if core == 0:
-        return [(zb, yb) for zb in sorted((z, (z + 4) % Z)) for yb in range(Y)]
+        return [(zb, yb) for zb in (z % 4, z % 4 + 4) for yb in range(Y)]
     return [(zb, y) for zb in range(Z)]
 
 
@@ -73,28 +57,19 @@
 
 
 def row_table():
-    table = np.zeros((CORES, Z, Y, 2, 2, 192), np.int32)
+    table = np.zeros((CORES, Z, Y, 32 * 24), np.int32)
     for core in range(CORES):
-        for chain in range(2):
-            places = [(z, y) for z in range(Z) for y in range(Y)]
-            orders = {place: group_of(core, *place) for place in places}
-            for step in reversed(STEPS[core][chain]):
-                orders = {place: orders[place] + orders[step(*place)] for place in places}
-            for (z, y), order in orders.items():
-                assert len(set(order)) == Z * Y
-                rows = []
-                for number, (zb, yb) in enumerate(order):
-                    first = (16, 8)[number % 2]
-                    cut = range(first) if chain == 0 else range(first, 24)
-                    rows += [(zb * Y + yb) * 48 + row for row in cut]
-                table[core, z, y, 0, chain] = rows[192:]
-                table[core, z, y, 1, chain] = rows[:192]
+        for z in range(Z):
+            for y in range(Y):
+                blocks = [block for place in (*partners(core, z, y), (z, y)) for block in group_of(core, *place)]
+                assert len(set(blocks)) == Z * Y
+                table[core, z, y] = [(zb * Y + yb) * 48 + row for zb, yb in blocks for row in range(24)]
     return table.reshape(CORES * Z * Y, 1, -1)
 
 
-def exchange(array, number, chain):
+def exchange(array, number):
     def move(x, y, z, core):
-        z, y = STEPS[core][chain][number](z, y)
+        z, y = partners(core, z, y)[number]
         return (x, y, z, core)
 
     return permute(array, move)
@@ -301,25 +276,16 @@
 
 def outer_first_kernel(examples, *refs):
     small, operands, (out, count_out, scale_out) = refs[:5], refs[5:9], refs[9:]
-    rows, width = out.shape[0] - TAIL, out.shape[1]
     scale, count = factors_of(examples, *small)
     count_out[...] = count
     scale_out[...] = scale
-    total = outer_rows(0, rows, scale, operands)
-    out[...] = jnp.concatenate([total, *tail_rows(count, TAIL, width)], axis=0).astype(out.dtype)
-
-
-def outer_second_kernel(scale, *refs):
-    operands, out = refs[:4], refs[4]
-    rows = out.shape[0]
-    out[...] = outer_rows(rows, rows, scale[...], operands).astype(out.dtype)
-
-
-def outer_keep_kernel(scale, *refs):
-    operands, outs = refs[:4], refs[4:]
-    rows = outs[0].shape[0]
-    for chain, out in enumerate(outs):
-        out[...] = outer_rows((2 + chain) * rows, rows, scale[...], operands)
+    write_message(0, scale, count, operands, out)
+
+
+def write_message(number, scale, count, operands, out):
+    rows = out.shape[0] - TAIL
+    total = outer_rows(number * rows, rows, scale, operands)
+    out[...] = jnp.concatenate([total, *tail_rows(count, TAIL, out.shape[1])], axis=0).astype(out.dtype)
 
 
 def outer_first(rows, examples, small, operands):
@@ -331,69 +297,39 @@
     return call(lambda *refs: outer_first_kernel(examples, *refs), "outer_first", outs, (*small, *operands))
 
 
-def outer_second(rows, scale, operands):
-    out = array((rows, operands[2].shape[2]), jnp.bfloat16)
-    return call(outer_second_kernel, "outer_second", out, (scale, *operands))
+def outer_next(number, rows, scale, count, operands):
+    out = array((rows + TAIL, operands[2].shape[2]), jnp.bfloat16)
+
+    def kernel(scale, count, *refs):
+        write_message(number, scale[...], count[...], refs[:4], refs[4])
+
+    return call(kernel, "outer_next", out, (scale, count, *operands))
 
 
 def outer_keep(rows, scale, operands):
-    outs = (array((rows, operands[2].shape[2]), jnp.float32),) * 2
-    return call(outer_keep_kernel, "outer_keep", outs, (scale, *operands))
-
-
-def step_first_kernel(count, kept, got, count_out, keep, send):
+    def kernel(scale, *refs):
+        refs[4][...] = outer_rows(3 * rows, rows, scale[...], refs[:4])
+
+    return call(kernel, "outer_keep", array((rows, operands[2].shape[2]), jnp.float32), (scale, *operands))
+
+
+SIDE = 128
+
+
+def step_join_kernel(count, kept, got0, got1, got2, send):
+    rows = kept.shape[0]
+    total, counted = kept[...], count[...]
+    for got in (got0, got1, got2):
+        message = got[...].astype(jnp.float32)
+        total = total + message[:rows]
+        counted = counted + count_in(message[rows:])
+    side = jnp.concatenate(list(tail_rows(counted, 24, SIDE)) * (rows // 24), axis=0)
+    send[...] = jnp.concatenate([total, side], axis=1).astype(send.dtype)
+
+
+def step_join(count, kept, *got):
     rows, width = kept.shape
-    half = rows // 2
-    message = got[...].astype(jnp.float32)
-    total = kept[...] + message[:rows]
-    keep[...] = total[:half]
-    counted = count[...] + count_in(message[rows:])
-    count_out[...] = counted
-    send[...] = jnp.concatenate([total[half:], *tail_rows(counted, TAIL, width)], axis=0).astype(send.dtype)
-
-
-def step_outs(kept, sent, width):
-    return (array(LANES, jnp.float32), array((kept, width), jnp.float32), array((sent, width), jnp.bfloat16))
-
-
-def step_first(count, kept, got):
-    rows, width = kept.shape
-    return call(step_first_kernel, "step_first", step_outs(rows // 2, rows // 2 + TAIL, width), (count, kept, got))
-
-
-def step_second_kernel(kept, got, keep, send):
-    half = kept.shape[0] // 2
-    total = kept[...] + got[...].astype(jnp.float32)
-    keep[...] = total[:half]
-    send[...] = total[half:].astype(send.dtype)
-
-
-def step_second(kept, got):
-    rows, width = kept.shape
-    outs = (array((rows // 2, width), jnp.float32), array((rows // 2, width), jnp.bfloat16))
-    return call(step_second_kernel, "step_second", outs, (kept, got))
-
-
-SIDE = 128
-
-
-def step_join_kernel(count, kept0, kept1, got0, got1, send):
-    rows, width = kept0.shape
-    message = got0[...].astype(jnp.float32)
-    total0 = kept0[...] + message[:rows]
-    total1 = kept1[...] + got1[...].astype(jnp.float32)
-    counted = count[...] + count_in(message[rows:])
-    pieces = []
-    for at in range(0, rows, 24):
-        pieces += [total0[at : at + 16], total1[at : at + 8], total0[at + 16 : at + 24], total1[at + 8 : at + 24]]
-    side = tail_rows(counted, 24, SIDE)
-    side = jnp.concatenate(list(side) * (rows // 12), axis=0)
-    send[...] = jnp.concatenate([jnp.concatenate(pieces, axis=0), side], axis=1).astype(send.dtype)
-
-
-def step_join(count, kept0, kept1, got0, got1):
-    rows, width = kept0.shape
-    return call(step_join_kernel, "step_join", array((2 * rows, width + SIDE), jnp.bfloat16), (count, kept0, kept1, got0, got1))
+    return call(step_join_kernel, "step_join", array((rows, width + SIDE), jnp.bfloat16), (count, kept, *got))
 
 
 def step_last_kernel(examples, ratio, noise, got, out, ratio_next):
@@ -441,7 +377,7 @@
 def per_device(inputs, cotangent, lengths, up_weight, down_weight, clip_ratio, count_noise):
     in_l = permute(inputs, right)
     masked = call(
-        mask_kernel, "mask", array(cotangent.shape, cotangent.dtype), (lengths.reshape(1, -1), cotangent), flops=5 * 10**9
+        mask_kernel, "mask", array(cotangent.shape, cotangent.dtype), (lengths.reshape(1, -1), cotangent)
     )
     co_r = permute(masked, left)
 
@@ -472,15 +408,10 @@
     examples_all = lax.axis_size("dp") * lengths.shape[0]
     operands = (hidden_ours, hidden_theirs, masked_ours, masked_theirs)
     quarter = units // 8
-    send0, count, scale = outer_first(quarter, examples_all, small, operands)
-    send1 = outer_second(quarter, scale, operands)
-    got0, got1 = exchange(send0, 0, 0), exchange(send1, 0, 1)
-    keep0, keep1 = outer_keep(quarter, scale, operands)
-    count, keep0, send0 = step_first(count, keep0, got0)
-    got0 = exchange(send0, 1, 0)
-    keep1, send1 = step_second(keep1, got1)
-    got1 = exchange(send1, 1, 1)
-    send = step_join(count, keep0, keep1, got0, got1)
+    send, count, scale = outer_first(quarter, examples_all, small, operands)
+    got = [exchange(send, 0)]
+    got += [exchange(outer_next(number, quarter, scale, count, operands), number) for number in (1, 2)]
+    send = step_join(count, outer_keep(quarter, scale, operands), *got)
     got = lax.all_to_all(send, AXES, 0, 0, axis_index_groups=GROUPS, tiled=True)
     grad_down, ratio_next = step_last(
         examples_all, ratio, count_noise, got, 4 * quarter // (Z * Y), send.shape[1] - SIDE

time: 89.1 us -> 91.9 us (1.031)
  the two profiles are of different devices: /device:TPU:6 before, /device:TPU:34 now
where the time goes in v6:
time: 91.9 us; the launch traced here: 91.6 us
  waiting for transfers between devices  36.9 us (40%)
  starting transfers between devices  28.7 us (31%)
  Pallas kernels  20.1 us (22%)
  local copies, waits for them, and re-layouts  4.55 us (5%)
  between operations  1.42 us (2%)
    ppermute x22, waiting for transfers between devices, permute(): return lax.ppermute(array, AXES, pairs)  25.5 us
    pallas_call x13, Pallas kernels, call(): pl.pallas_call(kernel, out_shape=outs, in_specs=specs or [VMEM] * len(arg...  20.1 us
    ppermute x22, starting transfers between devices, permute(): return lax.ppermute(array, AXES, pairs)  18.4 us
    all_to_all x1, waiting for transfers between devices, per_device(): got = lax.all_to_all(send, AXES, 0, 0, axis_index_groups=GROUPS, tiled=True)  11.4 us
    all_to_all x1, starting transfers between devices, per_device(): got = lax.all_to_all(send, AXES, 0, 0, axis_index_groups=GROUPS, tiled=True)  10.3 us
    unnamed x12, local copies, waits for them, and re-layouts  4.55 us
  transfers between devices with their start and end apart: 23, of which 13 were waited for; matrix products, arithmetic and copies ran while one was open for 0% of the time, Pallas kernels for 13%

profile of v6, /device:TPU:34, one launch (start us, length us, event | category | flops | bytes accessed | tf_op | source)
XLA Modules:
  0.0 91.6 jit_solution(8531656906782599710)
XLA Ops:
  3.0 1.5 %collective-permute-start.7 = (bf16[2,64,1152]{2,1,0:T(8,128)(2,1)S(1)}, bf16[2,64,1152]{2,1,0:T(8,128)(2,1)S(1)}, u32[]{:S(2)}, u32[]{:S(2)}) collective-permute-start(bf16[2,64,1152]{2,1,0:T(8,128)(2,1)S(1)} %mask.1.co_a.refs_4_), channel_id=1, source_target_pairs={{0,4},{1,5},{2,6},{3,7},{4,2},{5,3},{6,0},{7,1},{8,12},{9,13},{10,... | collective-permute-start | bytes 884744 | tf_op jit(solution)/shard_map/ppermute | solution.py:36
  4.5 1.5 %collective-permute-start.2 = (bf16[2,64,1152]{2,1,0:T(8,128)(2,1)}, bf16[2,64,1152]{2,1,0:T(8,128)(2,1)S(1)}, u32[]{:S(2)}, u32[]{:S(2)}) collective-permute-start(bf16[2,64,1152]{2,1,0:T(8,128)(2,1)} %refs_0_.1), channel_id=1, source_target_pairs={{0,4},{1,5},{2,6},{3,7},{4,2},{5,3},{6,0},{7,1},{8,12},{9,13},{10,... | collective-permute-start | bytes 884744 | tf_op jit(solution)/shard_map/ppermute | solution.py:36
  6.5 2.0 %copy-done = bf16[1152,1536]{1,0:T(8,128)(2,1)S(1)} copy-done((bf16[1152,1536]{1,0:T(8,128)(2,1)S(1)}, bf16[1152,1536]{1,0:T(8,128)(2,1)}, u32[]{:S(2)}) %copy-start) | copy-done | bytes 3538968
  9.4 2.9 %select_up.1.up.refs_8_ = bf16[1152,768]{1,0:T(8,128)(2,1)S(1)} custom-call(s32[64,1,768]{2,1,0:T(1,128)S(1)} %copy-done.3, bf16[1152,1536]{1,0:T(8,128)(2,1)S(1)} %copy-done), custom_call_target="tpu_custom_call" | custom-call | tf_op jit(solution)/shard_map/select_up/pallas_call | solution.py:96
  12.4 3.5 %select_down.1.down.refs_9_ = bf16[768,1152]{1,0:T(8,128)(2,1)S(1)} custom-call(s32[64,1,768]{2,1,0:T(1,128)S(1)} %copy-done.3, bf16[1536,1152]{1,0:T(8,128)(2,1)S(1)} %copy-done.1), custom_call_target="tpu_custom_call" | custom-call | tf_op jit(solution)/shard_map/select_down/pallas_call | solution.py:96
  16.0 1.4 %collective-permute-done.refs_0_ = f32[1,1]{1,0:T(1,128)} collective-permute-done((f32[1,1]{1,0:T(1,128)}, f32[1,1]{1,0:T(1,128)}, u32[]{:S(2)}, u32[]{:S(2)}) %collective-permute-start) | collective-permute-done | bytes 36 | tf_op jit(solution)/shard_map/ppermute | solution.py:36
  19.4 3.1 %collective-permute-start.13 = (bf16[2,64,1152]{2,1,0:T(8,128)(2,1)S(1)}, bf16[2,64,1152]{2,1,0:T(8,128)(2,1)S(1)}, u32[]{:S(2)}, u32[]{:S(2)}) collective-permute-start(bf16[2,64,1152]{2,1,0:T(8,128)(2,1)S(1)} %collective-permute-done.9.refs_6_), channel_id=1, source_target_pairs={{0,6},{1,7},{2,4},{3,5},{4,0},{5,1},{6,2},{7,3},{8,14},{9,15},{10,... | collective-permute-start | bytes 884744 | tf_op jit(solution)/shard_map/ppermute | solution.py:36
  22.5 1.4 %early_pass.1 = (bf16[256,768]{1,0:T(8,128)(2,1)S(1)}, bf16[256,768]{1,0:T(8,128)(2,1)S(1)}) custom-call(bf16[2,64,1152]{2,1,0:T(8,128)(2,1)S(1)} %copy-done.2, bf16[2,64,1152]{2,1,0:T(8,128)(2,1)S(1)} %collective-permute-done.1.in_b.refs_1_, bf16[2,64,1152]{2,1,0:T(8,128)(2,1)S(1)} %mask.1.co_a.refs_4_, ...), custom_call_target="tpu_custom_call" | custom-call | tf_op jit(solution)/shard_map/early_pass/pallas_call | solution.py:96
  24.0 3.6 %theirs_pass.1 = (bf16[2,768,256]{2,1,0:T(8,128)(2,1)S(1)}, bf16[2,256,1152]{2,1,0:T(8,128)(2,1)S(1)}, f32[2,8,128]{2,1,0:T(8,128)S(1)}) custom-call(bf16[2,64,1152]{2,1,0:T(8,128)(2,1)S(1)} %collective-permute-done.2.refs_0_, bf16[2,64,1152]{2,1,0:T(8,128)(2,1)S(1)} %collective-permute-done.4.refs_1_, ...), custom_call_target="tpu_custom_call" | custom-call | tf_op jit(solution)/shard_map/theirs_pass/pallas_call | solution.py:96
  27.6 1.6 %collective-permute-done.13.refs_6_ = bf16[2,64,1152]{2,1,0:T(8,128)(2,1)S(1)} collective-permute-done((bf16[2,64,1152]{2,1,0:T(8,128)(2,1)S(1)}, bf16[2,64,1152]{2,1,0:T(8,128)(2,1)S(1)}, u32[]{:S(2)}, u32[]{:S(2)}) %collective-permute-start.13) | collective-permute-done | bytes 294944 | tf_op jit(solution)/shard_map/ppermute | solution.py:36
  29.2 2.2 %collective-permute-done.3.refs_2_ = bf16[2,64,1152]{2,1,0:T(8,128)(2,1)S(1)} collective-permute-done((bf16[2,64,1152]{2,1,0:T(8,128)(2,1)S(1)}, bf16[2,64,1152]{2,1,0:T(8,128)(2,1)S(1)}, u32[]{:S(2)}, u32[]{:S(2)}) %collective-permute-start.3) | collective-permute-done | bytes 294944 | tf_op jit(solution)/shard_map/ppermute | solution.py:36
  31.4 1.6 %collective-permute-done.12.refs_3_ = bf16[2,64,1152]{2,1,0:T(8,128)(2,1)S(1)} collective-permute-done((bf16[2,64,1152]{2,1,0:T(8,128)(2,1)S(1)}, bf16[2,64,1152]{2,1,0:T(8,128)(2,1)S(1)}, u32[]{:S(2)}, u32[]{:S(2)}) %collective-permute-start.12) | collective-permute-done | bytes 294944 | tf_op jit(solution)/shard_map/ppermute | solution.py:36
  33.0 2.5 %ours_pass.1 = (bf16[2,768,256]{2,1,0:T(8,128)(2,1)S(1)}, bf16[2,256,1152]{2,1,0:T(8,128)(2,1)S(1)}, f32[4,8,128]{2,1,0:T(8,128)S(1)}) custom-call(bf16[2,64,1152]{2,1,0:T(8,128)(2,1)S(1)} %copy-done.2, bf16[2,64,1152]{2,1,0:T(8,128)(2,1)S(1)} %collective-permute-done.1.in_b.refs_1_, bf16[2,64,1152]{2,1,0:T(8,128)(2,1)S(1)} %collective-permute-done.3.refs_2_, ...), custom_call_target="tpu_custom_call" | custom-call | tf_op jit(solution)/shard_map/ours_pass/pallas_call | solution.py:96
  36.8 2.1 %collective-permute-start.16 = (f32[4,8,128]{2,1,0:T(8,128)S(1)}, f32[4,8,128]{2,1,0:T(8,128)S(1)}, u32[]{:S(2)}, u32[]{:S(2)}) collective-permute-start(f32[4,8,128]{2,1,0:T(8,128)S(1)} %chip_squares.1.refs_1_), channel_id=1, source_target_pairs={{0,2},{1,3},{2,0},{3,1},{4,6},{5,7},{6,4},{7,5},{8,10},{9,11},{10,... | collective-permute-start | bytes 49160 | tf_op jit(solution)/shard_map/ppermute | solution.py:36
  38.8 1.9 %collective-permute-start.17 = (f32[4,8,128]{2,1,0:T(8,128)S(1)}, f32[4,8,128]{2,1,0:T(8,128)S(1)}, u32[]{:S(2)}, u32[]{:S(2)}) collective-permute-start(f32[4,8,128]{2,1,0:T(8,128)S(1)} %chip_squares.1.refs_1_), channel_id=1, source_target_pairs={{0,4},{1,5},{2,6},{3,7},{4,2},{5,3},{6,0},{7,1},{8,12},{9,13},{10,... | collective-permute-start | bytes 49160 | tf_op jit(solution)/shard_map/ppermute | solution.py:36
  42.6 1.9 %collective-permute-done.18.refs_4_ = f32[4,8,128]{2,1,0:T(8,128)S(1)} collective-permute-done((f32[4,8,128]{2,1,0:T(8,128)S(1)}, f32[4,8,128]{2,1,0:T(8,128)S(1)}, u32[]{:S(2)}, u32[]{:S(2)}) %collective-permute-start.18) | collective-permute-done | bytes 16416 | tf_op jit(solution)/shard_map/ppermute | solution.py:36
  44.5 1.3 %outer_first.1 = (bf16[208,1152]{1,0:T(8,128)(2,1)S(1)}, f32[8,128]{1,0:T(8,128)S(1)}, f32[4,8,128]{2,1,0:T(8,128)S(1)}) custom-call(f32[1,1]{1,0:T(1,128)} %collective-permute-done.refs_0_, f32[4,8,128]{2,1,0:T(8,128)S(1)} %chip_squares.1.refs_1_, f32[4,8,128]{2,1,0:T(8,128)S(1)} %collective-permute-done.16.refs_2_, ...), custom_call_target="tpu_custom_call" | custom-call | tf_op jit(solution)/shard_map/outer_first/pallas_call | solution.py:96
  47.3 3.4 %collective-permute-start.21 = (bf16[208,1152]{1,0:T(8,128)(2,1)S(1)}, bf16[208,1152]{1,0:T(8,128)(2,1)S(1)}, u32[]{:S(2)}, u32[]{:S(2)}) collective-permute-start(bf16[208,1152]{1,0:T(8,128)(2,1)S(1)} %outer_next.3), channel_id=1, source_target_pairs={{0,64},{1,17},{2,66},{3,19},{4,68},{5,21},{6,70},{7,23},{8,72},{9,... | collective-permute-start | bytes 1437704 | tf_op jit(solution)/shard_map/ppermute | solution.py:36
  50.8 1.9 %collective-permute-start.19 = (bf16[208,1152]{1,0:T(8,128)(2,1)S(1)}, bf16[208,1152]{1,0:T(8,128)(2,1)S(1)}, u32[]{:S(2)}, u32[]{:S(2)}) collective-permute-start(bf16[208,1152]{1,0:T(8,128)(2,1)S(1)} %get-tuple-element.43), channel_id=1, source_target_pairs={{0,32},{1,9},{2,34},{3,11},{4,36},{5,13},{6,38},{7,15},{8,40},{9,1... | collective-permute-start | bytes 1437704 | tf_op jit(solution)/shard_map/ppermute | solution.py:36
  53.5 8.2 %collective-permute-done.21.got2 = bf16[208,1152]{1,0:T(8,128)(2,1)S(1)} collective-permute-done((bf16[208,1152]{1,0:T(8,128)(2,1)S(1)}, bf16[208,1152]{1,0:T(8,128)(2,1)S(1)}, u32[]{:S(2)}, u32[]{:S(2)}) %collective-permute-start.21) | collective-permute-done | bytes 479264 | tf_op jit(solution)/shard_map/ppermute | solution.py:36
  61.6 4.7 %collective-permute-done.20.got1 = bf16[208,1152]{1,0:T(8,128)(2,1)S(1)} collective-permute-done((bf16[208,1152]{1,0:T(8,128)(2,1)S(1)}, bf16[208,1152]{1,0:T(8,128)(2,1)S(1)}, u32[]{:S(2)}, u32[]{:S(2)}) %collective-permute-start.20) | collective-permute-done | bytes 479264 | tf_op jit(solution)/shard_map/ppermute | solution.py:36
  68.0 10.3 %all-to-all-start = ((bf16[8,24,1280]{2,1,0:T(8,128)(2,1)}), bf16[8,24,1280]{2,1,0:T(8,128)(2,1)S(1)}, u32[]{:S(2)}, u32[]{:S(2)}) async-start(bf16[8,24,1280]{2,1,0:T(8,128)(2,1)} %bitcast.3), calls=%async_computation | async-start | bytes 983040 | tf_op jit(solution)/shard_map/all_to_all | solution.py:415
  78.9 11.4 %all-to-all-done = bf16[8,24,1280]{2,1,0:T(8,128)(2,1)S(1)} async-done(((bf16[8,24,1280]{2,1,0:T(8,128)(2,1)}), bf16[8,24,1280]{2,1,0:T(8,128)(2,1)S(1)}, u32[]{:S(2)}, u32[]{:S(2)}) %all-to-all-start) | async-done | bytes 491552 | tf_op jit(solution)/shard_map/all_to_all | solution.py:415
  90.3 1.3 %step_last.1 = (f32[24,1152]{1,0:T(8,128)}, f32[1,1]{1,0:T(1,128)}) custom-call(f32[1,1]{1,0:T(1,128)} %collective-permute-done.refs_0_, f32[1,1]{1,0:T(1,128)} %bitcast.6.refs_1_, bf16[192,1280]{1,0:T(8,128)(2,1)S(1)} %bitcast.7), custom_call_target="tpu_custom_call" | custom-call | tf_op jit(solution)/shard_map/step_last/pallas_call | solution.py:96
  (47 shorter events, 13.0 us)
Async XLA Ops:
  2.4 15.2 %collective-permute-start.9 = (bf16[2,64,1152]{2,1,0:T(8,128)(2,1)S(1)}, bf16[2,64,1152]{2,1,0:T(8,128)(2,1)S(1)}, u32[]{:S(2)}, u32[]{:S(2)}) collective-permute-start(bf16[2,64,1152]{2,1,0:T(8,128)(2,1)S(1)} %mask.1.co_a.refs_4_), channel_id=1, source_target_pairs={{0,6},{1,7},{2,4},{3,5},{4,0},{5,1},{6,2},{7,3},{8,14},{9,15},{10,... | collective-permute-start | bytes 884744 | tf_op jit(solution)/shard_map/ppermute | solution.py:36
  3.0 14.9 %collective-permute-start.7 = (bf16[2,64,1152]{2,1,0:T(8,128)(2,1)S(1)}, bf16[2,64,1152]{2,1,0:T(8,128)(2,1)S(1)}, u32[]{:S(2)}, u32[]{:S(2)}) collective-permute-start(bf16[2,64,1152]{2,1,0:T(8,128)(2,1)S(1)} %mask.1.co_a.refs_4_), channel_id=1, source_target_pairs={{0,4},{1,5},{2,6},{3,7},{4,2},{5,3},{6,0},{7,1},{8,12},{9,13},{10,... | collective-permute-start | bytes 884744 | tf_op jit(solution)/shard_map/ppermute | solution.py:36
  4.5 14.3 %collective-permute-start.2 = (bf16[2,64,1152]{2,1,0:T(8,128)(2,1)}, bf16[2,64,1152]{2,1,0:T(8,128)(2,1)S(1)}, u32[]{:S(2)}, u32[]{:S(2)}) collective-permute-start(bf16[2,64,1152]{2,1,0:T(8,128)(2,1)} %refs_0_.1), channel_id=1, source_target_pairs={{0,4},{1,5},{2,6},{3,7},{4,2},{5,3},{6,0},{7,1},{8,12},{9,13},{10,... | collective-permute-start | bytes 884744 | tf_op jit(solution)/shard_map/ppermute | solution.py:36
  6.0 12.8 %collective-permute-start.5 = (bf16[2,64,1152]{2,1,0:T(8,128)(2,1)}, bf16[2,64,1152]{2,1,0:T(8,128)(2,1)S(1)}, u32[]{:S(2)}, u32[]{:S(2)}) collective-permute-start(bf16[2,64,1152]{2,1,0:T(8,128)(2,1)} %refs_0_.1), channel_id=1, source_target_pairs={{0,6},{1,7},{2,4},{3,5},{4,0},{5,1},{6,2},{7,3},{8,14},{9,15},{10,... | collective-permute-start | bytes 884744 | tf_op jit(solution)/shard_map/ppermute | solution.py:36
  12.4 5.2 %copy-start.2 = (bf16[2,64,1152]{2,1,0:T(8,128)(2,1)S(1)}, bf16[2,64,1152]{2,1,0:T(8,128)(2,1)}, u32[]{:S(2)}) copy-start(bf16[2,64,1152]{2,1,0:T(8,128)(2,1)} %refs_0_.1) | copy-start | bytes 884740
  15.9 1.5 %collective-permute-start = (f32[1,1]{1,0:T(1,128)}, f32[1,1]{1,0:T(1,128)}, u32[]{:S(2)}, u32[]{:S(2)}) collective-permute-start(f32[1,1]{1,0:T(1,128)} %bitcast), channel_id=1, source_target_pairs={{0,1},{1,0},{2,3},{3,2},{4,5},{5,4},{6,7},{7,6},{8,9},{9,8},{10,11... | collective-permute-start | bytes 20 | tf_op jit(solution)/shard_map/ppermute | solution.py:36
  17.4 1.9 %collective-permute-start.11 = (bf16[2,64,1152]{2,1,0:T(8,128)(2,1)S(1)}, bf16[2,64,1152]{2,1,0:T(8,128)(2,1)S(1)}, u32[]{:S(2)}, u32[]{:S(2)}) collective-permute-start(bf16[2,64,1152]{2,1,0:T(8,128)(2,1)S(1)} %mask.1.co_a.refs_4_), channel_id=1, source_target_pairs={{0,1},{1,0},{2,3},{3,2},{4,5},{5,4},{6,7},{7,6},{8,9},{9,8},{10,11... | collective-permute-start | bytes 884744 | tf_op jit(solution)/shard_map/ppermute | solution.py:36
  17.6 1.8 %collective-permute-start.1 = (bf16[2,64,1152]{2,1,0:T(8,128)(2,1)S(1)}, bf16[2,64,1152]{2,1,0:T(8,128)(2,1)S(1)}, u32[]{:S(2)}, u32[]{:S(2)}) collective-permute-start(bf16[2,64,1152]{2,1,0:T(8,128)(2,1)S(1)} %copy-done.2), channel_id=1, source_target_pairs={{0,1},{1,0},{2,3},{3,2},{4,5},{5,4},{6,7},{7,6},{8,9},{9,8},{10,11... | collective-permute-start | bytes 884744 | tf_op jit(solution)/shard_map/ppermute | solution.py:36
  17.9 4.6 %collective-permute-start.10 = (bf16[2,64,1152]{2,1,0:T(8,128)(2,1)S(1)}, bf16[2,64,1152]{2,1,0:T(8,128)(2,1)S(1)}, u32[]{:S(2)}, u32[]{:S(2)}) collective-permute-start(bf16[2,64,1152]{2,1,0:T(8,128)(2,1)S(1)} %collective-permute-done.9.refs_6_), channel_id=1, source_target_pairs={{0,1},{1,0},{2,3},{3,2},{4,5},{5,4},{6,7},{7,6},{8,9},{9,8},{10,11... | collective-permute-start | bytes 884744 | tf_op jit(solution)/shard_map/ppermute | solution.py:36
  18.8 5.1 %collective-permute-start.8 = (bf16[2,64,1152]{2,1,0:T(8,128)(2,1)S(1)}, bf16[2,64,1152]{2,1,0:T(8,128)(2,1)S(1)}, u32[]{:S(2)}, u32[]{:S(2)}) collective-permute-start(bf16[2,64,1152]{2,1,0:T(8,128)(2,1)S(1)} %collective-permute-done.7.refs_4_), channel_id=1, source_target_pairs={{0,1},{1,0},{2,3},{3,2},{4,5},{5,4},{6,7},{7,6},{8,9},{9,8},{10,11... | collective-permute-start | bytes 884744 | tf_op jit(solution)/shard_map/ppermute | solution.py:36
  18.8 5.1 %collective-permute-start.4 = (bf16[2,64,1152]{2,1,0:T(8,128)(2,1)S(1)}, bf16[2,64,1152]{2,1,0:T(8,128)(2,1)S(1)}, u32[]{:S(2)}, u32[]{:S(2)}) collective-permute-start(bf16[2,64,1152]{2,1,0:T(8,128)(2,1)S(1)} %collective-permute-done.2.refs_0_), channel_id=1, source_target_pairs={{0,1},{1,0},{2,3},{3,2},{4,5},{5,4},{6,7},{7,6},{8,9},{9,8},{10,11... | collective-permute-start | bytes 884744 | tf_op jit(solution)/shard_map/ppermute | solution.py:36
  19.3 4.6 %collective-permute-start.6 = (bf16[2,64,1152]{2,1,0:T(8,128)(2,1)S(1)}, bf16[2,64,1152]{2,1,0:T(8,128)(2,1)S(1)}, u32[]{:S(2)}, u32[]{:S(2)}) collective-permute-start(bf16[2,64,1152]{2,1,0:T(8,128)(2,1)S(1)} %collective-permute-done.5.refs_2_), channel_id=1, source_target_pairs={{0,1},{1,0},{2,3},{3,2},{4,5},{5,4},{6,7},{7,6},{8,9},{9,8},{10,11... | collective-permute-start | bytes 884744 | tf_op jit(solution)/shard_map/ppermute | solution.py:36
  19.4 9.8 %collective-permute-start.13 = (bf16[2,64,1152]{2,1,0:T(8,128)(2,1)S(1)}, bf16[2,64,1152]{2,1,0:T(8,128)(2,1)S(1)}, u32[]{:S(2)}, u32[]{:S(2)}) collective-permute-start(bf16[2,64,1152]{2,1,0:T(8,128)(2,1)S(1)} %collective-permute-done.9.refs_6_), channel_id=1, source_target_pairs={{0,6},{1,7},{2,4},{3,5},{4,0},{5,1},{6,2},{7,3},{8,14},{9,15},{10,... | collective-permute-start | bytes 884744 | tf_op jit(solution)/shard_map/ppermute | solution.py:36
  22.5 8.9 %collective-permute-start.3 = (bf16[2,64,1152]{2,1,0:T(8,128)(2,1)S(1)}, bf16[2,64,1152]{2,1,0:T(8,128)(2,1)S(1)}, u32[]{:S(2)}, u32[]{:S(2)}) collective-permute-start(bf16[2,64,1152]{2,1,0:T(8,128)(2,1)S(1)} %collective-permute-done.2.refs_0_), channel_id=1, source_target_pairs={{0,4},{1,5},{2,6},{3,7},{4,2},{5,3},{6,0},{7,1},{8,12},{9,13},{10,... | collective-permute-start | bytes 884744 | tf_op jit(solution)/shard_map/ppermute | solution.py:36
  29.2 2.2 %collective-permute-start.14 = (bf16[2,64,1152]{2,1,0:T(8,128)(2,1)S(1)}, bf16[2,64,1152]{2,1,0:T(8,128)(2,1)S(1)}, u32[]{:S(2)}, u32[]{:S(2)}) collective-permute-start(bf16[2,64,1152]{2,1,0:T(8,128)(2,1)S(1)} %collective-permute-done.13.refs_6_), channel_id=1, source_target_pairs={{0,1},{1,0},{2,3},{3,2},{4,5},{5,4},{6,7},{7,6},{8,9},{9,8},{10,11... | collective-permute-start | bytes 884744 | tf_op jit(solution)/shard_map/ppermute | solution.py:36
  31.4 1.6 %collective-permute-start.12 = (bf16[2,64,1152]{2,1,0:T(8,128)(2,1)S(1)}, bf16[2,64,1152]{2,1,0:T(8,128)(2,1)S(1)}, u32[]{:S(2)}, u32[]{:S(2)}) collective-permute-start(bf16[2,64,1152]{2,1,0:T(8,128)(2,1)S(1)} %collective-permute-done.3.refs_2_), channel_id=1, source_target_pairs={{0,1},{1,0},{2,3},{3,2},{4,5},{5,4},{6,7},{7,6},{8,9},{9,8},{10,11... | collective-permute-start | bytes 884744 | tf_op jit(solution)/shard_map/ppermute | solution.py:36
  35.5 1.3 %collective-permute-start.15 = (f32[4,8,128]{2,1,0:T(8,128)S(1)}, f32[4,8,128]{2,1,0:T(8,128)S(1)}, u32[]{:S(2)}, u32[]{:S(2)}) collective-permute-start(f32[4,8,128]{2,1,0:T(8,128)S(1)} %get-tuple-element.36.left), channel_id=1, source_target_pairs={{0,1},{1,0},{2,3},{3,2},{4,5},{5,4},{6,7},{7,6},{8,9},{9,8},{10,11... | collective-permute-start | bytes 49160 | tf_op jit(solution)/shard_map/ppermute | solution.py:36
  36.8 5.2 %collective-permute-start.16 = (f32[4,8,128]{2,1,0:T(8,128)S(1)}, f32[4,8,128]{2,1,0:T(8,128)S(1)}, u32[]{:S(2)}, u32[]{:S(2)}) collective-permute-start(f32[4,8,128]{2,1,0:T(8,128)S(1)} %chip_squares.1.refs_1_), channel_id=1, source_target_pairs={{0,2},{1,3},{2,0},{3,1},{4,6},{5,7},{6,4},{7,5},{8,10},{9,11},{10,... | collective-permute-start | bytes 49160 | tf_op jit(solution)/shard_map/ppermute | solution.py:36
  38.8 3.7 %collective-permute-start.17 = (f32[4,8,128]{2,1,0:T(8,128)S(1)}, f32[4,8,128]{2,1,0:T(8,128)S(1)}, u32[]{:S(2)}, u32[]{:S(2)}) collective-permute-start(f32[4,8,128]{2,1,0:T(8,128)S(1)} %chip_squares.1.refs_1_), channel_id=1, source_target_pairs={{0,4},{1,5},{2,6},{3,7},{4,2},{5,3},{6,0},{7,1},{8,12},{9,13},{10,... | collective-permute-start | bytes 49160 | tf_op jit(solution)/shard_map/ppermute | solution.py:36
  40.8 3.7 %collective-permute-start.18 = (f32[4,8,128]{2,1,0:T(8,128)S(1)}, f32[4,8,128]{2,1,0:T(8,128)S(1)}, u32[]{:S(2)}, u32[]{:S(2)}) collective-permute-start(f32[4,8,128]{2,1,0:T(8,128)S(1)} %chip_squares.1.refs_1_), channel_id=1, source_target_pairs={{0,6},{1,7},{2,4},{3,5},{4,0},{5,1},{6,2},{7,3},{8,14},{9,15},{10,... | collective-permute-start | bytes 49160 | tf_op jit(solution)/shard_map/ppermute | solution.py:36
  47.3 14.3 %collective-permute-start.21 = (bf16[208,1152]{1,0:T(8,128)(2,1)S(1)}, bf16[208,1152]{1,0:T(8,128)(2,1)S(1)}, u32[]{:S(2)}, u32[]{:S(2)}) collective-permute-start(bf16[208,1152]{1,0:T(8,128)(2,1)S(1)} %outer_next.3), channel_id=1, source_target_pairs={{0,64},{1,17},{2,66},{3,19},{4,68},{5,21},{6,70},{7,23},{8,72},{9,... | collective-permute-start | bytes 1437704 | tf_op jit(solution)/shard_map/ppermute | solution.py:36
  50.7 15.6 %collective-permute-start.20 = (bf16[208,1152]{1,0:T(8,128)(2,1)S(1)}, bf16[208,1152]{1,0:T(8,128)(2,1)S(1)}, u32[]{:S(2)}, u32[]{:S(2)}) collective-permute-start(bf16[208,1152]{1,0:T(8,128)(2,1)S(1)} %outer_next.2), channel_id=1, source_target_pairs={{0,224},{1,25},{2,226},{3,27},{4,228},{5,29},{6,230},{7,31},{8,232... | collective-permute-start | bytes 1437704 | tf_op jit(solution)/shard_map/ppermute | solution.py:36
  50.8 16.0 %collective-permute-start.19 = (bf16[208,1152]{1,0:T(8,128)(2,1)S(1)}, bf16[208,1152]{1,0:T(8,128)(2,1)S(1)}, u32[]{:S(2)}, u32[]{:S(2)}) collective-permute-start(bf16[208,1152]{1,0:T(8,128)(2,1)S(1)} %get-tuple-element.43), channel_id=1, source_target_pairs={{0,32},{1,9},{2,34},{3,11},{4,36},{5,13},{6,38},{7,15},{8,40},{9,1... | collective-permute-start | bytes 1437704 | tf_op jit(solution)/shard_map/ppermute | solution.py:36
  68.0 22.3 %all-to-all-start = ((bf16[8,24,1280]{2,1,0:T(8,128)(2,1)}), bf16[8,24,1280]{2,1,0:T(8,128)(2,1)S(1)}, u32[]{:S(2)}, u32[]{:S(2)}) async-start(bf16[8,24,1280]{2,1,0:T(8,128)(2,1)} %bitcast.3), calls=%async_computation | async-start | bytes 983040 | tf_op jit(solution)/shard_map/all_to_all | solution.py:415
  (5 other events, 7.5 us)

commit v7 on v5

--- a/solution.py
+++ b/solution.py
@@ -441,7 +441,7 @@
 def per_device(inputs, cotangent, lengths, up_weight, down_weight, clip_ratio, count_noise):
     in_l = permute(inputs, right)
     masked = call(
-        mask_kernel, "mask", array(cotangent.shape, cotangent.dtype), (lengths.reshape(1, -1), cotangent), flops=5 * 10**9
+        mask_kernel, "mask", array(cotangent.shape, cotangent.dtype), (lengths.reshape(1, -1), cotangent)
     )
     co_r = permute(masked, left)
 

time: 89.1 us -> 89.7 us (level)
  local copies, waits for them, and re-layouts: 1.63 us -> 4.55 us
  waiting for transfers between devices: 29.8 us -> 28.4 us
  starting transfers between devices: 35.9 us -> 34.8 us
    unnamed x12, local copies, waits for them, and re-layouts: 1.63 us -> 4.55 us
    ppermute x23, waiting for transfers between devices: 18.3 us -> 16.5 us  [permute(): return lax.ppermute(array, AXES, pairs)]
    ppermute x23, starting transfers between devices: 28.2 us -> 27.2 us  [permute(): return lax.ppermute(array, AXES, pairs)]
  transfers between devices with their start and end apart: 24 -> 24, of which waited for: 12 -> 13; matrix products, arithmetic and copies ran while one was open for 0% -> 0% of each run, Pallas kernels for 15% -> 15%
where the time goes in v7:
time: 89.7 us; the launch traced here: 89.4 us
  starting transfers between devices  34.8 us (39%)
  waiting for transfers between devices  28.4 us (32%)
  Pallas kernels  20.1 us (22%)
  local copies, waits for them, and re-layouts  4.55 us (5%)
  between operations  1.45 us (2%)
    ppermute x23, starting transfers between devices, permute(): return lax.ppermute(array, AXES, pairs)  27.2 us
    pallas_call x14, Pallas kernels, call(): pl.pallas_call(kernel, out_shape=outs, in_specs=specs or [VMEM] * len(arg...  20.1 us
    ppermute x23, waiting for transfers between devices, permute(): return lax.ppermute(array, AXES, pairs)  16.5 us
    all_to_all x1, waiting for transfers between devices, per_device(): got = lax.all_to_all(send, AXES, 0, 0, axis_index_groups=GROUPS, tiled=True)  11.9 us
    all_to_all x1, starting transfers between devices, per_device(): got = lax.all_to_all(send, AXES, 0, 0, axis_index_groups=GROUPS, tiled=True)  7.61 us
    unnamed x12, local copies, waits for them, and re-layouts  4.55 us
  transfers between devices with their start and end apart: 24, of which 13 were waited for; matrix products, arithmetic and copies ran while one was open for 0% of the time, Pallas kernels for 15%

profile of v7, /device:TPU:6, one launch (start us, length us, event | category | flops | bytes accessed | tf_op | source)
XLA Modules:
  0.0 89.4 jit_solution(3976529111390792237)
XLA Ops:
  3.3 2.4 %collective-permute-start.7 = (bf16[2,64,1152]{2,1,0:T(8,128)(2,1)S(1)}, bf16[2,64,1152]{2,1,0:T(8,128)(2,1)S(1)}, u32[]{:S(2)}, u32[]{:S(2)}) collective-permute-start(bf16[2,64,1152]{2,1,0:T(8,128)(2,1)S(1)} %mask.1.co_a.refs_4_), channel_id=1, source_target_pairs={{0,4},{1,5},{2,6},{3,7},{4,2},{5,3},{6,0},{7,1},{8,12},{9,13},{10,... | collective-permute-start | bytes 884744 | tf_op jit(solution)/shard_map/ppermute | solution.py:36
  7.7 2.0 %copy-done = bf16[1152,1536]{1,0:T(8,128)(2,1)S(1)} copy-done((bf16[1152,1536]{1,0:T(8,128)(2,1)S(1)}, bf16[1152,1536]{1,0:T(8,128)(2,1)}, u32[]{:S(2)}) %copy-start) | copy-done | bytes 3538968
  10.7 2.9 %select_up.1.up.refs_8_ = bf16[1152,768]{1,0:T(8,128)(2,1)S(1)} custom-call(s32[64,1,768]{2,1,0:T(1,128)S(1)} %copy-done.3, bf16[1152,1536]{1,0:T(8,128)(2,1)S(1)} %copy-done), custom_call_target="tpu_custom_call" | custom-call | tf_op jit(solution)/shard_map/select_up/pallas_call | solution.py:121
  13.6 3.5 %select_down.1.down.refs_9_ = bf16[768,1152]{1,0:T(8,128)(2,1)S(1)} custom-call(s32[64,1,768]{2,1,0:T(1,128)S(1)} %copy-done.3, bf16[1536,1152]{1,0:T(8,128)(2,1)S(1)} %copy-done.1), custom_call_target="tpu_custom_call" | custom-call | tf_op jit(solution)/shard_map/select_down/pallas_call | solution.py:121
  17.2 1.2 %collective-permute-done.refs_0_ = f32[1,1]{1,0:T(1,128)} collective-permute-done((f32[1,1]{1,0:T(1,128)}, f32[1,1]{1,0:T(1,128)}, u32[]{:S(2)}, u32[]{:S(2)}) %collective-permute-start) | collective-permute-done | bytes 36 | tf_op jit(solution)/shard_map/ppermute | solution.py:36
  20.9 2.8 %collective-permute-start.3 = (bf16[2,64,1152]{2,1,0:T(8,128)(2,1)S(1)}, bf16[2,64,1152]{2,1,0:T(8,128)(2,1)S(1)}, u32[]{:S(2)}, u32[]{:S(2)}) collective-permute-start(bf16[2,64,1152]{2,1,0:T(8,128)(2,1)S(1)} %collective-permute-done.2.refs_0_), channel_id=1, source_target_pairs={{0,4},{1,5},{2,6},{3,7},{4,2},{5,3},{6,0},{7,1},{8,12},{9,13},{10,... | collective-permute-start | bytes 884744 | tf_op jit(solution)/shard_map/ppermute | solution.py:36
  23.7 1.4 %early_pass.1 = (bf16[256,768]{1,0:T(8,128)(2,1)S(1)}, bf16[256,768]{1,0:T(8,128)(2,1)S(1)}) custom-call(bf16[2,64,1152]{2,1,0:T(8,128)(2,1)S(1)} %copy-done.2, bf16[2,64,1152]{2,1,0:T(8,128)(2,1)S(1)} %collective-permute-done.1.in_b.refs_1_, bf16[2,64,1152]{2,1,0:T(8,128)(2,1)S(1)} %mask.1.co_a.refs_4_, ...), custom_call_target="tpu_custom_call" | custom-call | tf_op jit(solution)/shard_map/early_pass/pallas_call | solution.py:121
  25.1 3.6 %theirs_pass.1 = (bf16[2,768,256]{2,1,0:T(8,128)(2,1)S(1)}, bf16[2,256,1152]{2,1,0:T(8,128)(2,1)S(1)}, f32[2,8,128]{2,1,0:T(8,128)S(1)}) custom-call(bf16[2,64,1152]{2,1,0:T(8,128)(2,1)S(1)} %collective-permute-done.2.refs_0_, bf16[2,64,1152]{2,1,0:T(8,128)(2,1)S(1)} %collective-permute-done.4.refs_1_, ...), custom_call_target="tpu_custom_call" | custom-call | tf_op jit(solution)/shard_map/theirs_pass/pallas_call | solution.py:121
  28.7 2.1 %collective-permute-done.13.refs_6_ = bf16[2,64,1152]{2,1,0:T(8,128)(2,1)S(1)} collective-permute-done((bf16[2,64,1152]{2,1,0:T(8,128)(2,1)S(1)}, bf16[2,64,1152]{2,1,0:T(8,128)(2,1)S(1)}, u32[]{:S(2)}, u32[]{:S(2)}) %collective-permute-start.13) | collective-permute-done | bytes 294944 | tf_op jit(solution)/shard_map/ppermute | solution.py:36
  31.3 1.1 %collective-permute-done.14.refs_7_ = bf16[2,64,1152]{2,1,0:T(8,128)(2,1)S(1)} collective-permute-done((bf16[2,64,1152]{2,1,0:T(8,128)(2,1)S(1)}, bf16[2,64,1152]{2,1,0:T(8,128)(2,1)S(1)}, u32[]{:S(2)}, u32[]{:S(2)}) %collective-permute-start.14) | collective-permute-done | bytes 294944 | tf_op jit(solution)/shard_map/ppermute | solution.py:36
  32.8 2.5 %ours_pass.1 = (bf16[2,768,256]{2,1,0:T(8,128)(2,1)S(1)}, bf16[2,256,1152]{2,1,0:T(8,128)(2,1)S(1)}, f32[4,8,128]{2,1,0:T(8,128)S(1)}) custom-call(bf16[2,64,1152]{2,1,0:T(8,128)(2,1)S(1)} %copy-done.2, bf16[2,64,1152]{2,1,0:T(8,128)(2,1)S(1)} %collective-permute-done.1.in_b.refs_1_, bf16[2,64,1152]{2,1,0:T(8,128)(2,1)S(1)} %collective-permute-done.3.refs_2_, ...), custom_call_target="tpu_custom_call" | custom-call | tf_op jit(solution)/shard_map/ours_pass/pallas_call | solution.py:121
  36.6 1.8 %collective-permute-start.16 = (f32[4,8,128]{2,1,0:T(8,128)S(1)}, f32[4,8,128]{2,1,0:T(8,128)S(1)}, u32[]{:S(2)}, u32[]{:S(2)}) collective-permute-start(f32[4,8,128]{2,1,0:T(8,128)S(1)} %chip_squares.1.refs_1_), channel_id=1, source_target_pairs={{0,2},{1,3},{2,0},{3,1},{4,6},{5,7},{6,4},{7,5},{8,10},{9,11},{10,... | collective-permute-start | bytes 49160 | tf_op jit(solution)/shard_map/ppermute | solution.py:36
  39.2 1.1 %collective-permute-start.18 = (f32[4,8,128]{2,1,0:T(8,128)S(1)}, f32[4,8,128]{2,1,0:T(8,128)S(1)}, u32[]{:S(2)}, u32[]{:S(2)}) collective-permute-start(f32[4,8,128]{2,1,0:T(8,128)S(1)} %chip_squares.1.refs_1_), channel_id=1, source_target_pairs={{0,6},{1,7},{2,4},{3,5},{4,0},{5,1},{6,2},{7,3},{8,14},{9,15},{10,... | collective-permute-start | bytes 49160 | tf_op jit(solution)/shard_map/ppermute | solution.py:36
  40.4 1.4 %collective-permute-done.16.refs_2_ = f32[4,8,128]{2,1,0:T(8,128)S(1)} collective-permute-done((f32[4,8,128]{2,1,0:T(8,128)S(1)}, f32[4,8,128]{2,1,0:T(8,128)S(1)}, u32[]{:S(2)}, u32[]{:S(2)}) %collective-permute-start.16) | collective-permute-done | bytes 16416 | tf_op jit(solution)/shard_map/ppermute | solution.py:36
  42.1 2.1 %collective-permute-done.18.refs_4_ = f32[4,8,128]{2,1,0:T(8,128)S(1)} collective-permute-done((f32[4,8,128]{2,1,0:T(8,128)S(1)}, f32[4,8,128]{2,1,0:T(8,128)S(1)}, u32[]{:S(2)}, u32[]{:S(2)}) %collective-permute-start.18) | collective-permute-done | bytes 16416 | tf_op jit(solution)/shard_map/ppermute | solution.py:36
  44.2 1.4 %outer_first.1 = (bf16[208,1152]{1,0:T(8,128)(2,1)S(1)}, f32[8,128]{1,0:T(8,128)S(1)}, f32[4,8,128]{2,1,0:T(8,128)S(1)}) custom-call(f32[1,1]{1,0:T(1,128)} %collective-permute-done.refs_0_, f32[4,8,128]{2,1,0:T(8,128)S(1)} %chip_squares.1.refs_1_, f32[4,8,128]{2,1,0:T(8,128)S(1)} %collective-permute-done.16.refs_2_, ...), custom_call_target="tpu_custom_call" | custom-call | tf_op jit(solution)/shard_map/outer_first/pallas_call | solution.py:121
  45.6 2.2 %collective-permute-start.19 = (bf16[208,1152]{1,0:T(8,128)(2,1)S(1)}, bf16[208,1152]{1,0:T(8,128)(2,1)S(1)}, u32[]{:S(2)}, u32[]{:S(2)}) collective-permute-start(bf16[208,1152]{1,0:T(8,128)(2,1)S(1)} %get-tuple-element.51), channel_id=1, source_target_pairs={{0,32},{1,9},{2,34},{3,11},{4,36},{5,13},{6,38},{7,15},{8,40},{9,1... | collective-permute-start | bytes 1437704 | tf_op jit(solution)/shard_map/ppermute | solution.py:36
  48.5 5.0 %collective-permute-start.20 = (bf16[192,1152]{1,0:T(8,128)(2,1)S(1)}, bf16[192,1152]{1,0:T(8,128)(2,1)S(1)}, u32[]{:S(2)}, u32[]{:S(2)}) collective-permute-start(bf16[192,1152]{1,0:T(8,128)(2,1)S(1)} %outer_second.1), channel_id=1, source_target_pairs={{0,224},{1,25},{2,226},{3,27},{4,228},{5,29},{6,230},{7,31},{8,232... | collective-permute-start | bytes 1327112 | tf_op jit(solution)/shard_map/ppermute | solution.py:36
  53.6 1.3 %outer_keep.1 = (f32[192,1152]{1,0:T(8,128)S(1)}, f32[192,1152]{1,0:T(8,128)S(1)}) custom-call(f32[4,8,128]{2,1,0:T(8,128)S(1)} %get-tuple-element.49.scale, bf16[2,768,256]{2,1,0:T(8,128)(2,1)S(1)} %get-tuple-element.44.refs_5_.refs_0_, bf16[2,768,256]{2,1,0:T(8,128)(2,1)S(1)} %get-tuple-element.45.refs_6_.refs_1_, ...), custom_call_target="tpu_custom_call" | custom-call | tf_op jit(solution)/shard_map/outer_keep/pallas_call | solution.py:121
  55.1 5.6 %collective-permute-start.21 = (bf16[112,1152]{1,0:T(8,128)(2,1)S(1)}, bf16[112,1152]{1,0:T(8,128)(2,1)S(1)}, u32[]{:S(2)}, u32[]{:S(2)}) collective-permute-start(bf16[112,1152]{1,0:T(8,128)(2,1)S(1)} %get-tuple-element.56), channel_id=1, source_target_pairs={{0,224},{1,25},{2,226},{3,27},{4,228},{5,29},{6,230},{7,31},{8,232... | collective-permute-start | bytes 774152 | tf_op jit(solution)/shard_map/ppermute | solution.py:36
  60.9 5.9 %collective-permute-done.22.got1 = bf16[96,1152]{1,0:T(8,128)(2,1)S(1)} collective-permute-done((bf16[96,1152]{1,0:T(8,128)(2,1)S(1)}, bf16[96,1152]{1,0:T(8,128)(2,1)S(1)}, u32[]{:S(2)}, u32[]{:S(2)}) %collective-permute-start.22) | collective-permute-done | bytes 221216 | tf_op jit(solution)/shard_map/ppermute | solution.py:36
  67.8 7.6 %all-to-all-start = ((bf16[8,24,1280]{2,1,0:T(8,128)(2,1)}), bf16[8,24,1280]{2,1,0:T(8,128)(2,1)S(1)}, u32[]{:S(2)}, u32[]{:S(2)}) async-start(bf16[8,24,1280]{2,1,0:T(8,128)(2,1)} %bitcast.3), calls=%async_computation | async-start | bytes 983040 | tf_op jit(solution)/shard_map/all_to_all | solution.py:484
  76.0 11.9 %all-to-all-done = bf16[8,24,1280]{2,1,0:T(8,128)(2,1)S(1)} async-done(((bf16[8,24,1280]{2,1,0:T(8,128)(2,1)}), bf16[8,24,1280]{2,1,0:T(8,128)(2,1)S(1)}, u32[]{:S(2)}, u32[]{:S(2)}) %all-to-all-start) | async-done | bytes 491552 | tf_op jit(solution)/shard_map/all_to_all | solution.py:484
  88.0 1.4 %step_last.1 = (f32[24,1152]{1,0:T(8,128)}, f32[1,1]{1,0:T(1,128)}) custom-call(f32[1,1]{1,0:T(1,128)} %collective-permute-done.refs_0_, f32[1,1]{1,0:T(1,128)} %bitcast.6.refs_1_, bf16[192,1280]{1,0:T(8,128)(2,1)S(1)} %bitcast.7), custom_call_target="tpu_custom_call" | custom-call | tf_op jit(solution)/shard_map/step_last/pallas_call | solution.py:121
  (50 shorter events, 13.5 us)
Async XLA Ops:
  2.4 16.3 %collective-permute-start.9 = (bf16[2,64,1152]{2,1,0:T(8,128)(2,1)S(1)}, bf16[2,64,1152]{2,1,0:T(8,128)(2,1)S(1)}, u32[]{:S(2)}, u32[]{:S(2)}) collective-permute-start(bf16[2,64,1152]{2,1,0:T(8,128)(2,1)S(1)} %mask.1.co_a.refs_4_), channel_id=1, source_target_pairs={{0,6},{1,7},{2,4},{3,5},{4,0},{5,1},{6,2},{7,3},{8,14},{9,15},{10,... | collective-permute-start | bytes 884744 | tf_op jit(solution)/shard_map/ppermute | solution.py:36
  3.3 15.7 %collective-permute-start.7 = (bf16[2,64,1152]{2,1,0:T(8,128)(2,1)S(1)}, bf16[2,64,1152]{2,1,0:T(8,128)(2,1)S(1)}, u32[]{:S(2)}, u32[]{:S(2)}) collective-permute-start(bf16[2,64,1152]{2,1,0:T(8,128)(2,1)S(1)} %mask.1.co_a.refs_4_), channel_id=1, source_target_pairs={{0,4},{1,5},{2,6},{3,7},{4,2},{5,3},{6,0},{7,1},{8,12},{9,13},{10,... | collective-permute-start | bytes 884744 | tf_op jit(solution)/shard_map/ppermute | solution.py:36
  5.7 13.5 %collective-permute-start.2 = (bf16[2,64,1152]{2,1,0:T(8,128)(2,1)}, bf16[2,64,1152]{2,1,0:T(8,128)(2,1)S(1)}, u32[]{:S(2)}, u32[]{:S(2)}) collective-permute-start(bf16[2,64,1152]{2,1,0:T(8,128)(2,1)} %refs_0_.1), channel_id=1, source_target_pairs={{0,4},{1,5},{2,6},{3,7},{4,2},{5,3},{6,0},{7,1},{8,12},{9,13},{10,... | collective-permute-start | bytes 884744 | tf_op jit(solution)/shard_map/ppermute | solution.py:36
  6.7 12.8 %collective-permute-start.5 = (bf16[2,64,1152]{2,1,0:T(8,128)(2,1)}, bf16[2,64,1152]{2,1,0:T(8,128)(2,1)S(1)}, u32[]{:S(2)}, u32[]{:S(2)}) collective-permute-start(bf16[2,64,1152]{2,1,0:T(8,128)(2,1)} %refs_0_.1), channel_id=1, source_target_pairs={{0,6},{1,7},{2,4},{3,5},{4,0},{5,1},{6,2},{7,3},{8,14},{9,15},{10,... | collective-permute-start | bytes 884744 | tf_op jit(solution)/shard_map/ppermute | solution.py:36
  17.1 1.3 %collective-permute-start = (f32[1,1]{1,0:T(1,128)}, f32[1,1]{1,0:T(1,128)}, u32[]{:S(2)}, u32[]{:S(2)}) collective-permute-start(f32[1,1]{1,0:T(1,128)} %bitcast), channel_id=1, source_target_pairs={{0,1},{1,0},{2,3},{3,2},{4,5},{5,4},{6,7},{7,6},{8,9},{9,8},{10,11... | collective-permute-start | bytes 20 | tf_op jit(solution)/shard_map/ppermute | solution.py:36
  18.5 1.6 %collective-permute-start.11 = (bf16[2,64,1152]{2,1,0:T(8,128)(2,1)S(1)}, bf16[2,64,1152]{2,1,0:T(8,128)(2,1)S(1)}, u32[]{:S(2)}, u32[]{:S(2)}) collective-permute-start(bf16[2,64,1152]{2,1,0:T(8,128)(2,1)S(1)} %mask.1.co_a.refs_4_), channel_id=1, source_target_pairs={{0,1},{1,0},{2,3},{3,2},{4,5},{5,4},{6,7},{7,6},{8,9},{9,8},{10,11... | collective-permute-start | bytes 884744 | tf_op jit(solution)/shard_map/ppermute | solution.py:36
  18.7 1.8 %collective-permute-start.1 = (bf16[2,64,1152]{2,1,0:T(8,128)(2,1)S(1)}, bf16[2,64,1152]{2,1,0:T(8,128)(2,1)S(1)}, u32[]{:S(2)}, u32[]{:S(2)}) collective-permute-start(bf16[2,64,1152]{2,1,0:T(8,128)(2,1)S(1)} %copy-done.2), channel_id=1, source_target_pairs={{0,1},{1,0},{2,3},{3,2},{4,5},{5,4},{6,7},{7,6},{8,9},{9,8},{10,11... | collective-permute-start | bytes 884744 | tf_op jit(solution)/shard_map/ppermute | solution.py:36
  19.0 1.9 %collective-permute-start.10 = (bf16[2,64,1152]{2,1,0:T(8,128)(2,1)S(1)}, bf16[2,64,1152]{2,1,0:T(8,128)(2,1)S(1)}, u32[]{:S(2)}, u32[]{:S(2)}) collective-permute-start(bf16[2,64,1152]{2,1,0:T(8,128)(2,1)S(1)} %collective-permute-done.9.refs_6_), channel_id=1, source_target_pairs={{0,1},{1,0},{2,3},{3,2},{4,5},{5,4},{6,7},{7,6},{8,9},{9,8},{10,11... | collective-permute-start | bytes 884744 | tf_op jit(solution)/shard_map/ppermute | solution.py:36
  19.2 5.9 %collective-permute-start.8 = (bf16[2,64,1152]{2,1,0:T(8,128)(2,1)S(1)}, bf16[2,64,1152]{2,1,0:T(8,128)(2,1)S(1)}, u32[]{:S(2)}, u32[]{:S(2)}) collective-permute-start(bf16[2,64,1152]{2,1,0:T(8,128)(2,1)S(1)} %collective-permute-done.7.refs_4_), channel_id=1, source_target_pairs={{0,1},{1,0},{2,3},{3,2},{4,5},{5,4},{6,7},{7,6},{8,9},{9,8},{10,11... | collective-permute-start | bytes 884744 | tf_op jit(solution)/shard_map/ppermute | solution.py:36
  19.5 5.6 %collective-permute-start.4 = (bf16[2,64,1152]{2,1,0:T(8,128)(2,1)S(1)}, bf16[2,64,1152]{2,1,0:T(8,128)(2,1)S(1)}, u32[]{:S(2)}, u32[]{:S(2)}) collective-permute-start(bf16[2,64,1152]{2,1,0:T(8,128)(2,1)S(1)} %collective-permute-done.2.refs_0_), channel_id=1, source_target_pairs={{0,1},{1,0},{2,3},{3,2},{4,5},{5,4},{6,7},{7,6},{8,9},{9,8},{10,11... | collective-permute-start | bytes 884744 | tf_op jit(solution)/shard_map/ppermute | solution.py:36
  20.0 5.1 %collective-permute-start.6 = (bf16[2,64,1152]{2,1,0:T(8,128)(2,1)S(1)}, bf16[2,64,1152]{2,1,0:T(8,128)(2,1)S(1)}, u32[]{:S(2)}, u32[]{:S(2)}) collective-permute-start(bf16[2,64,1152]{2,1,0:T(8,128)(2,1)S(1)} %collective-permute-done.5.refs_2_), channel_id=1, source_target_pairs={{0,1},{1,0},{2,3},{3,2},{4,5},{5,4},{6,7},{7,6},{8,9},{9,8},{10,11... | collective-permute-start | bytes 884744 | tf_op jit(solution)/shard_map/ppermute | solution.py:36
  20.5 10.4 %collective-permute-start.13 = (bf16[2,64,1152]{2,1,0:T(8,128)(2,1)S(1)}, bf16[2,64,1152]{2,1,0:T(8,128)(2,1)S(1)}, u32[]{:S(2)}, u32[]{:S(2)}) collective-permute-start(bf16[2,64,1152]{2,1,0:T(8,128)(2,1)S(1)} %collective-permute-done.9.refs_6_), channel_id=1, source_target_pairs={{0,6},{1,7},{2,4},{3,5},{4,0},{5,1},{6,2},{7,3},{8,14},{9,15},{10,... | collective-permute-start | bytes 884744 | tf_op jit(solution)/shard_map/ppermute | solution.py:36
  20.9 9.9 %collective-permute-start.3 = (bf16[2,64,1152]{2,1,0:T(8,128)(2,1)S(1)}, bf16[2,64,1152]{2,1,0:T(8,128)(2,1)S(1)}, u32[]{:S(2)}, u32[]{:S(2)}) collective-permute-start(bf16[2,64,1152]{2,1,0:T(8,128)(2,1)S(1)} %collective-permute-done.2.refs_0_), channel_id=1, source_target_pairs={{0,4},{1,5},{2,6},{3,7},{4,2},{5,3},{6,0},{7,1},{8,12},{9,13},{10,... | collective-permute-start | bytes 884744 | tf_op jit(solution)/shard_map/ppermute | solution.py:36
  30.8 1.6 %collective-permute-start.14 = (bf16[2,64,1152]{2,1,0:T(8,128)(2,1)S(1)}, bf16[2,64,1152]{2,1,0:T(8,128)(2,1)S(1)}, u32[]{:S(2)}, u32[]{:S(2)}) collective-permute-start(bf16[2,64,1152]{2,1,0:T(8,128)(2,1)S(1)} %collective-permute-done.13.refs_6_), channel_id=1, source_target_pairs={{0,1},{1,0},{2,3},{3,2},{4,5},{5,4},{6,7},{7,6},{8,9},{9,8},{10,11... | collective-permute-start | bytes 884744 | tf_op jit(solution)/shard_map/ppermute | solution.py:36
  30.8 2.0 %collective-permute-start.12 = (bf16[2,64,1152]{2,1,0:T(8,128)(2,1)S(1)}, bf16[2,64,1152]{2,1,0:T(8,128)(2,1)S(1)}, u32[]{:S(2)}, u32[]{:S(2)}) collective-permute-start(bf16[2,64,1152]{2,1,0:T(8,128)(2,1)S(1)} %collective-permute-done.3.refs_2_), channel_id=1, source_target_pairs={{0,1},{1,0},{2,3},{3,2},{4,5},{5,4},{6,7},{7,6},{8,9},{9,8},{10,11... | collective-permute-start | bytes 884744 | tf_op jit(solution)/shard_map/ppermute | solution.py:36
  35.3 1.3 %collective-permute-start.15 = (f32[4,8,128]{2,1,0:T(8,128)S(1)}, f32[4,8,128]{2,1,0:T(8,128)S(1)}, u32[]{:S(2)}, u32[]{:S(2)}) collective-permute-start(f32[4,8,128]{2,1,0:T(8,128)S(1)} %get-tuple-element.43.left), channel_id=1, source_target_pairs={{0,1},{1,0},{2,3},{3,2},{4,5},{5,4},{6,7},{7,6},{8,9},{9,8},{10,11... | collective-permute-start | bytes 49160 | tf_op jit(solution)/shard_map/ppermute | solution.py:36
  36.6 5.2 %collective-permute-start.16 = (f32[4,8,128]{2,1,0:T(8,128)S(1)}, f32[4,8,128]{2,1,0:T(8,128)S(1)}, u32[]{:S(2)}, u32[]{:S(2)}) collective-permute-start(f32[4,8,128]{2,1,0:T(8,128)S(1)} %chip_squares.1.refs_1_), channel_id=1, source_target_pairs={{0,2},{1,3},{2,0},{3,1},{4,6},{5,7},{6,4},{7,5},{8,10},{9,11},{10,... | collective-permute-start | bytes 49160 | tf_op jit(solution)/shard_map/ppermute | solution.py:36
  38.3 3.7 %collective-permute-start.17 = (f32[4,8,128]{2,1,0:T(8,128)S(1)}, f32[4,8,128]{2,1,0:T(8,128)S(1)}, u32[]{:S(2)}, u32[]{:S(2)}) collective-permute-start(f32[4,8,128]{2,1,0:T(8,128)S(1)} %chip_squares.1.refs_1_), channel_id=1, source_target_pairs={{0,4},{1,5},{2,6},{3,7},{4,2},{5,3},{6,0},{7,1},{8,12},{9,13},{10,... | collective-permute-start | bytes 49160 | tf_op jit(solution)/shard_map/ppermute | solution.py:36
  39.2 4.9 %collective-permute-start.18 = (f32[4,8,128]{2,1,0:T(8,128)S(1)}, f32[4,8,128]{2,1,0:T(8,128)S(1)}, u32[]{:S(2)}, u32[]{:S(2)}) collective-permute-start(f32[4,8,128]{2,1,0:T(8,128)S(1)} %chip_squares.1.refs_1_), channel_id=1, source_target_pairs={{0,6},{1,7},{2,4},{3,5},{4,0},{5,1},{6,2},{7,3},{8,14},{9,15},{10,... | collective-permute-start | bytes 49160 | tf_op jit(solution)/shard_map/ppermute | solution.py:36
  45.6 9.3 %collective-permute-start.19 = (bf16[208,1152]{1,0:T(8,128)(2,1)S(1)}, bf16[208,1152]{1,0:T(8,128)(2,1)S(1)}, u32[]{:S(2)}, u32[]{:S(2)}) collective-permute-start(bf16[208,1152]{1,0:T(8,128)(2,1)S(1)} %get-tuple-element.51), channel_id=1, source_target_pairs={{0,32},{1,9},{2,34},{3,11},{4,36},{5,13},{6,38},{7,15},{8,40},{9,1... | collective-permute-start | bytes 1437704 | tf_op jit(solution)/shard_map/ppermute | solution.py:36
  48.5 12.2 %collective-permute-start.20 = (bf16[192,1152]{1,0:T(8,128)(2,1)S(1)}, bf16[192,1152]{1,0:T(8,128)(2,1)S(1)}, u32[]{:S(2)}, u32[]{:S(2)}) collective-permute-start(bf16[192,1152]{1,0:T(8,128)(2,1)S(1)} %outer_second.1), channel_id=1, source_target_pairs={{0,224},{1,25},{2,226},{3,27},{4,228},{5,29},{6,230},{7,31},{8,232... | collective-permute-start | bytes 1327112 | tf_op jit(solution)/shard_map/ppermute | solution.py:36
  55.1 11.7 %collective-permute-start.21 = (bf16[112,1152]{1,0:T(8,128)(2,1)S(1)}, bf16[112,1152]{1,0:T(8,128)(2,1)S(1)}, u32[]{:S(2)}, u32[]{:S(2)}) collective-permute-start(bf16[112,1152]{1,0:T(8,128)(2,1)S(1)} %get-tuple-element.56), channel_id=1, source_target_pairs={{0,224},{1,25},{2,226},{3,27},{4,228},{5,29},{6,230},{7,31},{8,232... | collective-permute-start | bytes 774152 | tf_op jit(solution)/shard_map/ppermute | solution.py:36
  60.8 6.0 %collective-permute-start.22 = (bf16[96,1152]{1,0:T(8,128)(2,1)S(1)}, bf16[96,1152]{1,0:T(8,128)(2,1)S(1)}, u32[]{:S(2)}, u32[]{:S(2)}) collective-permute-start(bf16[96,1152]{1,0:T(8,128)(2,1)S(1)} %get-tuple-element.57), channel_id=1, source_target_pairs={{0,32},{1,9},{2,34},{3,11},{4,36},{5,13},{6,38},{7,15},{8,40},{9,1... | collective-permute-start | bytes 663560 | tf_op jit(solution)/shard_map/ppermute | solution.py:36
  67.8 20.2 %all-to-all-start = ((bf16[8,24,1280]{2,1,0:T(8,128)(2,1)}), bf16[8,24,1280]{2,1,0:T(8,128)(2,1)S(1)}, u32[]{:S(2)}, u32[]{:S(2)}) async-start(bf16[8,24,1280]{2,1,0:T(8,128)(2,1)} %bitcast.3), calls=%async_computation | async-start | bytes 983040 | tf_op jit(solution)/shard_map/all_to_all | solution.py:484
  (6 other events, 12.6 us)
